TPU v7x, 32 devices: a whole 2x2x4 slice. The times are simulated.
32 devices in a mesh: shard: 8 (over y, x, core), rep: 4 (over z).
Axes of the slice: x: 2, y: 2, z: 4, core: 2. Of those that a mesh axis runs over, the one named last changes fastest.
Arguments:
- image: bfloat16 [64, 64, 1536], P(('shard', 'rep')), may hold values from -6 to 6
- text: bfloat16 [64, 77, 1536], P(('shard', 'rep')), may hold values from -6 to 6
- condition: bfloat16 [64, 1536], P(('shard', 'rep')), may hold values from -6 to 6
- counts: int32 [32], P(('shard', 'rep')), may hold values from 1 to 2, as said below
- adaptive_weight: float32 [2, 1536, 9216], P(None, 'shard'), may hold values from -0.15625 to 0.15625
- adaptive_bias: float32 [2, 9216], P(None, 'shard'), may hold values from -1.8 to 1.8
- attend_weight: float32 [2, 1536, 4608], P(None, 'shard'), may hold values from -0.15625 to 0.15625
- attend_bias: float32 [2, 3072], P(None, 'shard'), may hold values from -1.8 to 1.8
- output_weight: float32 [2, 1536, 1536], P(None, 'shard'), may hold values from -0.875 to 0.875
- output_bias: float32 [2, 1536], P(None, 'shard'), may hold values from -1.8 to 1.8
- expand_weight: float32 [2, 1536, 6144], P(None, 'shard'), may hold values from -0.15625 to 0.15625
- expand_bias: float32 [2, 6144], P(None, 'shard'), may hold values from -1.8 to 1.8
- reduce_weight: float32 [2, 6144, 1536], P(None, 'shard'), may hold values from -0.109375 to 0.109375
- reduce_bias: float32 [2, 1536], P(None, 'shard'), may hold values from -1.8 to 1.8
- image_cotangent: bfloat16 [64, 64, 1536], P(('shard', 'rep')), may hold values from -6 to 6
- text_cotangent: bfloat16 [64, 77, 1536], P(('shard', 'rep')), may hold values from -6 to 6
Outputs:
- image_output: bfloat16 [64, 64, 1536], P(('shard', 'rep'))
- text_output: bfloat16 [64, 77, 1536], P(('shard', 'rep'))
- image_grad: bfloat16 [64, 64, 1536], P(('shard', 'rep'))
- text_grad: bfloat16 [64, 77, 1536], P(('shard', 'rep'))
- condition_grad: bfloat16 [64, 1536], P(('shard', 'rep'))
- adaptive_weight_grad: float32 [2, 1536, 9216], P(None, 'shard')
- adaptive_bias_grad: float32 [2, 9216], P(None, 'shard')
- attend_weight_grad: float32 [2, 1536, 4608], P(None, 'shard')
- attend_bias_grad: float32 [2, 3072], P(None, 'shard')
- output_weight_grad: float32 [2, 1536, 1536], P(None, 'shard')
- output_bias_grad: float32 [2, 1536], P(None, 'shard')
- expand_weight_grad: float32 [2, 1536, 6144], P(None, 'shard')
- expand_bias_grad: float32 [2, 6144], P(None, 'shard')
- reduce_weight_grad: float32 [2, 6144, 1536], P(None, 'shard')
- reduce_bias_grad: float32 [2, 1536], P(None, 'shard')
Inputs may be any that keep to these rules, and one draw needn't show every extreme that they name: `counts`: number of live sequences on each device; both 1 and 2 occur in every draw.
All inputs are finite; a program needn't handle non-finite values.
Results may differ from a plain program's by a relative error of at most 0.019.
The roundings to bfloat16 on the way count: a program that leaves them out, or rounds other values in their place, can miss the bound.
Values may be sent and summed in bfloat16 or wider, within the bound.
No kernel may reach another device: no remote copies, remote signals or barrier semaphores. Data moves between devices by JAX's collectives and lax.ppermute only.
A program may use at most 448 MiB of HBM per device.

v0:
```python
import jax
import jax.numpy as jnp
from jax import lax
from jax.sharding import PartitionSpec as P

HEADS = 24


EPS = 1e-06
LOWER = jnp.bfloat16
WIDE = jnp.float32


def normalize(values):
    mean = jnp.mean(values, axis=-1, keepdims=True)
    centred = values - mean
    spread = jnp.mean(centred * centred, axis=-1, keepdims=True)
    return centred * lax.rsqrt(spread + EPS)


def modulate(field, shift, scale):
    return normalize(field) * (1.0 + scale[:, None, :]) + shift[:, None, :]


def project(form, left, right):
    return jnp.einsum(form, left, right, preferred_element_type=WIDE)


def heads_view(tensor):
    return tensor.reshape(tensor.shape[0], tensor.shape[1], HEADS, tensor.shape[2] // HEADS)


def smooth_gelu(values):
    return jax.nn.gelu(values, approximate=True)


def body(
    image,
    text,
    condition,
    counts,
    adaptive_weight,
    adaptive_bias,
    attend_weight,
    attend_bias,
    output_weight,
    output_bias,
    expand_weight,
    expand_bias,
    reduce_weight,
    reduce_bias,
    image_cotangent,
    text_cotangent,
):
    slots = image.shape[0]
    split_at = image.shape[1]
    width = image.shape[2]
    alive = (jnp.arange(slots, dtype=jnp.int32) < counts[0]).astype(WIDE)[:, None, None]
    streams = (image.astype(WIDE), text.astype(WIDE))
    cond_value = condition.astype(WIDE)
    cond_low = jax.nn.silu(cond_value).astype(LOWER)
    adaptive_bias_full, attend_full, attend_bias_full, output_full, output_bias_full, cond_all = (
        lax.all_gather(adaptive_bias.astype(LOWER), "shard", axis=1, tiled=True),
        lax.all_gather(attend_weight.astype(LOWER), "shard", axis=1, tiled=True),
        lax.all_gather(attend_bias.astype(LOWER), "shard", axis=1, tiled=True),
        lax.all_gather(output_weight.astype(LOWER), "shard", axis=1, tiled=True),
        lax.all_gather(output_bias.astype(LOWER), "shard", axis=1, tiled=True),
        lax.all_gather(cond_low, "shard", axis=0, tiled=True),
    )
    shard_rows = adaptive_weight.shape[1]
    cond_cols = lax.dynamic_slice_in_dim(
        cond_all, lax.axis_index("shard") * shard_rows, shard_rows, 1
    )
    adaptive_local = adaptive_weight.astype(LOWER)
    partial_terms = project("gd,sde->gse", cond_cols, adaptive_local)
    modulation = (
        lax.psum_scatter(partial_terms, "shard", scatter_dimension=0, tiled=True)
        + adaptive_bias_full.astype(WIDE)[None]
    )
    parts = [
        [modulation[:, which, piece * width : (piece + 1) * width] for piece in range(6)]
        for which in range(2)
    ]
    hidden_front = []
    triples = []
    for which in range(2):
        hidden = modulate(streams[which], parts[which][0], parts[which][1]).astype(LOWER)
        bias_row = attend_bias_full[which].astype(WIDE)
        bias_full = jnp.concatenate([bias_row[:width], jnp.zeros((width,), WIDE), bias_row[width:]])
        triples.append(
            (project("grd,de->gre", hidden, attend_full[which]) + bias_full).astype(LOWER)
        )
        hidden_front.append(hidden)
    joint = jnp.concatenate(triples, axis=1)
    length = joint.shape[1]
    queries = heads_view(joint[:, :, :width])
    keys = heads_view(joint[:, :, width : 2 * width])
    values = heads_view(joint[:, :, 2 * width :])
    factor = queries.shape[-1] ** (-0.5)
    scores = project("gqhe,gkhe->ghqk", queries, keys) * factor
    peak = jnp.max(scores, axis=-1, keepdims=True)
    raised = jnp.exp(scores - peak)
    summed_rows = jnp.sum(raised, axis=-1, keepdims=True)
    log_total = peak + jnp.log(summed_rows)
    attended = project("ghqk,gkhe->gqhe", (raised / summed_rows).astype(LOWER), values)
    attended = attended.reshape(slots, length, width).astype(LOWER)
    pieces = (attended[:, :split_at], attended[:, split_at:])
    branches = []
    middles = []
    for which in range(2):
        branch = project("grd,de->gre", pieces[which], output_full[which]) + output_bias_full[
            which
        ].astype(WIDE)
        branches.append(branch)
        middles.append(streams[which] + parts[which][2][:, None, :] * branch)
    expand_full, expand_bias_full, reduce_full, reduce_bias_full = (
        lax.all_gather(expand_weight.astype(LOWER), "shard", axis=1, tiled=True),
        lax.all_gather(expand_bias.astype(LOWER), "shard", axis=1, tiled=True),
        lax.all_gather(reduce_weight.astype(LOWER), "shard", axis=1, tiled=True),
        lax.all_gather(reduce_bias.astype(LOWER), "shard", axis=1, tiled=True),
    )
    hidden_feed = []
    befores = []
    actives = []
    seconds = []
    outputs = []
    for which in range(2):
        part = parts[which]
        hidden = modulate(middles[which], part[3], part[4]).astype(LOWER)
        before = project("grd,df->grf", hidden, expand_full[which]) + expand_bias_full[
            which
        ].astype(WIDE)
        active = smooth_gelu(before).astype(LOWER)
        second = project("grf,fd->grd", active, reduce_full[which]) + reduce_bias_full[
            which
        ].astype(WIDE)
        outputs.append(((middles[which] + part[5][:, None, :] * second) * alive).astype(LOWER))
        hidden_feed.append(hidden)
        befores.append(before)
        actives.append(active)
        seconds.append(second)
    cotangents = (image_cotangent.astype(WIDE) * alive, text_cotangent.astype(WIDE) * alive)
    expand_back, expand_bias_back, reduce_back, reduce_bias_back = (
        lax.all_gather(expand_weight.astype(LOWER), "shard", axis=1, tiled=True),
        lax.all_gather(expand_bias.astype(LOWER), "shard", axis=1, tiled=True),
        lax.all_gather(reduce_weight.astype(LOWER), "shard", axis=1, tiled=True),
        lax.all_gather(reduce_bias.astype(LOWER), "shard", axis=1, tiled=True),
    )
    feed_shares = []
    d_middles = []
    feed_mods = []
    for which in range(2):
        part = parts[which]
        cotangent = cotangents[which]
        d_second = (cotangent * part[5][:, None, :]).astype(LOWER)
        d_gate_feed = jnp.sum(cotangent * seconds[which], axis=1)
        reduce_grad = project("grf,grd->fd", actives[which], d_second)
        reduce_bias_grad = jnp.sum(d_second, axis=(0, 1), dtype=WIDE)
        d_active = project("grd,fd->grf", d_second, reduce_back[which])
        d_before = jax.vjp(smooth_gelu, befores[which])[1](d_active)[0].astype(LOWER)
        expand_grad = project("grd,grf->df", hidden_feed[which], d_before)
        expand_bias_grad = jnp.sum(d_before, axis=(0, 1), dtype=WIDE)
        d_hidden = project("grf,df->grd", d_before, expand_back[which])
        d_mid, d_shift_feed, d_scale_feed = jax.vjp(modulate, middles[which], part[3], part[4])[1](
            d_hidden
        )
        feed_shares.append(
            (
                lax.psum_scatter(
                    expand_grad.astype(jnp.bfloat16), "shard", scatter_dimension=0, tiled=True
                ).astype(jnp.float32),
                lax.psum_scatter(
                    expand_bias_grad.astype(jnp.bfloat16), "shard", scatter_dimension=0, tiled=True
                ).astype(jnp.float32),
                lax.psum_scatter(
                    reduce_grad.astype(jnp.bfloat16), "shard", scatter_dimension=0, tiled=True
                ).astype(jnp.float32),
                lax.psum_scatter(
                    reduce_bias_grad.astype(jnp.bfloat16), "shard", scatter_dimension=0, tiled=True
                ).astype(jnp.float32),
            )
        )
        d_middles.append(cotangent + d_mid)
        feed_mods.append((d_shift_feed, d_scale_feed, d_gate_feed))
    attend_back, output_back = (
        lax.all_gather(attend_weight.astype(LOWER), "shard", axis=1, tiled=True),
        lax.all_gather(output_weight.astype(LOWER), "shard", axis=1, tiled=True),
    )
    d_pieces = []
    gate_front = []
    output_grads = []
    output_bias_grads = []
    for which in range(2):
        d_branch = (d_middles[which] * parts[which][2][:, None, :]).astype(LOWER)
        gate_front.append(jnp.sum(d_middles[which] * branches[which], axis=1))
        output_grads.append(project("grd,gre->de", pieces[which], d_branch))
        output_bias_grads.append(jnp.sum(d_branch, axis=(0, 1), dtype=WIDE))
        d_pieces.append(project("gre,de->grd", d_branch, output_back[which]).astype(LOWER))
    d_attended = heads_view(jnp.concatenate(d_pieces, axis=1))
    again = project("gqhe,gkhe->ghqk", queries, keys) * factor
    probs = jnp.exp(again - log_total)
    d_probs = project("gqhe,gkhe->ghqk", d_attended, values)
    center = jnp.sum(probs * d_probs, axis=-1, keepdims=True)
    d_scores = (probs * (d_probs - center)).astype(LOWER)
    d_queries = project("ghqk,gkhe->gqhe", d_scores, keys) * factor
    d_keys = project("ghqk,gqhe->gkhe", d_scores, queries) * factor
    d_values = project("ghqk,gqhe->gkhe", probs.astype(LOWER), d_attended)
    d_joint = jnp.concatenate(
        [
            d_queries.reshape(slots, length, width),
            d_keys.reshape(slots, length, width),
            d_values.reshape(slots, length, width),
        ],
        axis=-1,
    ).astype(LOWER)
    d_triples = (d_joint[:, :split_at], d_joint[:, split_at:])
    attend_grads = []
    attend_bias_grads = []
    input_grads = []
    d_mods = []
    for which in range(2):
        part = parts[which]
        attend_grads.append(project("grd,gre->de", hidden_front[which], d_triples[which]))
        column_sums = jnp.sum(d_triples[which], axis=(0, 1), dtype=WIDE)
        attend_bias_grads.append(jnp.concatenate([column_sums[:width], column_sums[2 * width :]]))
        d_hidden = project("gre,de->grd", d_triples[which], attend_back[which])
        d_stream, d_shift_front, d_scale_front = jax.vjp(
            modulate, streams[which], part[0], part[1]
        )[1](d_hidden)
        input_grads.append((d_middles[which] + d_stream).astype(LOWER))
        d_shift_feed, d_scale_feed, d_gate_feed = feed_mods[which]
        d_mods.append(
            jnp.concatenate(
                [
                    d_shift_front,
                    d_scale_front,
                    gate_front[which],
                    d_shift_feed,
                    d_scale_feed,
                    d_gate_feed,
                ],
                axis=-1,
            )
        )
    d_modulation = jnp.stack(d_mods, axis=1).astype(LOWER)
    adaptive_bias_grads = jnp.sum(d_modulation, axis=0, dtype=WIDE)
    modulation_all = lax.all_gather(d_modulation, "shard", axis=0, tiled=True)
    adaptive_share = project("gd,gse->sde", cond_cols, modulation_all)
    cond_parts = project("gse,sde->gd", modulation_all, adaptive_local)
    d_cond_act = lax.all_to_all(cond_parts, "shard", split_axis=0, concat_axis=1, tiled=True)
    front_shares = []
    for which in range(2):
        front_shares.append(
            (
                lax.psum_scatter(
                    adaptive_bias_grads[which].astype(jnp.bfloat16),
                    "shard",
                    scatter_dimension=0,
                    tiled=True,
                ).astype(jnp.float32),
                lax.psum_scatter(
                    attend_grads[which].astype(jnp.bfloat16),
                    "shard",
                    scatter_dimension=0,
                    tiled=True,
                ).astype(jnp.float32),
                lax.psum_scatter(
                    attend_bias_grads[which].astype(jnp.bfloat16),
                    "shard",
                    scatter_dimension=0,
                    tiled=True,
                ).astype(jnp.float32),
                lax.psum_scatter(
                    output_grads[which].astype(jnp.bfloat16),
                    "shard",
                    scatter_dimension=0,
                    tiled=True,
                ).astype(jnp.float32),
                lax.psum_scatter(
                    output_bias_grads[which].astype(jnp.bfloat16),
                    "shard",
                    scatter_dimension=0,
                    tiled=True,
                ).astype(jnp.float32),
            )
        )
    adaptive_bias_share = jnp.stack([share[0] for share in front_shares])
    attend_share = jnp.stack([share[1] for share in front_shares])
    attend_bias_share = jnp.stack([share[2] for share in front_shares])
    output_share = jnp.stack([share[3] for share in front_shares])
    output_bias_share = jnp.stack([share[4] for share in front_shares])
    expand_share = jnp.stack([share[0] for share in feed_shares])
    expand_bias_share = jnp.stack([share[1] for share in feed_shares])
    reduce_share = jnp.stack([share[2] for share in feed_shares])
    reduce_bias_share = jnp.stack([share[3] for share in feed_shares])
    totals = (
        lax.psum(adaptive_share.astype(jnp.bfloat16), "rep").astype(jnp.float32),
        lax.psum(adaptive_bias_share.astype(jnp.bfloat16), "rep").astype(jnp.float32),
        lax.psum(attend_share.astype(jnp.bfloat16), "rep").astype(jnp.float32),
        lax.psum(attend_bias_share.astype(jnp.bfloat16), "rep").astype(jnp.float32),
        lax.psum(output_share.astype(jnp.bfloat16), "rep").astype(jnp.float32),
        lax.psum(output_bias_share.astype(jnp.bfloat16), "rep").astype(jnp.float32),
        lax.psum(expand_share.astype(jnp.bfloat16), "rep").astype(jnp.float32),
        lax.psum(expand_bias_share.astype(jnp.bfloat16), "rep").astype(jnp.float32),
        lax.psum(reduce_share.astype(jnp.bfloat16), "rep").astype(jnp.float32),
        lax.psum(reduce_bias_share.astype(jnp.bfloat16), "rep").astype(jnp.float32),
    )
    condition_grad = jax.vjp(jax.nn.silu, cond_value)[1](d_cond_act)[0].astype(LOWER)
    return (
        outputs[0],
        outputs[1],
        input_grads[0],
        input_grads[1],
        condition_grad,
        totals[0],
        totals[1],
        totals[2],
        totals[3],
        totals[4],
        totals[5],
        totals[6],
        totals[7],
        totals[8],
        totals[9],
    )


def solution(mesh):
    in_specs = (
        P(("shard", "rep"), None, None),
        P(("shard", "rep"), None, None),
        P(("shard", "rep"), None),
        P(("shard", "rep")),
        P(None, "shard", None),
        P(None, "shard"),
        P(None, "shard", None),
        P(None, "shard"),
        P(None, "shard", None),
        P(None, "shard"),
        P(None, "shard", None),
        P(None, "shard"),
        P(None, "shard", None),
        P(None, "shard"),
        P(("shard", "rep"), None, None),
        P(("shard", "rep"), None, None),
    )
    out_specs = (
        P(("shard", "rep"), None, None),
        P(("shard", "rep"), None, None),
        P(("shard", "rep"), None, None),
        P(("shard", "rep"), None, None),
        P(("shard", "rep"), None),
        P(None, "shard", None),
        P(None, "shard"),
        P(None, "shard", None),
        P(None, "shard"),
        P(None, "shard", None),
        P(None, "shard"),
        P(None, "shard", None),
        P(None, "shard"),
        P(None, "shard", None),
        P(None, "shard"),
    )
    return jax.shard_map(body, mesh=mesh, in_specs=in_specs, out_specs=out_specs, check_vma=False)
```

profile of v0, /device:TPU:0, one launch (start us, length us, event | category | flops | bytes accessed | tf_op | source)
XLA Modules:
  0.0 2340.6 jit_solution(3968276200672782012)
XLA Ops:
  8.0 10.6 all-gather
  18.6 7.1 fusion.38
  25.8 5.2 convert_element_type.338
  34.0 6.6 convert_element_type.355
  40.7 6.6 convert_element_type.360
  48.2 9.2 all_gather.38
  57.5 7.8 all-gather.1
  65.4 9.0 all-gather.2
  75.7 7.8 all_gather.40
  83.5 9.2 all_gather.44
  96.8 127.0 %all-gather.8.cloned.1.call-done = bf16[2,1536,4608]{2,1,0:T(8,128)(2,1)} async-done(((bf16[2,192,4608]{2,1,0:T(8,128)(2,1)}), bf16[2,1536,4608]{2,1,0:T(8,128)(2,1)}) %all-gather.8.cloned.1.call-update) | async-done | bytes 28311568 | tf_op jit(solution)/shard_map/all_gather | solution.py:64
  223.8 7.1 fusion.19
  231.0 8.8 fusion.18
  241.0 2.9 copy.136
  246.0 3.2 multiply_reduce_fusion.1
  253.9 30.8 %all-gather.10.cloned.1.call-done = bf16[2,1536,1536]{2,1,0:T(8,128)(2,1)} async-done(((bf16[2,192,1536]{2,1,0:T(8,128)(2,1)}), bf16[2,1536,1536]{2,1,0:T(8,128)(2,1)}) %all-gather.10.cloned.1.call-update) | async-done | bytes 9437200 | tf_op jit(solution)/shard_map/all_gather | solution.py:66
  284.7 4.3 fusion.139
  292.7 173.1 %all-gather.12.cloned.1.call-done = bf16[2,1536,6144]{2,1,0:T(8,128)(2,1)} async-done(((bf16[2,192,6144]{2,1,0:T(8,128)(2,1)}), bf16[2,1536,6144]{2,1,0:T(8,128)(2,1)}) %all-gather.12.cloned.1.call-update) | async-done | bytes 37748752 | tf_op jit(solution)/shard_map/all_gather | solution.py:117
  465.9 12.5 fusion.13
  478.4 168.6 %all-gather.14.cloned.1.call-done = bf16[2,6144,1536]{2,1,0:T(8,128)(2,1)} async-done(((bf16[2,768,1536]{2,1,0:T(8,128)(2,1)}), bf16[2,6144,1536]{2,1,0:T(8,128)(2,1)}) %all-gather.14.cloned.1.call-update) | async-done | bytes 37748752 | tf_op jit(solution)/shard_map/all_gather | solution.py:119
  647.0 12.7 fusion.142
  659.7 11.2 multiply_reduce_fusion.5
  671.0 10.6 multiply_reduce_fusion.2
  684.7 4.1 bitcast_convert_fusion.6
  689.9 8.7 fusion.14
  698.7 13.3 fusion.143
  711.9 10.9 multiply_reduce_fusion.10
  722.9 9.7 multiply_reduce_fusion.7
  735.5 3.6 bitcast_convert_fusion.7
  740.1 4.1 fusion.53
  744.2 4.0 fusion.52
  749.3 6.6 fusion.55
  755.9 2.7 copy.123
  758.6 9.3 multiply_reduce_fusion
  767.9 6.1 multiply_convert_fusion
  778.3 2.5 copy.122
  780.8 3.9 multiply_convert_fusion.3
  786.4 8.8 bitcast_convert_fusion.4
  798.7 7.3 bitcast_convert_fusion.5
  807.2 14.8 bitcast_convert_fusion.2
  823.2 10.9 bitcast_convert_fusion.3
  835.2 12.9 bitcast_convert_fusion
  849.2 12.2 bitcast_convert_fusion.1
  861.5 8.4 fusion.84
  870.8 8.4 fusion.75
  885.4 12.9 all_gather.47
  898.3 5.8 fusion.12
  908.0 104.8 %reduce-scatter.10.cloned.1.call-done = bf16[192,4608]{1,0:T(8,128)(2,1)} async-done(((bf16[1536,4608]{1,0:T(8,128)(2,1)}), bf16[192,4608]{1,0:T(8,128)(2,1)}) %reduce-scatter.10.cloned.1.call-update) | async-done | bytes 1769488 | tf_op jit(solution)/shard_map/reduce_scatter | solution.py:261
  1012.7 4.1 pad_maximum_fusion.2
  1016.8 125.9 %reduce-scatter.20.cloned.1.call-done = bf16[192,6144]{1,0:T(8,128)(2,1)} async-done(((bf16[1536,6144]{1,0:T(8,128)(2,1)}), bf16[192,6144]{1,0:T(8,128)(2,1)}) %reduce-scatter.20.cloned.1.call-update) | async-done | bytes 2359312 | tf_op jit(solution)/shard_map/reduce_scatter | solution.py:169
  1142.8 130.2 %reduce-scatter.18.cloned.1.call-done = bf16[192,6144]{1,0:T(8,128)(2,1)} async-done(((bf16[1536,6144]{1,0:T(8,128)(2,1)}), bf16[192,6144]{1,0:T(8,128)(2,1)}) %reduce-scatter.18.cloned.1.call-update) | async-done | bytes 2359312 | tf_op jit(solution)/shard_map/reduce_scatter | solution.py:169
  1273.0 5.0 pad_maximum_fusion
  1278.0 125.1 %reduce-scatter.24.cloned.1.call-done = bf16[768,1536]{1,0:T(8,128)(2,1)} async-done(((bf16[6144,1536]{1,0:T(8,128)(2,1)}), bf16[768,1536]{1,0:T(8,128)(2,1)}) %reduce-scatter.24.cloned.1.call-update) | async-done | bytes 2359312 | tf_op jit(solution)/shard_map/reduce_scatter | solution.py:175
  1403.0 130.2 %reduce-scatter.22.cloned.1.call-done = bf16[768,1536]{1,0:T(8,128)(2,1)} async-done(((bf16[6144,1536]{1,0:T(8,128)(2,1)}), bf16[768,1536]{1,0:T(8,128)(2,1)}) %reduce-scatter.22.cloned.1.call-update) | async-done | bytes 2359312 | tf_op jit(solution)/shard_map/reduce_scatter | solution.py:175
  1533.2 5.0 pad_maximum_fusion.1
  1538.3 7.0 fusion.68
  1545.9 3.3 all-to-all-start
  1555.0 37.3 %all-reduce.20.cloned.1.call-done = (bf16[9216]{0:T(1024)(128)(2,1)}, bf16[9216]{0:T(1024)(128)(2,1)}, bf16[3072]{0:T(1024)(128)(2,1)}, bf16[3072]{0:T(1024)(128...) async-done(((bf16[9216]{0:T(1024)(128)(2,1)}, ...) | async-done | bytes 86032
  1600.0 20.4 all-reduce.12
  1623.3 684.3 %all-reduce.22.cloned.1.call-done = (bf16[2,192,9216]{2,1,0:T(8,128)(2,1)}, bf16[2,192,4608]{2,1,0:T(8,128)(2,1)}, bf16[2,192,1536]{2,1,0:T(8,128)(2,1)}, bf16[2...) async-done(((bf16[2,192,9216]{2,1,0:T(8,128)(2,1)}, bf16[2,192,4608]{2,1,0:T(8,128)(2,1)}, bf16[2,192,1536]{2,1,0:T(8,128)(2,1)}, bf16[2,192,6144]{2,1,0:T(8,128)(2,1)}, ...) | async-done | bytes 21233680 | tf_op jit(solution)/shard_map/psum | solution.py:297
  2307.5 10.2 convert_element_type.392
  2317.7 4.2 convert_element_type.399
  2323.7 4.9 convert_element_type.409
  2328.6 5.1 convert_element_type.413
  (327 shorter events, 70.6 us)
Async XLA Ops:
  7.2 88.3 %all-reduce.18.cloned.1.call-start = ((), (), s32[]{:S(2)}) async-start(), calls=%async_computation.21 | async-start | bytes 2359296
  18.6 7.2 copy-start.49
  25.8 198.0 %all-gather.8.cloned.1.call-start = ((), (), s32[]{:S(2)}) async-start(), calls=%async_computation.9 | async-start | bytes 31850496 | tf_op jit(solution)/shard_map/all_gather | solution.py:64
  31.0 253.7 %all-gather.10.cloned.1.call-start = ((), (), s32[]{:S(2)}) async-start(), calls=%async_computation.10 | async-start | bytes 10616832 | tf_op jit(solution)/shard_map/all_gather | solution.py:66
  33.9 431.9 %all-gather.12.cloned.1.call-start = ((), (), s32[]{:S(2)}) async-start(), calls=%async_computation.11 | async-start | bytes 42467328 | tf_op jit(solution)/shard_map/all_gather | solution.py:117
  40.7 606.4 %all-gather.14.cloned.1.call-start = ((), (), s32[]{:S(2)}) async-start(), calls=%async_computation.12 | async-start | bytes 42467328 | tf_op jit(solution)/shard_map/all_gather | solution.py:119
  47.3 10.2 copy-start.76
  47.3 18.1 copy-start.75
  47.3 18.1 copy-start.69
  47.3 18.1 copy-start.77
  47.3 27.2 %copy-start.78 = (u32[32]{0:T(128)S(1)}, u32[32]{0:T(128)}, u32[]{:S(2)}) copy-start(u32[32]{0:T(128)} %constant.86) | copy-start | bytes 388
  47.3 46.7 %copy-start.6 = (bf16[2,64,1536]{2,1,0:T(8,128)(2,1)S(1)}, bf16[2,64,1536]{2,1,0:T(8,128)(2,1)}, u32[]{:S(2)}) copy-start(bf16[2,64,1536]{2,1,0:T(8,128)(2,1)} %param.16) | copy-start | bytes 1179652
  47.3 47.1 %copy-start.3 = (bf16[2,77,1536]{2,0,1:T(2,128)(2,1)S(1)}, bf16[2,77,1536]{2,0,1:T(2,128)(2,1)}, u32[]{:S(2)}) copy-start(bf16[2,77,1536]{2,0,1:T(2,128)(2,1)} %param.17) | copy-start | bytes 1419268
  47.3 857.1 %reduce-scatter.16.cloned.1.call-start = ((), (), s32[]{:S(2)}) async-start(), calls=%async_computation.16 | async-start | bytes 5308416 | tf_op jit(solution)/shard_map/reduce_scatter | solution.py:273
  94.1 136.8 %copy-start.54 = (f32[2,64]{1,0:T(2,128)}, f32[2,64]{1,0:T(2,128)S(1)}, u32[]{:S(2)}) copy-start(f32[2,64]{1,0:T(2,128)S(1)} %broadcast_multiply_fusion.3) | copy-start | bytes 1540
  94.5 136.5 %copy-start.56 = (f32[2,77]{1,0:T(2,128)}, f32[2,77]{1,0:T(2,128)S(1)}, u32[]{:S(2)}) copy-start(f32[2,77]{1,0:T(2,128)S(1)} %broadcast_multiply_fusion.1) | copy-start | bytes 1852
  95.4 135.6 %copy-start.60 = (f32[2,77]{1,0:T(2,128)}, f32[2,77]{1,0:T(2,128)S(1)}, u32[]{:S(2)}) copy-start(f32[2,77]{1,0:T(2,128)S(1)} %fusion.124) | copy-start | bytes 1852
  95.4 135.6 %copy-start.58 = (f32[2,64]{1,0:T(2,128)}, f32[2,64]{1,0:T(2,128)S(1)}, u32[]{:S(2)}) copy-start(f32[2,64]{1,0:T(2,128)S(1)} %fusion.123) | copy-start | bytes 1540
  96.8 134.2 %copy-start.45 = (f32[2,1536]{1,0:T(2,128)}, f32[2,1536]{1,0:T(2,128)S(1)}, u32[]{:S(2)}) copy-start(f32[2,1536]{1,0:T(2,128)S(1)} %get-tuple-element.160) | copy-start | bytes 36868
  96.8 134.2 %copy-start.50 = (f32[2,1536]{1,0:T(2,128)}, f32[2,1536]{1,0:T(2,128)S(1)}, u32[]{:S(2)}) copy-start(f32[2,1536]{1,0:T(2,128)S(1)} %get-tuple-element.159) | copy-start | bytes 36868
  96.8 134.2 %copy-start.47 = (f32[2,1536]{1,0:T(2,128)}, f32[2,1536]{1,0:T(2,128)S(1)}, u32[]{:S(2)}) copy-start(f32[2,1536]{1,0:T(2,128)S(1)} %get-tuple-element.158) | copy-start | bytes 36868
  96.8 134.2 %copy-start.52 = (f32[2,1536]{1,0:T(2,128)}, f32[2,1536]{1,0:T(2,128)S(1)}, u32[]{:S(2)}) copy-start(f32[2,1536]{1,0:T(2,128)S(1)} %get-tuple-element.157) | copy-start | bytes 36868
  284.7 5.7 copy-start.2
  292.4 389.2 %copy-start.4 = (f32[2,77,1536]{2,1,0:T(8,128)}, f32[2,77,1536]{2,1,0:T(8,128)S(1)}, u32[]{:S(2)}) copy-start(f32[2,77,1536]{2,1,0:T(8,128)S(1)} %get-tuple-element.128) | copy-start | bytes 2838532
  465.9 181.2 %copy-start.73 = (f32[2]{0:T(128)S(1)}, f32[2]{0:T(128)}, u32[]{:S(2)}) copy-start(f32[2]{0:T(128)} %compare_convert_fusion) | copy-start | bytes 28
  659.7 11.2 copy-start.32
  659.7 11.3 copy-start.43
  659.7 11.3 copy-start.68
  659.7 11.3 copy-start.79
  688.8 215.7 %reduce-scatter.14.cloned.1.call-start = ((), (), s32[]{:S(2)}) async-start(), calls=%async_computation.15 | async-start | bytes 5308416 | tf_op jit(solution)/shard_map/reduce_scatter | solution.py:273
  689.9 8.7 copy-start.36
  698.6 24.3 %copy-start.20 = (f32[2,64,6144]{2,1,0:T(8,128)}, f32[2,64,6144]{2,1,0:T(8,128)S(1)}, u32[]{:S(2)}) copy-start(f32[2,64,6144]{2,1,0:T(8,128)S(1)} %fusion.14) | copy-start | bytes 9437188
  711.9 11.0 copy-start.40
  739.1 168.9 %reduce-scatter.12.cloned.1.call-start = ((), (), s32[]{:S(2)}) async-start(), calls=%async_computation.14 | async-start | bytes 15925248 | tf_op jit(solution)/shard_map/reduce_scatter | solution.py:261
  749.3 6.6 copy-start.11
  755.9 12.0 slice-start
  758.6 9.3 slice-start.1
  767.9 7.9 copy-start.14
  780.7 5.6 copy-start.15
  780.7 5.6 copy-start.48
  780.7 5.6 copy-start.53
  780.8 5.6 copy-start.57
  780.8 5.6 copy-start.61
  786.4 8.8 copy-start.18
  795.3 217.4 %reduce-scatter.10.cloned.1.call-start = ((), (), s32[]{:S(2)}) async-start(), calls=%async_computation.13 | async-start | bytes 15925248 | tf_op jit(solution)/shard_map/reduce_scatter | solution.py:261
  806.0 336.8 %reduce-scatter.20.cloned.1.call-start = ((), (), s32[]{:S(2)}) async-start(), calls=%async_computation.18 | async-start | bytes 21233664 | tf_op jit(solution)/shard_map/reduce_scatter | solution.py:169
  822.0 451.0 %reduce-scatter.18.cloned.1.call-start = ((), (), s32[]{:S(2)}) async-start(), calls=%async_computation.17 | async-start | bytes 21233664 | tf_op jit(solution)/shard_map/reduce_scatter | solution.py:169
  834.2 568.8 %reduce-scatter.24.cloned.1.call-start = ((), (), s32[]{:S(2)}) async-start(), calls=%async_computation.20 | async-start | bytes 21233664 | tf_op jit(solution)/shard_map/reduce_scatter | solution.py:175
  848.1 685.1 %reduce-scatter.22.cloned.1.call-start = ((), (), s32[]{:S(2)}) async-start(), calls=%async_computation.19 | async-start | bytes 21233664 | tf_op jit(solution)/shard_map/reduce_scatter | solution.py:175
  861.4 8.5 copy-start.66
  861.4 9.4 copy-start.17
  861.4 730.9 %all-reduce.20.cloned.1.call-start = ((), (), s32[]{:S(2)}) async-start(), calls=%async_computation.22 | async-start | bytes 180224
  861.4 9.3 copy-start.19
  870.8 8.5 copy-start.64
  870.8 9.3 copy-start.24
  870.8 9.3 copy-start.25
  904.1 1403.4 %all-reduce.22.cloned.1.call-start = ((), (), s32[]{:S(2)}) async-start(), calls=%async_computation.23 | async-start | bytes 42467328 | tf_op jit(solution)/shard_map/psum | solution.py:297
  1538.2 13.5 copy-start.42
  1538.2 14.8 copy-start.33
  1538.2 16.1 copy-start.62
  1545.9 8.3 all-to-all-start
  2307.5 10.2 copy-start.26
  2317.7 5.9 copy-start.23
  2322.0 6.6 slice-start.2
  (36 other events, 77.0 us)
Sparse Core Ops, SparseCore 0:
  25.9 57.3 all-reduce.17
  86.0 137.7 all-gather.7
  225.9 58.8 all-gather.9
  287.2 178.6 all-gather.11
  468.4 178.6 all-gather.13
  688.9 53.8 reduce-scatter.15
  746.3 53.8 reduce-scatter.13
  804.8 103.1 reduce-scatter.11
  912.0 100.6 reduce-scatter.9
  1016.6 126.0 reduce-scatter.19
  1146.8 126.0 reduce-scatter.17
  1276.9 126.0 reduce-scatter.23
  1407.1 126.0 reduce-scatter.21
  1539.1 53.1 all-reduce.19
  1596.4 711.0 all-reduce.21
where the time goes:
time: 2350 us; the launch traced here: 2340 us
  waiting for transfers between devices  1840 us (78%)
  matrix products  258 us (11%)
  other arithmetic  90.3 us (4%)
  blocking collectives  86.8 us (4%)
  local copies, waits for them, and re-layouts  42.8 us (2%)
    psum x1, waiting for transfers between devices, body(): lax.psum(adaptive_share.astype(jnp.bfloat16), 'rep').astype(jnp.float32)  684 us
    dot_general x33, matrix products, project(): return jnp.einsum(form, left, right, preferred_element_type=WIDE)  258 us
    reduce_scatter x2, waiting for transfers between devices, body(): lax.psum_scatter(expand_grad.astype(jnp.bfloat16), 'shard', scatter_dimen...  256 us
    reduce_scatter x2, waiting for transfers between devices, body(): lax.psum_scatter(reduce_grad.astype(jnp.bfloat16), 'shard', scatter_dimen...  255 us
    all_gather x1, waiting for transfers between devices, body(): lax.all_gather(expand_weight.astype(LOWER), 'shard', axis=1, tiled=True)  173 us
    all_gather x1, waiting for transfers between devices, body(): lax.all_gather(reduce_weight.astype(LOWER), 'shard', axis=1, tiled=True)  169 us
    all_gather x1, waiting for transfers between devices, body(): lax.all_gather(attend_weight.astype(LOWER), 'shard', axis=1, tiled=True)  127 us
    reduce_scatter x2, waiting for transfers between devices, body(): lax.psum_scatter(attend_grads[which].astype(jnp.bfloat16), 'shard', scatt...  106 us
  transfers between devices with their start and end apart: 16, of which 12 were waited for; matrix products, arithmetic and copies ran while one was open for 13% of the time, Pallas kernels for 0%

commit v1 on v0

--- a/solution.py
+++ b/solution.py
@@ -1,6 +1,8 @@
 import jax
 import jax.numpy as jnp
 from jax import lax
+from jax.experimental import pallas as pl
+from jax.experimental.pallas import tpu as pltpu
 from jax.sharding import PartitionSpec as P
 
 HEADS = 24
@@ -34,7 +36,7 @@
     return jax.nn.gelu(values, approximate=True)
 
 
-def body(
+def gathered_body(
     image,
     text,
     condition,
@@ -325,6 +327,452 @@
     )
 
 
+GROUP = 8
+REPLICAS = 4
+SPAN = 80
+ORDER_ONE = (2, 4, 1)
+ORDER_TWO = (4, 2, 1)
+
+
+def distances(order):
+    found = [0]
+    for step in order:
+        found = found + [item ^ step for item in found]
+    return found
+
+
+def swap(array, step):
+    return lax.ppermute(array, "shard", [(item, item ^ step) for item in range(GROUP)])
+
+
+def collect(array, order):
+    for step in order:
+        array = jnp.concatenate([array, swap(array, step)], axis=0)
+    return array
+
+
+def scatter_sum(array, order):
+    for step in reversed(order):
+        half = array.shape[0] // 2
+        other = swap(array[half:], step)
+        array = array[:half].astype(WIDE) + other.astype(WIDE)
+        if step != order[0]:
+            array = array.astype(LOWER)
+    return array
+
+
+def exchange(blocks, order):
+    return [
+        block if step == 0 else swap(block, step)
+        for block, step in zip(blocks, distances(order), strict=True)
+    ]
+
+
+def contract(left, right, dims):
+    return lax.dot_general(left, right, (dims, ((), ())), preferred_element_type=WIDE)
+
+
+def head_softmax(query, key, length):
+    scores = contract(query, key, ((1,), (1,))) * (query.shape[-1] ** (-0.5))
+    column = lax.broadcasted_iota(jnp.int32, scores.shape, 1)
+    scores = jnp.where(column < length, scores, -1e30)
+    raised = jnp.exp(scores - jnp.max(scores, axis=-1, keepdims=True))
+    return raised / jnp.sum(raised, axis=-1, keepdims=True)
+
+
+def attend_kernel(size, length, image_ref, text_ref, out_ref):
+    joint = jnp.concatenate([image_ref[0], text_ref[0]], axis=0)
+    width = joint.shape[1] // 3
+    found = []
+    for at in range(0, width, size):
+        query = joint[:, at : at + size]
+        key = joint[:, width + at : width + at + size]
+        value = joint[:, 2 * width + at : 2 * width + at + size]
+        probs = head_softmax(query, key, length)
+        found.append(contract(probs.astype(LOWER), value, ((1,), (0,))).astype(LOWER))
+    out_ref[0] = jnp.concatenate(found, axis=1)
+
+
+def attend_back_kernel(
+    size, length, image_ref, text_ref, grad_ref, image_out_ref, text_out_ref
+):
+    joint = jnp.concatenate([image_ref[0], text_ref[0]], axis=0)
+    grad = grad_ref[0]
+    width = joint.shape[1] // 3
+    factor = size ** (-0.5)
+    d_queries, d_keys, d_values = [], [], []
+    for at in range(0, width, size):
+        query = joint[:, at : at + size]
+        key = joint[:, width + at : width + at + size]
+        value = joint[:, 2 * width + at : 2 * width + at + size]
+        d_out = grad[:, at : at + size]
+        probs = head_softmax(query, key, length)
+        d_probs = contract(d_out, value, ((1,), (1,)))
+        center = jnp.sum(probs * d_probs, axis=-1, keepdims=True)
+        d_scores = (probs * (d_probs - center)).astype(LOWER)
+        d_queries.append((contract(d_scores, key, ((1,), (0,))) * factor).astype(LOWER))
+        d_keys.append((contract(d_scores, query, ((0,), (0,))) * factor).astype(LOWER))
+        d_values.append(contract(probs.astype(LOWER), d_out, ((0,), (0,))).astype(LOWER))
+    whole = jnp.concatenate(d_queries + d_keys + d_values, axis=1)
+    split_at = image_ref.shape[1]
+    image_out_ref[0] = whole[:split_at]
+    text_out_ref[0] = whole[split_at:]
+
+
+def block_of(rows, columns, swapped=False):
+    def place(index):
+        if not swapped:
+            return (index, 0, 0)
+        slot, low, high, top = index % 2, (index // 2) % 2, (index // 4) % 2, index // 8
+        return (slot + 4 * low + 2 * high + 8 * top, 0, 0)
+
+    return pl.BlockSpec((1, rows, columns), place)
+
+
+def attend_forward(image, text, size, length):
+    count, rows, columns = image.shape
+    more = text.shape[1]
+    return pl.pallas_call(
+        lambda *refs: attend_kernel(size, length, *refs),
+        out_shape=jax.ShapeDtypeStruct((count, rows + more, columns // 3), LOWER),
+        grid=(count,),
+        in_specs=[block_of(rows, columns), block_of(more, columns, True)],
+        out_specs=block_of(rows + more, columns // 3),
+        cost_estimate=pl.CostEstimate(
+            flops=4 * count * (rows + more) ** 2 * columns // 3,
+            bytes_accessed=3 * count * (rows + more) * columns,
+            transcendentals=count * (rows + more) ** 2 * 3,
+        ),
+        name="attend",
+    )(image, text)
+
+
+def attend_backward(image, text, grad, size, length):
+    count, rows, columns = image.shape
+    more = text.shape[1]
+    return pl.pallas_call(
+        lambda *refs: attend_back_kernel(size, length, *refs),
+        out_shape=(
+            jax.ShapeDtypeStruct(image.shape, LOWER),
+            jax.ShapeDtypeStruct(text.shape, LOWER),
+        ),
+        grid=(count,),
+        in_specs=[
+            block_of(rows, columns),
+            block_of(more, columns, True),
+            block_of(rows + more, columns // 3),
+        ],
+        out_specs=(block_of(rows, columns), block_of(more, columns, True)),
+        cost_estimate=pl.CostEstimate(
+            flops=10 * count * (rows + more) ** 2 * columns // 3,
+            bytes_accessed=5 * count * (rows + more) * columns,
+            transcendentals=count * (rows + more) ** 2 * 3,
+        ),
+        name="attend_back",
+    )(image, text, grad)
+
+
+def split_body(
+    image,
+    text,
+    condition,
+    counts,
+    adaptive_weight,
+    adaptive_bias,
+    attend_weight,
+    attend_bias,
+    output_weight,
+    output_bias,
+    expand_weight,
+    expand_bias,
+    reduce_weight,
+    reduce_bias,
+    image_cotangent,
+    text_cotangent,
+):
+    slots, rows, width = image.shape
+    extra = text.shape[1]
+    me = lax.axis_index("shard")
+    share = width // GROUP
+    size = width // HEADS
+    orders = (ORDER_ONE, ORDER_TWO)
+    spans = (rows, SPAN)
+
+    def padded(array):
+        return jnp.pad(array, ((0, 0), (0, SPAN - extra), (0, 0)))
+
+    alive = (jnp.arange(slots, dtype=jnp.int32) < counts[0]).astype(WIDE)[:, None, None]
+    streams = (image.astype(WIDE), padded(text).astype(WIDE))
+    cotangents = (image_cotangent.astype(WIDE) * alive, padded(text_cotangent).astype(WIDE) * alive)
+    cond_value = condition.astype(WIDE)
+    cond_low = jax.nn.silu(cond_value).astype(LOWER)
+
+    small = jnp.concatenate(
+        [
+            cond_low,
+            *[
+                item.astype(LOWER)
+                for item in (adaptive_bias, attend_bias, output_bias, expand_bias, reduce_bias)
+            ],
+        ],
+        axis=1,
+    )
+    small_all = lax.all_gather(small, "shard", axis=0, tiled=False)
+    cond_group = small_all[:, :, :width].reshape(GROUP * slots, width)
+    cond_cols = lax.dynamic_slice_in_dim(cond_group, me * share, share, 1)
+
+    def whole_bias(start, length):
+        piece = small_all[:, :, start : start + length]
+        return jnp.moveaxis(piece, 0, 1).reshape(2, GROUP * length).astype(WIDE)
+
+    at = width
+    biases = []
+    for item in (adaptive_bias, attend_bias, output_bias, expand_bias, reduce_bias):
+        biases.append(whole_bias(at, item.shape[1]))
+        at += item.shape[1]
+    adaptive_bias_full, attend_bias_full, output_bias_full, _, reduce_bias_full = biases
+    expand_bias_own = expand_bias.astype(LOWER).astype(WIDE)
+
+    adaptive_local = adaptive_weight.astype(LOWER)
+    partial_terms = project("gd,sde->gse", cond_cols, adaptive_local)
+    arrived = lax.all_to_all(partial_terms, "shard", split_axis=0, concat_axis=0, tiled=True)
+    modulation = (
+        jnp.sum(arrived.reshape(GROUP, slots, 2, 6 * width), axis=0) + adaptive_bias_full[None]
+    )
+    parts = [
+        [modulation[:, which, piece * width : (piece + 1) * width] for piece in range(6)]
+        for which in range(2)
+    ]
+
+    attend_low = attend_weight.astype(LOWER).reshape(2, share, 3, GROUP, share)
+    attend_own = lax.all_to_all(attend_low, "shard", split_axis=3, concat_axis=1, tiled=True)
+    attend_own = attend_own.reshape(2, width, 3 * share)
+    expand_own = lax.all_to_all(
+        expand_weight.astype(LOWER), "shard", split_axis=2, concat_axis=1, tiled=True
+    )
+    reduce_own = reduce_weight.astype(LOWER)
+    output_low = output_weight.astype(LOWER)
+    output_full = [collect(output_low[which], orders[which]) for which in range(2)]
+
+    fronts = []
+    triples = []
+    query_bias = lax.dynamic_slice_in_dim(attend_bias_full, me * share, share, 1)
+    value_bias = lax.dynamic_slice_in_dim(attend_bias_full, width + me * share, share, 1)
+    triple_bias = jnp.concatenate([query_bias, jnp.zeros_like(query_bias), value_bias], axis=1)
+    for which in range(2):
+        hidden = modulate(streams[which], parts[which][0], parts[which][1]).astype(LOWER)
+        front = collect(hidden, orders[which])
+        front = front.reshape(GROUP * slots * spans[which], width)
+        fronts.append(front)
+        triple = (project("rd,de->re", front, attend_own[which]) + triple_bias[which]).astype(LOWER)
+        triples.append(triple.reshape(GROUP * slots, spans[which], 3 * share))
+    attended = attend_forward(triples[0], triples[1], size, rows + extra)
+
+    blocks = attended.reshape(GROUP, slots, rows + SPAN, share)
+    arrived = dict(
+        zip(
+            distances(ORDER_ONE),
+            exchange([blocks[item] for item in range(GROUP)], ORDER_ONE),
+            strict=True,
+        )
+    )
+    branches = []
+    middles = []
+    feeds = []
+    d_seconds = []
+    for which in range(2):
+        low, high = (0, rows) if which == 0 else (rows, rows + SPAN)
+        own = jnp.concatenate(
+            [arrived[item][:, low:high] for item in distances(orders[which])], axis=-1
+        )
+        branch = project("grd,de->gre", own, output_full[which]) + output_bias_full[which]
+        middle = streams[which] + parts[which][2][:, None, :] * branch
+        hidden = modulate(middle, parts[which][3], parts[which][4]).astype(LOWER)
+        branches.append(branch)
+        middles.append(middle)
+        feeds.append(collect(hidden, orders[which]).reshape(-1, width))
+        d_second = (cotangents[which] * parts[which][5][:, None, :]).astype(LOWER)
+        d_seconds.append(collect(d_second, orders[which]).reshape(-1, width))
+
+    outputs = []
+    feed_mods = []
+    d_middles = []
+    expand_grads = []
+    expand_bias_grads = []
+    reduce_grads = []
+    reduce_bias_grads = []
+    d_branches = []
+    gate_front = []
+    d_pieces = []
+    for which in range(2):
+        part = parts[which]
+        before = project("rd,df->rf", feeds[which], expand_own[which]) + expand_bias_own[which]
+        active = smooth_gelu(before).astype(LOWER)
+        d_active = project("rd,fd->rf", d_seconds[which], reduce_own[which])
+        d_before = jax.vjp(smooth_gelu, before)[1](d_active)[0].astype(LOWER)
+        d_hidden = project("rf,df->rd", d_before, expand_own[which]).astype(LOWER)
+        d_hidden = d_hidden.reshape(GROUP * slots, spans[which], width)
+        d_hidden = scatter_sum(d_hidden, orders[which])
+        reduce_grads.append(project("rf,rd->fd", active, d_seconds[which]).astype(LOWER))
+        expand_grads.append(project("rd,rf->df", feeds[which], d_before).astype(LOWER))
+        expand_bias_grads.append(jnp.sum(d_before, axis=0, dtype=WIDE))
+        d_cols = lax.dynamic_slice_in_dim(d_seconds[which], me * share, share, 1)
+        reduce_bias_grads.append(jnp.sum(d_cols, axis=0, dtype=WIDE))
+        second = project("rf,fd->rd", active, reduce_own[which]).astype(LOWER)
+        second = second.reshape(GROUP * slots, spans[which], width)
+        second = scatter_sum(second, orders[which]) + reduce_bias_full[which]
+        outputs.append(((middles[which] + part[5][:, None, :] * second) * alive).astype(LOWER))
+        d_gate_feed = jnp.sum(cotangents[which] * second, axis=1)
+        d_mid, d_shift_feed, d_scale_feed = jax.vjp(modulate, middles[which], part[3], part[4])[1](
+            d_hidden
+        )
+        feed_mods.append((d_shift_feed, d_scale_feed, d_gate_feed))
+        d_middle = cotangents[which] + d_mid
+        d_middles.append(d_middle)
+        d_branch = (d_middle * part[2][:, None, :]).astype(LOWER)
+        gate_front.append(jnp.sum(d_middle * branches[which], axis=1))
+        d_branches.append(d_branch)
+        d_piece = project("gre,de->grd", d_branch, output_full[which]).astype(LOWER)
+        d_piece = d_piece.reshape(slots, spans[which], GROUP, share)
+        if which == 1:
+            d_piece = jnp.stack(
+                [
+                    d_piece[:, :, distances(ORDER_TWO).index(item)]
+                    for item in distances(ORDER_ONE)
+                ],
+                axis=2,
+            )
+        d_pieces.append(d_piece)
+    d_joint = jnp.concatenate(d_pieces, axis=1)
+    d_blocks = exchange([d_joint[:, :, item] for item in range(GROUP)], ORDER_ONE)
+    d_attended = jnp.concatenate(d_blocks, axis=0)
+    d_triples = attend_backward(triples[0], triples[1], d_attended, size, rows + extra)
+
+    output_grads = []
+    output_bias_grads = []
+    attend_grads = []
+    attend_bias_grads = []
+    input_grads = []
+    d_mods = []
+    for which in range(2):
+        part = parts[which]
+        d_triple = d_triples[which].reshape(-1, 3 * share)
+        attend_grads.append(project("rd,re->de", fronts[which], d_triple).astype(LOWER))
+        column_sums = jnp.sum(d_triple, axis=0, dtype=WIDE)
+        attend_bias_grads.append(
+            jnp.concatenate([column_sums[:share], column_sums[2 * share :]]).astype(LOWER)
+        )
+        d_hidden = project("re,de->rd", d_triple, attend_own[which]).astype(LOWER)
+        d_hidden = scatter_sum(
+            d_hidden.reshape(GROUP * slots, spans[which], width), orders[which]
+        )
+        d_stream, d_shift_front, d_scale_front = jax.vjp(
+            modulate, streams[which], part[0], part[1]
+        )[1](d_hidden)
+        input_grads.append((d_middles[which] + d_stream).astype(LOWER))
+        d_shift_feed, d_scale_feed, d_gate_feed = feed_mods[which]
+        d_mods.append(
+            jnp.concatenate(
+                [
+                    d_shift_front,
+                    d_scale_front,
+                    gate_front[which],
+                    d_shift_feed,
+                    d_scale_feed,
+                    d_gate_feed,
+                ],
+                axis=-1,
+            )
+        )
+        d_branch_all = collect(d_branches[which], orders[which])
+        pieces = attended[:, :rows] if which == 0 else attended[:, rows:]
+        if which == 1:
+            tall = pieces.reshape(GROUP, slots, SPAN, share)
+            pieces = jnp.concatenate(
+                [
+                    tall[distances(ORDER_ONE).index(item)]
+                    for item in distances(ORDER_TWO)
+                ],
+                axis=0,
+            )
+        output_grads.append(project("grd,gre->de", pieces, d_branch_all).astype(LOWER))
+        d_cols = lax.dynamic_slice_in_dim(d_branch_all, me * share, share, 2)
+        output_bias_grads.append(jnp.sum(d_cols, axis=(0, 1), dtype=WIDE))
+
+    reduce_total = lax.psum(jnp.stack(reduce_grads), "rep").astype(WIDE)
+    expand_back = lax.all_to_all(
+        jnp.stack(expand_grads), "shard", split_axis=1, concat_axis=2, tiled=True
+    )
+    expand_total = lax.psum(expand_back, "rep").astype(WIDE)
+    attend_back = jnp.stack(attend_grads).reshape(2, width, 3, 1, share)
+    attend_back = lax.all_to_all(attend_back, "shard", split_axis=1, concat_axis=3, tiled=True)
+    attend_back = attend_back.reshape(2, share, 3 * width)
+    attend_total, output_total = lax.psum((attend_back, jnp.stack(output_grads)), "rep")
+    attend_total = attend_total.astype(WIDE)
+    output_total = output_total.astype(WIDE)
+
+    d_modulation = jnp.stack(d_mods, axis=1).astype(LOWER)
+    packed = jnp.concatenate(
+        [
+            d_modulation.reshape(-1),
+            cond_low.reshape(-1),
+            *[item for item in attend_bias_grads],
+            *[item.astype(LOWER) for item in output_bias_grads],
+            *[item.astype(LOWER) for item in expand_bias_grads],
+            *[item.astype(LOWER) for item in reduce_bias_grads],
+        ]
+    )
+    across = lax.all_gather(packed, "rep", axis=0, tiled=False)
+    modulation_size = d_modulation.size
+    cond_size = cond_low.size
+    keep = modulation_size + cond_size + 4 * share
+    rest = jnp.sum(across[:, keep:], axis=0, dtype=WIDE)
+    output_bias_total = rest[: 2 * share].reshape(2, share)
+    expand_bias_total = rest[2 * share : 10 * share].reshape(2, 4 * share)
+    reduce_bias_total = rest[10 * share :].reshape(2, share)
+    every = lax.all_gather(across[:, :keep], "shard", axis=0, tiled=False)
+    modulation_all = every[:, :, :modulation_size].reshape(
+        GROUP, REPLICAS, slots, 2, 6 * width
+    )
+    cond_all = every[:, :, modulation_size : modulation_size + cond_size].reshape(
+        GROUP * REPLICAS * slots, width
+    )
+    bias_all = jnp.sum(every[:, :, modulation_size + cond_size :], axis=1, dtype=WIDE)
+    bias_all = bias_all.reshape(GROUP, 2, 2, share).transpose(1, 2, 0, 3).reshape(2, 2 * width)
+    attend_bias_total = lax.dynamic_slice_in_dim(bias_all, me * 2 * share, 2 * share, 1)
+    group_modulation = lax.dynamic_index_in_dim(
+        modulation_all, lax.axis_index("rep"), 1, keepdims=False
+    ).reshape(GROUP * slots, 2, 6 * width)
+    modulation_all = modulation_all.reshape(GROUP * REPLICAS * slots, 2, 6 * width)
+    adaptive_total = project(
+        "gd,gse->sde",
+        lax.dynamic_slice_in_dim(cond_all, me * share, share, 1),
+        modulation_all,
+    )
+    own_cols = lax.dynamic_slice_in_dim(modulation_all, me * 6 * share, 6 * share, 2)
+    adaptive_bias_total = jnp.sum(own_cols, axis=0, dtype=WIDE)
+    cond_parts = project("gse,sde->gd", group_modulation, adaptive_local)
+    d_cond_act = lax.all_to_all(cond_parts, "shard", split_axis=0, concat_axis=1, tiled=True)
+    condition_grad = jax.vjp(jax.nn.silu, cond_value)[1](d_cond_act)[0].astype(LOWER)
+    return (
+        outputs[0],
+        outputs[1][:, :extra],
+        input_grads[0],
+        input_grads[1][:, :extra],
+        condition_grad,
+        adaptive_total,
+        adaptive_bias_total,
+        attend_total,
+        attend_bias_total,
+        output_total,
+        output_bias_total,
+        expand_total,
+        expand_bias_total,
+        reduce_total,
+        reduce_bias_total,
+    )
+
+
 def solution(mesh):
     in_specs = (
         P(("shard", "rep"), None, None),
@@ -361,4 +809,6 @@
         P(None, "shard", None),
         P(None, "shard"),
     )
+    fits = mesh.shape["shard"] == GROUP and mesh.shape["rep"] == REPLICAS
+    body = split_body if fits else gathered_body
     return jax.shard_map(body, mesh=mesh, in_specs=in_specs, out_specs=out_specs, check_vma=False)

time: 2350 us -> 1480 us (0.63)
  waiting for transfers between devices: 1840 us -> 791 us
  local copies, waits for them, and re-layouts: 42.8 us -> 245 us
  matrix products: 258 us -> 118 us
  starting transfers between devices: 4.21 us -> 74.5 us
  blocking collectives: 86.8 us -> 25.2 us
  other arithmetic: 90.3 us -> 148 us
  Pallas kernels: 0 us -> 49.4 us
    reduce_scatter x8 -> x0, waiting for transfers between devices: 617 us -> none  [the longest x2 256 us: body(): lax.psum_scatter(expand_grad.astype(jnp.bfloat16), 'shard', scatter_dimen...]
    all_gather x4 -> x1, waiting for transfers between devices: 500 us -> 0.01 us  [split_body(): every = lax.all_gather(across[:, :keep], 'shard', axis=0, tiled=False)]
    ppermute x0 -> x62, waiting for transfers between devices: none -> 325 us  [swap(): lax.ppermute(array, 'shard', [(item, item ^ step) for item in range(GROUP)])]
    psum x1, waiting for transfers between devices: 684 us -> 435 us  [split_body(): lax.psum((attend_back, jnp.stack(output_grads)), 'rep')]
    dot_general x33 -> x27, matrix products: 258 us -> 118 us  [project(): return jnp.einsum(form, left, right, preferred_element_type=WIDE)]
    another operation x12 -> x6, local copies, waits for them, and re-layouts: 0.13 us -> 60.8 us  [the longest x1 33.7 us: split_body(): jnp.stack(expand_grads)]
    pallas_call x0 -> x2, Pallas kernels: none -> 49.4 us  [the longest x1 31.5 us: attend_backward(): pl.pallas_call(lambda *refs: attend_back_kernel(size, length, *refs), out...]
    ppermute x0 -> x62, starting transfers between devices: none -> 48.6 us  [swap(): lax.ppermute(array, 'shard', [(item, item ^ step) for item in range(GROUP)])]
  transfers between devices with their start and end apart: 16 -> 70, of which waited for: 12 -> 26; matrix products, arithmetic and copies ran while one was open for 13% -> 31% of each run, Pallas kernels for 0% -> 3%
where the time goes in v1:
time: 1480 us; the launch traced here: 1470 us
  waiting for transfers between devices  791 us (53%)
  local copies, waits for them, and re-layouts  245 us (17%)
  other arithmetic  148 us (10%)
  matrix products  118 us (8%)
  starting transfers between devices  74.5 us (5%)
  Pallas kernels  49.4 us (3%)
  blocking collectives  25.2 us (2%)
  between operations  19 us (1%)
    psum x1, waiting for transfers between devices, split_body(): lax.psum((attend_back, jnp.stack(output_grads)), 'rep')  435 us
    ppermute x62, waiting for transfers between devices, swap(): lax.ppermute(array, 'shard', [(item, item ^ step) for item in range(GROUP)])  325 us
    dot_general x27, matrix products, project(): return jnp.einsum(form, left, right, preferred_element_type=WIDE)  118 us
    ppermute x62, starting transfers between devices, swap(): lax.ppermute(array, 'shard', [(item, item ^ step) for item in range(GROUP)])  48.6 us
    concatenate x28, other arithmetic, collect(): array = jnp.concatenate([array, swap(array, step)], axis=0)  45.4 us
    unnamed x356, local copies, waits for them, and re-layouts  35.5 us
    another operation x1, local copies, waits for them, and re-layouts, split_body(): jnp.stack(expand_grads)  33.7 us
    pallas_call x1, Pallas kernels, attend_backward(): pl.pallas_call(lambda *refs: attend_back_kernel(size, length, *refs), out...  31.5 us
  transfers between devices with their start and end apart: 70, of which 26 were waited for; matrix products, arithmetic and copies ran while one was open for 31% of the time, Pallas kernels for 3%

profile of v1, /device:TPU:0, one launch (start us, length us, event | category | flops | bytes accessed | tf_op | source)
XLA Modules:
  0.0 1471.0 jit_solution(13175370846018230894)
XLA Ops:
  12.9 10.7 all-gather.3
  23.7 6.1 fusion.13
  47.3 5.2 convert_element_type.426
  52.4 7.9 reshape.364
  60.4 7.4 copy.180
  67.7 6.5 convert_element_type.438
  74.3 15.8 %copy.186 = bf16[2,192,6144]{1,0,2:T(2,128)(2,1)} copy(bf16[2,192,6144]{2,1,0:T(8,128)(2,1)} %convert_element_type.438) | data formatting | bytes 9437184 | tf_op jit(solution)/shard_map/convert_element_type | solution.py:551
  95.5 4.8 all-to-all-start.1
  108.6 79.2 %collective-permute-done = bf16[2,64,1536]{2,1,0:T(8,128)(2,1)S(1)} collective-permute-done((bf16[2,64,1536]{2,1,0:T(8,128)(2,1)S(1)}, bf16[2,64,1536]{2,1,0:T(8,128)(2,1)S(1)}, u32[]{:S(2)}, u32[]{:S(2)}) %collective-permute-start) | collective-permute-done | bytes 393248 | tf_op jit(solution)/shard_map/ppermute | solution.py:345
  192.6 24.0 %collective-permute-done.37 = bf16[2,80,1536]{2,1,0:T(8,128)(2,1)S(1)} collective-permute-done((bf16[2,80,1536]{2,1,0:T(8,128)(2,1)S(1)}, bf16[2,80,1536]{2,1,0:T(8,128)(2,1)S(1)}, u32[]{:S(2)}, u32[]{:S(2)}) %collective-permute-start.37) | collective-permute-done | bytes 491552 | tf_op jit(solution)/shard_map/ppermute | solution.py:345
  227.5 6.4 collective-permute-done.32
  240.9 4.7 all-to-all-start.2
  245.6 4.2 fusion.114
  252.6 4.6 squeeze.36
  257.2 4.4 copy.181
  261.6 4.6 squeeze.35
  282.5 17.9 %attend.1 = bf16[16,144,192]{2,1,0:T(8,128)(2,1)} custom-call(bf16[16,64,576]{2,1,0:T(8,128)(2,1)} %bitcast.246, bf16[16,80,576]{2,1,0:T(8,128)(2,1)} %bitcast.244), custom_call_target="tpu_custom_call" | custom-call | flops 254803968 | bytes 3981312 | tf_op jit(solution)/shard_map/attend/pallas_call | solution.py:435
  309.6 10.3 collective-permute-done.12
  334.1 3.9 fusion.112
  341.5 4.4 fusion.110
  358.3 6.5 convert_element_type.441
  365.4 7.1 collective-permute-done.17
  375.0 6.1 collective-permute-done.25
  388.7 10.9 copy.213
  413.5 4.8 fusion.127
  438.6 5.6 fusion.128
  444.3 6.3 convolution_convert_fusion.2
  450.6 3.7 convolution_convert_fusion.1
  469.9 33.7 %copy.208 = bf16[2,1536,768]{2,0,1:T(2,128)(2,1)} copy(bf16[2,1536,768]{2,1,0:T(8,128)(2,1)S(1)} %pad_maximum_fusion.1) | data formatting | bytes 9437184 | tf_op jit(solution)/shard_map/stack | solution.py:704
  503.7 4.6 all-to-all-start.5
  522.2 48.7 %collective-permute-done.36 = bf16[2,64,1536]{2,1,0:T(8,128)(2,1)S(1)} collective-permute-done((bf16[2,64,1536]{2,1,0:T(8,128)(2,1)S(1)}, bf16[2,64,1536]{2,1,0:T(8,128)(2,1)S(1)}, u32[]{:S(2)}, u32[]{:S(2)}) %collective-permute-start.36) | collective-permute-done | bytes 393248 | tf_op jit(solution)/shard_map/ppermute | solution.py:345
  571.8 7.5 collective-permute-done.21
  582.2 4.5 convolution_convert_fusion.11
  591.2 38.3 %collective-permute-done.56 = bf16[2,64,1536]{2,1,0:T(8,128)(2,1)} collective-permute-done((bf16[2,64,1536]{2,1,0:T(8,128)(2,1)S(1)}, bf16[2,64,1536]{2,1,0:T(8,128)(2,1)}, u32[]{:S(2)}, u32[]{:S(2)}) %collective-permute-start.56) | collective-permute-done | bytes 393248 | tf_op jit(solution)/shard_map/ppermute | solution.py:345
  637.3 13.8 collective-permute-done.57
  653.7 7.9 collective-permute-done.42
  662.7 8.1 collective-permute-done.30
  672.8 4.2 convolution_convert_fusion.10
  683.9 5.5 collective-permute-done.43
  691.3 9.8 collective-permute-done.44
  710.8 31.5 %attend_back.1 = (bf16[16,64,576]{2,1,0:T(8,128)(2,1)}, bf16[16,80,576]{2,1,0:T(8,128)(2,1)}) custom-call(bf16[16,64,576]{2,1,0:T(8,128)(2,1)} %bitcast.247, bf16[16,80,576]{2,1,0:T(8,128)(2,1)} %bitcast.245, bf16[16,144,192]{2,1,0:T(8,128)(2,1)} %constant_dynamic-update-slice_fusion.refs_2_), custom_call_target="tpu_custom_call" | custom-call | flops 637009920 | bytes 6635520 | tf_op jit(solution)/shard_map/attend_back/pallas_call | solution.py:453
  745.6 4.5 convolution_convert_fusion.3
  758.1 5.5 bitcast_convert_fusion
  763.6 4.7 bitcast_convert_fusion.1
  774.6 11.8 copy.205
  786.4 11.8 copy.204
  809.5 7.6 collective-permute-done.52
  818.7 19.1 %collective-permute-done.54 = bf16[4,80,1536]{2,1,0:T(8,128)(2,1)S(1)} collective-permute-done((bf16[4,80,1536]{2,1,0:T(8,128)(2,1)S(1)}, bf16[4,80,1536]{2,1,0:T(8,128)(2,1)S(1)}, u32[]{:S(2)}, u32[]{:S(2)}) %collective-permute-start.54) | collective-permute-done | bytes 983072 | tf_op jit(solution)/shard_map/ppermute | solution.py:345
  840.9 10.0 collective-permute-done.55
  852.5 14.5 all-gather.1
  868.1 13.4 pad_maximum_fusion
  881.5 4.6 all-to-all-start.4
  886.2 6.3 fusion.27
  898.8 7.2 copy.209
  906.0 7.7 all_to_all.77
  916.5 31.3 %all-to-all-done.4 = bf16[2,1536,3,1,192]{4,0,3,2,1:T(2,128)(2,1)} async-done(((bf16[2,1536,3,1,192]{4,0,3,2,1:T(2,128)(2,1)}), bf16[2,1536,3,1,192]{4,0,3,2,1:T(2,128)(2,1)}, u32[]{:S(2)}, u32[]{:S(2)}) %all-to-all-start.4) | async-done | bytes 3538976 | tf_op jit(solution)/shard_map/all_to_all | solution.py:708
  947.8 7.2 copy.206
  955.0 8.4 reshape.380
  989.5 7.1 fusion.47
  1001.3 7.4 convolution_bitcast_fusion
  1010.3 435.5 %all-reduce.5.cloned.1.call-done = (bf16[2,192,4608]{2,1,0:T(8,128)(2,1)}, bf16[2,192,1536]{2,1,0:T(8,128)(2,1)}, bf16[2,192,6144]{2,1,0:T(8,128)(2,1)}, bf16[2,768,1536]{2,1,0:T(8,128)(2,1)}) async-done(((bf16[2,192,4608]{2,1,0:T(8,128)(2,1)}, bf16[2,192,1536]{2,1,0:T(8,128)(2,1)}, bf16[2,192,6144]{2,1,0:T(8,128)(2,1)}, bf16[2,768,1536]{2,1,0:T(8,128)(2,1)}), (bf16[2,192,4608]{2,1,0:T(8,128)(2,1)}, ...) | async-done | bytes 14155792 | tf_op jit(solution)/shard_map/psum | solution.py:710
  1448.9 4.5 convert_element_type.528
  1453.3 4.9 convert_element_type.536
  1458.3 5.1 convert_element_type.539
  (703 shorter events, 309.9 us)
Async XLA Ops:
  31.7 63.8 %all-to-all-start = ((f32[16,2,9216]{2,1,0:T(2,128)}), f32[16,2,9216]{2,1,0:T(2,128)S(1)}, u32[]{:S(2)}, u32[]{:S(2)}) async-start(f32[16,2,9216]{2,1,0:T(2,128)} %copy.179), calls=%async_computation | async-start | bytes 2359296 | tf_op jit(solution)/shard_map/all_to_all | solution.py:538
  37.3 53.2 %collective-permute-start.22 = (bf16[192,1536]{1,0:T(8,128)(2,1)S(1)}, bf16[192,1536]{1,0:T(8,128)(2,1)}, u32[]{:S(2)}, u32[]{:S(2)}) collective-permute-start(bf16[192,1536]{1,0:T(8,128)(2,1)S(1)} %get-tuple-element.191), channel_id=1, source_target_pairs={{0,16},{4,20},{8,24},{12,28},{16,0},{20,4},{24,8},{28,12},{1,17},{... | collective-permute-start | bytes 1769480 | tf_op jit(solution)/shard_map/ppermute | solution.py:345
  39.3 53.9 %collective-permute-start.13 = (bf16[192,1536]{1,0:T(8,128)(2,1)S(1)}, bf16[192,1536]{1,0:T(8,128)(2,1)}, u32[]{:S(2)}, u32[]{:S(2)}) collective-permute-start(bf16[192,1536]{1,0:T(8,128)(2,1)S(1)} %get-tuple-element.192), channel_id=1, source_target_pairs={{0,8},{4,12},{8,0},{12,4},{16,24},{20,28},{24,16},{28,20},{1,9},{5... | collective-permute-start | bytes 1769480 | tf_op jit(solution)/shard_map/ppermute | solution.py:345
  92.6 126.8 %collective-permute-start.23 = (bf16[384,1536]{1,0:T(8,128)(2,1)}, bf16[384,1536]{1,0:T(8,128)(2,1)}, u32[]{:S(2)}, u32[]{:S(2)}) collective-permute-start(bf16[384,1536]{1,0:T(8,128)(2,1)} %pad_maximum_fusion.22), channel_id=1, source_target_pairs={{0,8},{4,12},{8,0},{12,4},{16,24},{20,28},{24,16},{28,20},{1,9},{5... | collective-permute-start | bytes 3538952 | tf_op jit(solution)/shard_map/ppermute | solution.py:345
  95.3 129.1 %collective-permute-start.14 = (bf16[384,1536]{1,0:T(8,128)(2,1)}, bf16[384,1536]{1,0:T(8,128)(2,1)}, u32[]{:S(2)}, u32[]{:S(2)}) collective-permute-start(bf16[384,1536]{1,0:T(8,128)(2,1)} %pad_maximum_fusion.21), channel_id=1, source_target_pairs={{0,16},{4,20},{8,24},{12,28},{16,0},{20,4},{24,8},{28,12},{1,17},{... | collective-permute-start | bytes 3538952 | tf_op jit(solution)/shard_map/ppermute | solution.py:345
  95.5 145.4 %all-to-all-start.1 = ((bf16[2,192,3,8,192]{1,4,2,0,3:T(8,128)(2,1)}), bf16[2,192,3,8,192]{1,4,2,0,3:T(8,128)(2,1)}, u32[]{:S(2)}, u32[]{:S(2)}) async-start(bf16[2,192,3,8,192]{1,4,2,0,3:T(8,128)(2,1)} %copy.180), calls=%async_computation.1 | async-start | bytes 9437184 | tf_op jit(solution)/shard_map/all_to_all | solution.py:548
  101.2 90.7 %collective-permute-start.31 = (bf16[2,64,1536]{2,1,0:T(8,128)(2,1)S(1)}, bf16[2,64,1536]{2,1,0:T(8,128)(2,1)S(1)}, u32[]{:S(2)}, u32[]{:S(2)}) collective-permute-start(bf16[2,64,1536]{2,1,0:T(8,128)(2,1)S(1)} %multiply_convert_fusion.5), channel_id=1, source_target_pairs={{0,8},{4,12},{8,0},{12,4},{16,24},{20,28},{24,16},{28,20},{1,9},{5... | collective-permute-start | bytes 1179656 | tf_op jit(solution)/shard_map/ppermute | solution.py:345
  104.2 83.6 %collective-permute-start = (bf16[2,64,1536]{2,1,0:T(8,128)(2,1)S(1)}, bf16[2,64,1536]{2,1,0:T(8,128)(2,1)S(1)}, u32[]{:S(2)}, u32[]{:S(2)}) collective-permute-start(bf16[2,64,1536]{2,1,0:T(8,128)(2,1)S(1)} %fusion.63), channel_id=1, source_target_pairs={{0,8},{4,12},{8,0},{12,4},{16,24},{20,28},{24,16},{28,20},{1,9},{5... | collective-permute-start | bytes 1179656 | tf_op jit(solution)/shard_map/ppermute | solution.py:345
  104.8 85.5 %collective-permute-start.3 = (bf16[2,80,1536]{2,1,0:T(8,128)(2,1)S(1)}, bf16[2,80,1536]{2,1,0:T(8,128)(2,1)S(1)}, u32[]{:S(2)}, u32[]{:S(2)}) collective-permute-start(bf16[2,80,1536]{2,1,0:T(8,128)(2,1)S(1)} %fusion.51), channel_id=1, source_target_pairs={{0,16},{4,20},{8,24},{12,28},{16,0},{20,4},{24,8},{28,12},{1,17},{... | collective-permute-start | bytes 1474568 | tf_op jit(solution)/shard_map/ppermute | solution.py:345
  187.9 29.4 %collective-permute-start.1 = (bf16[4,64,1536]{2,1,0:T(8,128)(2,1)S(1)}, bf16[4,64,1536]{2,1,0:T(8,128)(2,1)S(1)}, u32[]{:S(2)}, u32[]{:S(2)}) collective-permute-start(bf16[4,64,1536]{2,1,0:T(8,128)(2,1)S(1)} %pad_maximum_fusion.28), channel_id=1, source_target_pairs={{0,16},{4,20},{8,24},{12,28},{16,0},{20,4},{24,8},{28,12},{1,17},{... | collective-permute-start | bytes 2359304 | tf_op jit(solution)/shard_map/ppermute | solution.py:345
  190.3 26.3 %collective-permute-start.37 = (bf16[2,80,1536]{2,1,0:T(8,128)(2,1)S(1)}, bf16[2,80,1536]{2,1,0:T(8,128)(2,1)S(1)}, u32[]{:S(2)}, u32[]{:S(2)}) collective-permute-start(bf16[2,80,1536]{2,1,0:T(8,128)(2,1)S(1)} %multiply_convert_fusion.3), channel_id=1, source_target_pairs={{0,16},{4,20},{8,24},{12,28},{16,0},{20,4},{24,8},{28,12},{1,17},{... | collective-permute-start | bytes 1474568 | tf_op jit(solution)/shard_map/ppermute | solution.py:345
  191.9 30.5 %collective-permute-start.4 = (bf16[4,80,1536]{2,1,0:T(8,128)(2,1)S(1)}, bf16[4,80,1536]{2,1,0:T(8,128)(2,1)S(1)}, u32[]{:S(2)}, u32[]{:S(2)}) collective-permute-start(bf16[4,80,1536]{2,1,0:T(8,128)(2,1)S(1)} %pad_maximum_fusion.24), channel_id=1, source_target_pairs={{0,8},{4,12},{8,0},{12,4},{16,24},{20,28},{24,16},{28,20},{1,9},{5... | collective-permute-start | bytes 2949128 | tf_op jit(solution)/shard_map/ppermute | solution.py:345
  216.6 17.2 %collective-permute-start.32 = (bf16[4,64,1536]{2,1,0:T(8,128)(2,1)S(1)}, bf16[4,64,1536]{2,1,0:T(8,128)(2,1)S(1)}, u32[]{:S(2)}, u32[]{:S(2)}) collective-permute-start(bf16[4,64,1536]{2,1,0:T(8,128)(2,1)S(1)} %pad_maximum_fusion.30), channel_id=1, source_target_pairs={{0,16},{4,20},{8,24},{12,28},{16,0},{20,4},{24,8},{28,12},{1,17},{... | collective-permute-start | bytes 2359304 | tf_op jit(solution)/shard_map/ppermute | solution.py:345
  217.3 21.2 %collective-permute-start.38 = (bf16[4,80,1536]{2,1,0:T(8,128)(2,1)S(1)}, bf16[4,80,1536]{2,1,0:T(8,128)(2,1)S(1)}, u32[]{:S(2)}, u32[]{:S(2)}) collective-permute-start(bf16[4,80,1536]{2,1,0:T(8,128)(2,1)S(1)} %pad_maximum_fusion.26), channel_id=1, source_target_pairs={{0,8},{4,12},{8,0},{12,4},{16,24},{20,28},{24,16},{28,20},{1,9},{5... | collective-permute-start | bytes 2949128 | tf_op jit(solution)/shard_map/ppermute | solution.py:345
  219.4 46.9 %collective-permute-start.2 = (bf16[8,64,1536]{2,1,0:T(8,128)(2,1)}, bf16[8,64,1536]{2,1,0:T(8,128)(2,1)}, u32[]{:S(2)}, u32[]{:S(2)}) collective-permute-start(bf16[8,64,1536]{2,1,0:T(8,128)(2,1)} %pad_maximum_fusion.17), channel_id=1, source_target_pairs={{0,4},{4,0},{8,12},{12,8},{16,20},{20,16},{24,28},{28,24},{1,5},{5... | collective-permute-start | bytes 4718600 | tf_op jit(solution)/shard_map/ppermute | solution.py:345
  222.4 119.1 %collective-permute-start.24 = (bf16[768,1536]{1,0:T(8,128)(2,1)}, bf16[768,1536]{1,0:T(8,128)(2,1)}, u32[]{:S(2)}, u32[]{:S(2)}) collective-permute-start(bf16[768,1536]{1,0:T(8,128)(2,1)} %pad_maximum_fusion.12), channel_id=1, source_target_pairs={{0,4},{4,0},{8,12},{12,8},{16,20},{20,16},{24,28},{28,24},{1,5},{5... | collective-permute-start | bytes 7077896 | tf_op jit(solution)/shard_map/ppermute | solution.py:345
  224.4 49.4 %collective-permute-start.5 = (bf16[8,80,1536]{2,1,0:T(8,128)(2,1)}, bf16[8,80,1536]{2,1,0:T(8,128)(2,1)}, u32[]{:S(2)}, u32[]{:S(2)}) collective-permute-start(bf16[8,80,1536]{2,1,0:T(8,128)(2,1)} %pad_maximum_fusion.13), channel_id=1, source_target_pairs={{0,4},{4,0},{8,12},{12,8},{16,20},{20,16},{24,28},{28,24},{1,5},{5... | collective-permute-start | bytes 5898248 | tf_op jit(solution)/shard_map/ppermute | solution.py:345
  233.8 100.2 %collective-permute-start.15 = (bf16[768,1536]{1,0:T(8,128)(2,1)}, bf16[768,1536]{1,0:T(8,128)(2,1)}, u32[]{:S(2)}, u32[]{:S(2)}) collective-permute-start(bf16[768,1536]{1,0:T(8,128)(2,1)} %pad_maximum_fusion.11), channel_id=1, source_target_pairs={{0,4},{4,0},{8,12},{12,8},{16,20},{20,16},{24,28},{28,24},{1,5},{5... | collective-permute-start | bytes 7077896 | tf_op jit(solution)/shard_map/ppermute | solution.py:345
  240.9 147.8 %all-to-all-start.2 = ((bf16[2,192,6144]{1,0,2:T(2,128)(2,1)}), bf16[2,192,6144]{1,0,2:T(2,128)(2,1)}, u32[]{:S(2)}, u32[]{:S(2)}) async-start(bf16[2,192,6144]{1,0,2:T(2,128)(2,1)} %copy.186), calls=%async_computation.2 | async-start | bytes 12582912 | tf_op jit(solution)/shard_map/all_to_all | solution.py:550
  301.8 18.1 %collective-permute-start.12 = (bf16[2,144,192]{2,1,0:T(8,128)(2,1)S(1)}, bf16[2,144,192]{2,1,0:T(8,128)(2,1)S(1)}, u32[]{:S(2)}, u32[]{:S(2)}) collective-permute-start(bf16[2,144,192]{2,1,0:T(8,128)(2,1)S(1)} %get-tuple-element.193), channel_id=1, source_target_pairs={{0,28},{4,24},{8,20},{12,16},{16,12},{20,8},{24,4},{28,0},{1,29},{... | collective-permute-start | bytes 331784 | tf_op jit(solution)/shard_map/ppermute | solution.py:345
  309.0 14.4 collective-permute-start.11
  309.5 14.2 collective-permute-start.10
  323.7 8.8 collective-permute-start.7
  331.1 53.5 %collective-permute-start.33 = (bf16[8,64,1536]{2,1,0:T(8,128)(2,1)}, bf16[8,64,1536]{2,1,0:T(8,128)(2,1)}, u32[]{:S(2)}, u32[]{:S(2)}) collective-permute-start(bf16[8,64,1536]{2,1,0:T(8,128)(2,1)} %pad_maximum_fusion.19), channel_id=1, source_target_pairs={{0,4},{4,0},{8,12},{12,8},{16,20},{20,16},{24,28},{28,24},{1,5},{5... | collective-permute-start | bytes 4718600 | tf_op jit(solution)/shard_map/ppermute | solution.py:345
  332.5 70.7 %collective-permute-start.39 = (bf16[8,80,1536]{2,1,0:T(8,128)(2,1)}, bf16[8,80,1536]{2,1,0:T(8,128)(2,1)}, u32[]{:S(2)}, u32[]{:S(2)}) collective-permute-start(bf16[8,80,1536]{2,1,0:T(8,128)(2,1)} %pad_maximum_fusion.15), channel_id=1, source_target_pairs={{0,4},{4,0},{8,12},{12,8},{16,20},{20,16},{24,28},{28,24},{1,5},{5... | collective-permute-start | bytes 5898248 | tf_op jit(solution)/shard_map/ppermute | solution.py:345
  338.6 11.1 collective-permute-start.16
  351.6 20.8 %collective-permute-start.17 = (bf16[4,64,1536]{2,1,0:T(8,128)(2,1)}, bf16[4,64,1536]{2,1,0:T(8,128)(2,1)}, u32[]{:S(2)}, u32[]{:S(2)}) collective-permute-start(bf16[4,64,1536]{2,1,0:T(8,128)(2,1)} %pad_maximum_fusion.29), channel_id=1, source_target_pairs={{0,16},{4,20},{8,24},{12,28},{16,0},{20,4},{24,8},{28,12},{1,17},{... | collective-permute-start | bytes 2359304 | tf_op jit(solution)/shard_map/ppermute | solution.py:345
  353.7 27.4 %collective-permute-start.25 = (bf16[2,80,1536]{2,1,0:T(8,128)(2,1)S(1)}, bf16[2,80,1536]{2,1,0:T(8,128)(2,1)}, u32[]{:S(2)}, u32[]{:S(2)}) collective-permute-start(bf16[2,80,1536]{2,1,0:T(8,128)(2,1)S(1)} %add_convert_fusion.7), channel_id=1, source_target_pairs={{0,16},{4,20},{8,24},{12,28},{16,0},{20,4},{24,8},{28,12},{1,17},{... | collective-permute-start | bytes 1474568 | tf_op jit(solution)/shard_map/ppermute | solution.py:345
  375.0 33.8 %collective-permute-start.18 = (bf16[8,64,1536]{2,1,0:T(8,128)(2,1)}, bf16[8,64,1536]{2,1,0:T(8,128)(2,1)}, u32[]{:S(2)}, u32[]{:S(2)}) collective-permute-start(bf16[8,64,1536]{2,1,0:T(8,128)(2,1)} %pad_maximum_fusion.18), channel_id=1, source_target_pairs={{0,4},{4,0},{8,12},{12,8},{16,20},{20,16},{24,28},{28,24},{1,5},{5... | collective-permute-start | bytes 4718600 | tf_op jit(solution)/shard_map/ppermute | solution.py:345
  383.1 23.9 %collective-permute-start.26 = (bf16[4,80,1536]{2,1,0:T(8,128)(2,1)}, bf16[4,80,1536]{2,1,0:T(8,128)(2,1)}, u32[]{:S(2)}, u32[]{:S(2)}) collective-permute-start(bf16[4,80,1536]{2,1,0:T(8,128)(2,1)} %pad_maximum_fusion.25), channel_id=1, source_target_pairs={{0,8},{4,12},{8,0},{12,4},{16,24},{20,28},{24,16},{28,20},{1,9},{5... | collective-permute-start | bytes 2949128 | tf_op jit(solution)/shard_map/ppermute | solution.py:345
  408.6 23.2 %collective-permute-start.27 = (bf16[8,80,1536]{2,1,0:T(8,128)(2,1)S(1)}, bf16[8,80,1536]{2,1,0:T(8,128)(2,1)S(1)}, u32[]{:S(2)}, u32[]{:S(2)}) collective-permute-start(bf16[8,80,1536]{2,1,0:T(8,128)(2,1)S(1)} %pad_maximum_fusion.14), channel_id=1, source_target_pairs={{0,4},{4,0},{8,12},{12,8},{16,20},{20,16},{24,28},{28,24},{1,5},{5... | collective-permute-start | bytes 5898248 | tf_op jit(solution)/shard_map/ppermute | solution.py:345
  423.9 38.9 %collective-permute-start.34 = (bf16[8,64,1536]{2,1,0:T(8,128)(2,1)}, bf16[8,64,1536]{2,1,0:T(8,128)(2,1)}, u32[]{:S(2)}, u32[]{:S(2)}) collective-permute-start(bf16[8,64,1536]{2,1,0:T(8,128)(2,1)} %bitcast.36), channel_id=1, source_target_pairs={{0,4},{4,0},{8,12},{12,8},{16,20},{20,16},{24,28},{28,24},{1,5},{5... | collective-permute-start | bytes 4718600 | tf_op jit(solution)/shard_map/ppermute | solution.py:345
  427.7 38.2 %collective-permute-start.19 = (bf16[8,64,1536]{2,1,0:T(8,128)(2,1)S(1)}, bf16[8,64,1536]{2,1,0:T(8,128)(2,1)S(1)}, u32[]{:S(2)}, u32[]{:S(2)}) collective-permute-start(bf16[8,64,1536]{2,1,0:T(8,128)(2,1)S(1)} %bitcast.278), channel_id=1, source_target_pairs={{0,4},{4,0},{8,12},{12,8},{16,20},{20,16},{24,28},{28,24},{1,5},{5... | collective-permute-start | bytes 4718600 | tf_op jit(solution)/shard_map/ppermute | solution.py:345
  458.7 54.9 %collective-permute-start.40 = (bf16[8,80,1536]{2,1,0:T(8,128)(2,1)}, bf16[8,80,1536]{2,1,0:T(8,128)(2,1)}, u32[]{:S(2)}, u32[]{:S(2)}) collective-permute-start(bf16[8,80,1536]{2,1,0:T(8,128)(2,1)} %bitcast.39), channel_id=1, source_target_pairs={{0,4},{4,0},{8,12},{12,8},{16,20},{20,16},{24,28},{28,24},{1,5},{5... | collective-permute-start | bytes 5898248 | tf_op jit(solution)/shard_map/ppermute | solution.py:345
  458.7 60.1 %collective-permute-start.28 = (bf16[8,80,1536]{2,1,0:T(8,128)(2,1)}, bf16[8,80,1536]{2,1,0:T(8,128)(2,1)}, u32[]{:S(2)}, u32[]{:S(2)}) collective-permute-start(bf16[8,80,1536]{2,1,0:T(8,128)(2,1)} %bitcast.33), channel_id=1, source_target_pairs={{0,4},{4,0},{8,12},{12,8},{16,20},{20,16},{24,28},{28,24},{1,5},{5... | collective-permute-start | bytes 5898248 | tf_op jit(solution)/shard_map/ppermute | solution.py:345
  465.6 42.7 %collective-permute-start.35 = (bf16[4,64,1536]{2,1,0:T(8,128)(2,1)}, bf16[4,64,1536]{2,1,0:T(8,128)(2,1)}, u32[]{:S(2)}, u32[]{:S(2)}) collective-permute-start(bf16[4,64,1536]{2,1,0:T(8,128)(2,1)} %slice.682), channel_id=1, source_target_pairs={{0,16},{4,20},{8,24},{12,28},{16,0},{20,4},{24,8},{28,12},{1,17},{... | collective-permute-start | bytes 2359304 | tf_op jit(solution)/shard_map/ppermute | solution.py:345
  467.8 43.9 %collective-permute-start.20 = (bf16[4,64,1536]{2,1,0:T(8,128)(2,1)}, bf16[4,64,1536]{2,1,0:T(8,128)(2,1)}, u32[]{:S(2)}, u32[]{:S(2)}) collective-permute-start(bf16[4,64,1536]{2,1,0:T(8,128)(2,1)} %slice.648), channel_id=1, source_target_pairs={{0,16},{4,20},{8,24},{12,28},{16,0},{20,4},{24,8},{28,12},{1,17},{... | collective-permute-start | bytes 2359304 | tf_op jit(solution)/shard_map/ppermute | solution.py:345
  503.7 377.8 %all-to-all-start.5 = ((bf16[2,1536,768]{2,0,1:T(2,128)(2,1)}), bf16[2,1536,768]{2,0,1:T(2,128)(2,1)}, u32[]{:S(2)}, u32[]{:S(2)}) async-start(bf16[2,1536,768]{2,0,1:T(2,128)(2,1)} %copy.208), calls=%async_computation.5 | async-start | bytes 9437184 | tf_op jit(solution)/shard_map/all_to_all | solution.py:703
  508.3 469.2 %all-gather.7.cloned.1.call-start = ((), (), s32[]{:S(2)}) async-start(), calls=%async_computation.6 | async-start | bytes 2930688 | tf_op jit(solution)/shard_map/all_gather | solution.py:733
  509.9 61.0 %collective-permute-start.36 = (bf16[2,64,1536]{2,1,0:T(8,128)(2,1)S(1)}, bf16[2,64,1536]{2,1,0:T(8,128)(2,1)S(1)}, u32[]{:S(2)}, u32[]{:S(2)}) collective-permute-start(bf16[2,64,1536]{2,1,0:T(8,128)(2,1)S(1)} %slice.684), channel_id=1, source_target_pairs={{0,8},{4,12},{8,0},{12,4},{16,24},{20,28},{24,16},{28,20},{1,9},{5... | collective-permute-start | bytes 1179656 | tf_op jit(solution)/shard_map/ppermute | solution.py:345
  513.4 65.9 %collective-permute-start.21 = (bf16[2,64,1536]{2,1,0:T(8,128)(2,1)S(1)}, bf16[2,64,1536]{2,1,0:T(8,128)(2,1)S(1)}, u32[]{:S(2)}, u32[]{:S(2)}) collective-permute-start(bf16[2,64,1536]{2,1,0:T(8,128)(2,1)S(1)} %slice.650), channel_id=1, source_target_pairs={{0,8},{4,12},{8,0},{12,4},{16,24},{20,28},{24,16},{28,20},{1,9},{5... | collective-permute-start | bytes 1179656 | tf_op jit(solution)/shard_map/ppermute | solution.py:345
  517.0 115.2 %collective-permute-start.41 = (bf16[4,80,1536]{2,1,0:T(8,128)(2,1)}, bf16[4,80,1536]{2,1,0:T(8,128)(2,1)}, u32[]{:S(2)}, u32[]{:S(2)}) collective-permute-start(bf16[4,80,1536]{2,1,0:T(8,128)(2,1)} %slice.688), channel_id=1, source_target_pairs={{0,8},{4,12},{8,0},{12,4},{16,24},{20,28},{24,16},{28,20},{1,9},{5... | collective-permute-start | bytes 2949128 | tf_op jit(solution)/shard_map/ppermute | solution.py:345
  522.0 112.2 %collective-permute-start.29 = (bf16[4,80,1536]{2,1,0:T(8,128)(2,1)}, bf16[4,80,1536]{2,1,0:T(8,128)(2,1)}, u32[]{:S(2)}, u32[]{:S(2)}) collective-permute-start(bf16[4,80,1536]{2,1,0:T(8,128)(2,1)} %slice.673), channel_id=1, source_target_pairs={{0,8},{4,12},{8,0},{12,4},{16,24},{20,28},{24,16},{28,20},{1,9},{5... | collective-permute-start | bytes 2949128 | tf_op jit(solution)/shard_map/ppermute | solution.py:345
  582.0 47.5 %collective-permute-start.56 = (bf16[2,64,1536]{2,1,0:T(8,128)(2,1)S(1)}, bf16[2,64,1536]{2,1,0:T(8,128)(2,1)}, u32[]{:S(2)}, u32[]{:S(2)}) collective-permute-start(bf16[2,64,1536]{2,1,0:T(8,128)(2,1)S(1)} %multiply_convert_fusion.4), channel_id=1, source_target_pairs={{0,8},{4,12},{8,0},{12,4},{16,24},{20,28},{24,16},{28,20},{1,9},{5... | collective-permute-start | bytes 1179656 | tf_op jit(solution)/shard_map/ppermute | solution.py:345
  630.6 20.5 %collective-permute-start.57 = (bf16[4,64,1536]{2,1,0:T(8,128)(2,1)S(1)}, bf16[4,64,1536]{2,1,0:T(8,128)(2,1)S(1)}, u32[]{:S(2)}, u32[]{:S(2)}) collective-permute-start(bf16[4,64,1536]{2,1,0:T(8,128)(2,1)S(1)} %pad_maximum_fusion.31), channel_id=1, source_target_pairs={{0,16},{4,20},{8,24},{12,28},{16,0},{20,4},{24,8},{28,12},{1,17},{... | collective-permute-start | bytes 2359304 | tf_op jit(solution)/shard_map/ppermute | solution.py:345
  633.6 28.0 %collective-permute-start.42 = (bf16[2,80,1536]{2,1,0:T(8,128)(2,1)S(1)}, bf16[2,80,1536]{2,1,0:T(8,128)(2,1)S(1)}, u32[]{:S(2)}, u32[]{:S(2)}) collective-permute-start(bf16[2,80,1536]{2,1,0:T(8,128)(2,1)S(1)} %slice.690), channel_id=1, source_target_pairs={{0,16},{4,20},{8,24},{12,28},{16,0},{20,4},{24,8},{28,12},{1,17},{... | collective-permute-start | bytes 1474568 | tf_op jit(solution)/shard_map/ppermute | solution.py:345
  635.8 35.0 %collective-permute-start.30 = (bf16[2,80,1536]{2,1,0:T(8,128)(2,1)S(1)}, bf16[2,80,1536]{2,1,0:T(8,128)(2,1)S(1)}, u32[]{:S(2)}, u32[]{:S(2)}) collective-permute-start(bf16[2,80,1536]{2,1,0:T(8,128)(2,1)S(1)} %slice.675), channel_id=1, source_target_pairs={{0,16},{4,20},{8,24},{12,28},{16,0},{20,4},{24,8},{28,12},{1,17},{... | collective-permute-start | bytes 1474568 | tf_op jit(solution)/shard_map/ppermute | solution.py:345
  653.7 144.5 %collective-permute-start.58 = (bf16[8,64,1536]{2,1,0:T(8,128)(2,1)}, bf16[8,64,1536]{2,1,0:T(8,128)(2,1)}, u32[]{:S(2)}, u32[]{:S(2)}) collective-permute-start(bf16[8,64,1536]{2,1,0:T(8,128)(2,1)} %pad_maximum_fusion.20), channel_id=1, source_target_pairs={{0,4},{4,0},{8,12},{12,8},{16,20},{20,16},{24,28},{28,24},{1,5},{5... | collective-permute-start | bytes 4718600 | tf_op jit(solution)/shard_map/ppermute | solution.py:345
  679.7 88.6 %collective-permute-start.59 = (bf16[2,80,1536]{2,1,0:T(8,128)(2,1)S(1)}, bf16[2,80,1536]{2,1,0:T(8,128)(2,1)S(1)}, u32[]{:S(2)}, u32[]{:S(2)}) collective-permute-start(bf16[2,80,1536]{2,1,0:T(8,128)(2,1)S(1)} %multiply_convert_fusion.2), channel_id=1, source_target_pairs={{0,16},{4,20},{8,24},{12,28},{16,0},{20,4},{24,8},{28,12},{1,17},{... | collective-permute-start | bytes 1474568 | tf_op jit(solution)/shard_map/ppermute | solution.py:345
  681.6 28.5 %collective-permute-start.49 = (bf16[2,144,192]{2,1,0:T(8,128)(2,1)S(1)}, bf16[2,144,192]{2,1,0:T(8,128)(2,1)S(1)}, u32[]{:S(2)}, u32[]{:S(2)}) collective-permute-start(bf16[2,144,192]{2,1,0:T(8,128)(2,1)S(1)} %get-tuple-element.184), channel_id=1, source_target_pairs={{0,28},{4,24},{8,20},{12,16},{16,12},{20,8},{24,4},{28,0},{1,29},{... | collective-permute-start | bytes 331784 | tf_op jit(solution)/shard_map/ppermute | solution.py:345
  681.7 7.7 collective-permute-start.43
  682.3 18.8 %collective-permute-start.44 = (bf16[2,144,192]{2,1,0:T(8,128)(2,1)S(1)}, bf16[2,144,192]{2,1,0:T(8,128)(2,1)S(1)}, u32[]{:S(2)}, u32[]{:S(2)}) collective-permute-start(bf16[2,144,192]{2,1,0:T(8,128)(2,1)S(1)} %get-tuple-element.186), channel_id=1, source_target_pairs={{0,16},{4,20},{8,24},{12,28},{16,0},{20,4},{24,8},{28,12},{1,17},{... | collective-permute-start | bytes 331784 | tf_op jit(solution)/shard_map/ppermute | solution.py:345
  689.4 12.4 collective-permute-start.45
  750.3 20.2 %collective-permute-start.50 = (bf16[8,64,1536]{2,1,0:T(8,128)(2,1)S(1)}, bf16[8,64,1536]{2,1,0:T(8,128)(2,1)S(1)}, u32[]{:S(2)}, u32[]{:S(2)}) collective-permute-start(bf16[8,64,1536]{2,1,0:T(8,128)(2,1)S(1)} %bitcast.279), channel_id=1, source_target_pairs={{0,4},{4,0},{8,12},{12,8},{16,20},{20,16},{24,28},{28,24},{1,5},{5... | collective-permute-start | bytes 4718600 | tf_op jit(solution)/shard_map/ppermute | solution.py:345
  757.9 47.8 %collective-permute-start.53 = (bf16[8,80,1536]{2,1,0:T(8,128)(2,1)}, bf16[8,80,1536]{2,1,0:T(8,128)(2,1)}, u32[]{:S(2)}, u32[]{:S(2)}) collective-permute-start(bf16[8,80,1536]{2,1,0:T(8,128)(2,1)} %bitcast.53), channel_id=1, source_target_pairs={{0,4},{4,0},{8,12},{12,8},{16,20},{20,16},{24,28},{28,24},{1,5},{5... | collective-permute-start | bytes 5898248 | tf_op jit(solution)/shard_map/ppermute | solution.py:345
  769.4 32.6 %collective-permute-start.60 = (bf16[4,80,1536]{2,1,0:T(8,128)(2,1)}, bf16[4,80,1536]{2,1,0:T(8,128)(2,1)}, u32[]{:S(2)}, u32[]{:S(2)}) collective-permute-start(bf16[4,80,1536]{2,1,0:T(8,128)(2,1)} %pad_maximum_fusion.27), channel_id=1, source_target_pairs={{0,8},{4,12},{8,0},{12,4},{16,24},{20,28},{24,16},{28,20},{1,9},{5... | collective-permute-start | bytes 2949128 | tf_op jit(solution)/shard_map/ppermute | solution.py:345
  773.1 30.6 %collective-permute-start.51 = (bf16[4,64,1536]{2,1,0:T(8,128)(2,1)}, bf16[4,64,1536]{2,1,0:T(8,128)(2,1)}, u32[]{:S(2)}, u32[]{:S(2)}) collective-permute-start(bf16[4,64,1536]{2,1,0:T(8,128)(2,1)} %slice.715), channel_id=1, source_target_pairs={{0,16},{4,20},{8,24},{12,28},{16,0},{20,4},{24,8},{28,12},{1,17},{... | collective-permute-start | bytes 2359304 | tf_op jit(solution)/shard_map/ppermute | solution.py:345
  803.6 35.1 %collective-permute-start.61 = (bf16[8,80,1536]{2,1,0:T(8,128)(2,1)S(1)}, bf16[8,80,1536]{2,1,0:T(8,128)(2,1)S(1)}, u32[]{:S(2)}, u32[]{:S(2)}) collective-permute-start(bf16[8,80,1536]{2,1,0:T(8,128)(2,1)S(1)} %pad_maximum_fusion.16), channel_id=1, source_target_pairs={{0,4},{4,0},{8,12},{12,8},{16,20},{20,16},{24,28},{28,24},{1,5},{5... | collective-permute-start | bytes 5898248 | tf_op jit(solution)/shard_map/ppermute | solution.py:345
  805.1 12.0 collective-permute-start.52
  808.0 29.7 %collective-permute-start.54 = (bf16[4,80,1536]{2,1,0:T(8,128)(2,1)S(1)}, bf16[4,80,1536]{2,1,0:T(8,128)(2,1)S(1)}, u32[]{:S(2)}, u32[]{:S(2)}) collective-permute-start(bf16[4,80,1536]{2,1,0:T(8,128)(2,1)S(1)} %slice.721), channel_id=1, source_target_pairs={{0,8},{4,12},{8,0},{12,4},{16,24},{20,28},{24,16},{28,20},{1,9},{5... | collective-permute-start | bytes 2949128 | tf_op jit(solution)/shard_map/ppermute | solution.py:345
  838.0 12.9 collective-permute-start.55
  881.5 66.3 %all-to-all-start.4 = ((bf16[2,1536,3,1,192]{4,0,3,2,1:T(2,128)(2,1)}), bf16[2,1536,3,1,192]{4,0,3,2,1:T(2,128)(2,1)}, u32[]{:S(2)}, u32[]{:S(2)}) async-start(bf16[2,1536,3,1,192]{4,0,3,2,1:T(2,128)(2,1)} %pad_maximum_fusion), calls=%async_computation.4 | async-start | bytes 9437184 | tf_op jit(solution)/shard_map/all_to_all | solution.py:708
  886.1 559.6 %all-reduce.5.cloned.1.call-start = ((), (), s32[]{:S(2)}) async-start(), calls=%async_computation.7 | async-start | bytes 28311552 | tf_op jit(solution)/shard_map/psum | solution.py:710
  997.2 12.4 all-to-all-start.3
  (171 other events, 3165.2 us)
Sparse Core Ops, SparseCore 0:
  868.2 36.5 all-gather.6
Sparse Core Ops, SparseCore 1:
  968.0 477.7 all-reduce.4

commit v2 on v0

--- a/solution.py
+++ b/solution.py
@@ -1,6 +1,8 @@
 import jax
 import jax.numpy as jnp
 from jax import lax
+from jax.experimental import pallas as pl
+from jax.experimental.pallas import tpu as pltpu
 from jax.sharding import PartitionSpec as P
 
 HEADS = 24
@@ -34,7 +36,7 @@
     return jax.nn.gelu(values, approximate=True)
 
 
-def body(
+def gathered_body(
     image,
     text,
     condition,
@@ -325,6 +327,900 @@
     )
 
 
+GROUP = 8
+REPLICAS = 4
+SPAN = 80
+STEPS = 4
+ORDER_ONE = (2, 4, 1)
+ORDER_TWO = (4, 2, 1)
+
+
+def distances(order):
+    found = [0]
+    for step in order:
+        found = found + [item ^ step for item in found]
+    return found
+
+
+def swap(array, step):
+    return lax.ppermute(array, "shard", [(item, item ^ step) for item in range(GROUP)])
+
+
+def collect(array, order):
+    for step in order:
+        array = grow(array, step)
+    return array
+
+
+def grow(array, step):
+    return jnp.concatenate([array, swap(array, step)], axis=0)
+
+
+def scatter_halves(array, order):
+    for step in reversed(order):
+        half = array.shape[0] // 2
+        other = swap(array[half:], step)
+        if step == order[0]:
+            return array[:half], other
+        array = (array[:half].astype(WIDE) + other.astype(WIDE)).astype(LOWER)
+
+
+def scatter_sum(array, order):
+    own, other = scatter_halves(array, order)
+    return own.astype(WIDE) + other.astype(WIDE)
+
+
+def spread(array):
+    return lax.all_to_all(array, "shard", split_axis=0, concat_axis=0, tiled=True)
+
+
+def pick(array, indices):
+    return jnp.concatenate(
+        [lax.dynamic_slice_in_dim(array, item, 1, axis=0) for item in indices], axis=0
+    )
+
+
+def around(array):
+    found = [array]
+    for step in range(1, REPLICAS):
+        pairs = [(item, (item + step) % REPLICAS) for item in range(REPLICAS)]
+        found.append(lax.ppermute(array, "rep", pairs))
+    place = lax.axis_index("rep")
+    return pick(jnp.stack(found), [(place - item) % REPLICAS for item in range(REPLICAS)])
+
+
+def after(array, *others):
+    return lax.optimization_barrier((array, *others))[0]
+
+
+HOPS = ([(0, 1), (3, 2)], [(1, 2), (2, 1)], [(1, 0), (2, 3)])
+
+
+def together(*groups):
+    items = [item for group in groups for item in group]
+    items = list(lax.optimization_barrier(tuple(items)))
+    found = []
+    for group in groups:
+        found.append(items[: len(group)])
+        items = items[len(group) :]
+    return found
+
+
+class ReplicaSum:
+    def __init__(self):
+        self.entries = []
+
+    def add(self, array):
+        self.entries.append([array, None, 0])
+        return self.entries[-1]
+
+    def step(self, *groups):
+        moving = [entry for entry in self.entries if entry[2] < 3]
+        for entry in moving:
+            entry[1] = lax.ppermute(entry[0], "rep", HOPS[entry[2]])
+        pairs = [item for entry in moving for item in entry[:2]]
+        pairs, *groups = together(pairs, *groups)
+        for at, entry in enumerate(moving):
+            entry[0], entry[1] = pairs[2 * at : 2 * at + 2]
+            if entry[2] < 2:
+                entry[0] = (entry[0].astype(WIDE) + entry[1].astype(WIDE)).astype(LOWER)
+            entry[2] += 1
+        return groups
+
+
+def cost(flops, moved, transcendentals=0):
+    return pl.CostEstimate(flops=flops, bytes_accessed=moved, transcendentals=transcendentals)
+
+
+def pack(weight, place, count, pieces, streams):
+    _, rows, columns = weight.shape
+    rows = rows // count
+    step = rows // (STEPS // count)
+    width = columns // pieces
+    share = width // GROUP
+    low = streams[0]
+
+    def kernel(place_ref, source_ref, out_ref):
+        source = source_ref[0].astype(LOWER)
+        for item in range(GROUP):
+            cut = [
+                source[:, piece * width + item * share : piece * width + (item + 1) * share]
+                for piece in range(pieces)
+            ]
+            out_ref[item, 0] = cut[0] if pieces == 1 else jnp.concatenate(cut, axis=1)
+
+    return pl.pallas_call(
+        kernel,
+        out_shape=jax.ShapeDtypeStruct((GROUP, len(streams), rows, pieces * share), LOWER),
+        grid_spec=pltpu.PrefetchScalarGridSpec(
+            num_scalar_prefetch=1,
+            grid=(len(streams), rows // step),
+            in_specs=[
+                pl.BlockSpec(
+                    (1, step, columns),
+                    lambda s, i, at: (s + low, i + at[0] * (rows // step), 0),
+                )
+            ],
+            out_specs=pl.BlockSpec(
+                (GROUP, 1, step, pieces * share), lambda s, i, at: (0, s, i, 0)
+            ),
+        ),
+        cost_estimate=cost(0, len(streams) * rows * columns * 6),
+        name="pack",
+    )(place, weight)
+
+
+def arrange(blocks, place):
+    count, _, rows, columns = blocks[0].shape
+
+    def kernel(place_ref, *refs):
+        for step in range(REPLICAS):
+            at = lax.rem(place_ref[0] - step + REPLICAS, REPLICAS)
+            for which in range(2):
+                for item in range(group):
+                    refs[REPLICAS + which][item, at] = refs[step][item, which]
+
+    group = count // 2
+    block = pl.BlockSpec((group, 2, rows, columns), lambda item, at: (item, 0, 0, 0))
+    out = pl.BlockSpec((group, REPLICAS, rows, columns), lambda item, at: (item, 0, 0, 0))
+    shape = jax.ShapeDtypeStruct((count, REPLICAS, rows, columns), LOWER)
+    pair = pl.pallas_call(
+        kernel,
+        out_shape=(shape, shape),
+        grid_spec=pltpu.PrefetchScalarGridSpec(
+            num_scalar_prefetch=1,
+            grid=(count // group,),
+            in_specs=[block] * REPLICAS,
+            out_specs=(out, out),
+        ),
+        cost_estimate=cost(0, 4 * REPLICAS * blocks[0].size),
+        name="arrange",
+    )(place, *blocks)
+    return [item.reshape(count * REPLICAS * rows, columns) for item in pair]
+
+
+def ring(array):
+    found = [array]
+    for _ in range(1, REPLICAS):
+        pairs = [(item, (item + 1) % REPLICAS) for item in range(REPLICAS)]
+        found.append(lax.ppermute(found[-1], "rep", pairs))
+    return found
+
+
+def unpack(parts, edge, pieces):
+    count, rows, columns = parts[0][0][0].shape
+    each = len(parts[0][0])
+    chunks = len(parts[0])
+    total = rows * chunks
+    steps = max(1, min(STEPS, total // 48) // chunks)
+    step = rows // steps
+    share = columns // pieces
+    width = share * count
+
+    def kernel(edge_ref, *refs):
+        out_ref = refs[-1]
+
+        def write(sources):
+            for item in range(count):
+                source = sources[0][item].astype(WIDE)
+                if each == 2:
+                    source = jnp.where(edge_ref[0] > 0, sources[1][item].astype(WIDE), source)
+                for piece in range(pieces):
+                    at = piece * width + item * share
+                    out_ref[0, :, at : at + share] = source[:, piece * share : (piece + 1) * share]
+
+        for which in range(2):
+            for chunk in range(chunks):
+                low = (which * chunks + chunk) * each
+
+                @pl.when((pl.program_id(0) == which) & (pl.program_id(1) // steps == chunk))
+                def _(low=low):
+                    write(refs[low : low + each])
+
+    def spec(which, chunk):
+        def place(s, i, edge):
+            at = s * chunks * steps + i - (which * chunks + chunk) * steps
+            return (0, jnp.clip(at, 0, steps - 1), 0)
+
+        return pl.BlockSpec((count, step, columns), place)
+
+    inputs = [item for stream in parts for chunk in stream for item in chunk]
+    specs = [
+        spec(which, chunk) for which in range(2) for chunk in range(chunks) for _ in range(each)
+    ]
+    return pl.pallas_call(
+        kernel,
+        out_shape=jax.ShapeDtypeStruct((2, total, pieces * width), WIDE),
+        grid_spec=pltpu.PrefetchScalarGridSpec(
+            num_scalar_prefetch=1,
+            grid=(2, chunks * steps),
+            in_specs=specs,
+            out_specs=pl.BlockSpec((1, step, pieces * width), lambda s, i, edge: (s, i, 0)),
+        ),
+        cost_estimate=cost(0, total * columns * count * (8 + 4 * each)),
+        name="unpack",
+    )(edge, *inputs)
+
+
+def contract(left, right, dims):
+    return lax.dot_general(left, right, (dims, ((), ())), preferred_element_type=WIDE)
+
+
+def head_softmax(query, key, length):
+    scores = contract(query, key, ((1,), (1,))) * (query.shape[-1] ** (-0.5))
+    column = lax.broadcasted_iota(jnp.int32, scores.shape, 1)
+    scores = jnp.where(column < length, scores, -1e30)
+    raised = jnp.exp(scores - jnp.max(scores, axis=-1, keepdims=True))
+    return raised / jnp.sum(raised, axis=-1, keepdims=True)
+
+
+def attend_kernel(size, length, me_ref, image_ref, text_ref, out_ref):
+    for slot in range(image_ref.shape[1]):
+        joint = jnp.concatenate([image_ref[0, slot], text_ref[0, slot]], axis=0)
+        width = joint.shape[1] // 3
+        found = []
+        for at in range(0, width, size):
+            query = joint[:, at : at + size]
+            key = joint[:, width + at : width + at + size]
+            value = joint[:, 2 * width + at : 2 * width + at + size]
+            probs = head_softmax(query, key, length)
+            found.append(contract(probs.astype(LOWER), value, ((1,), (0,))).astype(LOWER))
+        out_ref[0, slot] = jnp.concatenate(found, axis=1)
+
+
+def attend_back_kernel(
+    size, length, me_ref, image_ref, text_ref, grad_ref, image_out_ref, text_out_ref
+):
+    for slot in range(image_ref.shape[1]):
+        joint = jnp.concatenate([image_ref[0, slot], text_ref[0, slot]], axis=0)
+        grad = grad_ref[0, slot]
+        width = joint.shape[1] // 3
+        factor = size ** (-0.5)
+        d_queries, d_keys, d_values = [], [], []
+        for at in range(0, width, size):
+            query = joint[:, at : at + size]
+            key = joint[:, width + at : width + at + size]
+            value = joint[:, 2 * width + at : 2 * width + at + size]
+            d_out = grad[:, at : at + size]
+            probs = head_softmax(query, key, length)
+            d_probs = contract(d_out, value, ((1,), (1,)))
+            center = jnp.sum(probs * d_probs, axis=-1, keepdims=True)
+            d_scores = (probs * (d_probs - center)).astype(LOWER)
+            d_queries.append((contract(d_scores, key, ((1,), (0,))) * factor).astype(LOWER))
+            d_keys.append((contract(d_scores, query, ((0,), (0,))) * factor).astype(LOWER))
+            d_values.append(contract(probs.astype(LOWER), d_out, ((0,), (0,))).astype(LOWER))
+        whole = jnp.concatenate(d_queries + d_keys + d_values, axis=1)
+        split_at = image_ref.shape[2]
+        image_out_ref[0, slot] = whole[:split_at]
+        text_out_ref[0, slot] = whole[split_at:]
+
+
+def image_place(index, me):
+    return (index, 0, 0, 0)
+
+
+def text_place(index, me):
+    low, high, top = index % 2, (index // 2) % 2, index // 4
+    return (high + 2 * low + 4 * top, 0, 0, 0)
+
+
+def joint_place(index, me):
+    low, high, top = index % 2, (index // 2) % 2, index // 4
+    return (me[0] ^ (2 * low + 4 * high + top), 0, 0, 0)
+
+
+def attend_forward(image, text, me, size, length):
+    devices, slots, rows, columns = image.shape
+    more = text.shape[2]
+    count = devices * slots
+    share = columns // 3
+    return pl.pallas_call(
+        lambda *refs: attend_kernel(size, length, *refs),
+        out_shape=jax.ShapeDtypeStruct((devices, slots, rows + more, share), LOWER),
+        grid_spec=pltpu.PrefetchScalarGridSpec(
+            num_scalar_prefetch=1,
+            grid=(devices,),
+            in_specs=[
+                pl.BlockSpec((1, slots, rows, columns), image_place),
+                pl.BlockSpec((1, slots, more, columns), text_place),
+            ],
+            out_specs=pl.BlockSpec((1, slots, rows + more, share), joint_place),
+        ),
+        cost_estimate=cost(
+            4 * count * (rows + more) ** 2 * share,
+            8 * count * (rows + more) * share,
+            count * (rows + more) ** 2 * 3,
+        ),
+        name="attend",
+    )(me, image, text)
+
+
+def attend_backward(image, text, grad, me, size, length):
+    devices, slots, rows, columns = image.shape
+    more = text.shape[2]
+    count = devices * slots
+    share = columns // 3
+    ours = pl.BlockSpec((1, slots, rows, columns), image_place)
+    theirs = pl.BlockSpec((1, slots, more, columns), text_place)
+    return pl.pallas_call(
+        lambda *refs: attend_back_kernel(size, length, *refs),
+        out_shape=(
+            jax.ShapeDtypeStruct(image.shape, LOWER),
+            jax.ShapeDtypeStruct(text.shape, LOWER),
+        ),
+        grid_spec=pltpu.PrefetchScalarGridSpec(
+            num_scalar_prefetch=1,
+            grid=(devices,),
+            in_specs=[
+                ours,
+                theirs,
+                pl.BlockSpec((1, slots, rows + more, share), joint_place),
+            ],
+            out_specs=(ours, theirs),
+        ),
+        cost_estimate=cost(
+            10 * count * (rows + more) ** 2 * share,
+            14 * count * (rows + more) * share,
+            count * (rows + more) ** 2 * 3,
+        ),
+        name="attend_back",
+    )(me, image, text, grad)
+
+
+def flat(array):
+    return array.reshape(-1, array.shape[-1])
+
+
+def normal_parts(field):
+    mean = jnp.mean(field, axis=-1, keepdims=True)
+    centred = field - mean
+    scale = lax.rsqrt(jnp.mean(centred * centred, axis=-1, keepdims=True) + EPS)
+    return centred * scale, scale
+
+
+def middle_kernel(width, joint_ref, weight_ref, bias_ref, mods_ref, *refs):
+    sources, outs = refs[:2], refs[2:]
+    at = pl.program_id(0)
+    low = 0
+    for which in range(2):
+        branch_ref, middle_ref, hidden_ref = outs[3 * which : 3 * which + 3]
+        slots, rows, _ = branch_ref.shape
+        left = joint_ref[0, :, low : low + rows].reshape(slots * rows, -1)
+        low += rows
+        term = contract(left, weight_ref[0, which], ((1,), (0,))).reshape(slots, rows, width)
+
+        @pl.when(at == 0)
+        def _(branch_ref=branch_ref, term=term, which=which):
+            branch_ref[...] = term + bias_ref[which]
+
+        @pl.when(at > 0)
+        def _(branch_ref=branch_ref, term=term):
+            branch_ref[...] += term
+
+        @pl.when(at == pl.num_programs(0) - 1)
+        def _(branch_ref=branch_ref, middle_ref=middle_ref, hidden_ref=hidden_ref, which=which):
+            for slot in range(slots):
+                mods = mods_ref[slot, which]
+                gate = mods[2 * width : 3 * width]
+                shift = mods[3 * width : 4 * width]
+                scale = mods[4 * width : 5 * width]
+                source = sources[which][slot].astype(WIDE)
+                middle = source + gate[None] * branch_ref[slot]
+                middle_ref[slot] = middle
+                normal, _ = normal_parts(middle)
+                hidden_ref[slot] = (normal * (1.0 + scale[None]) + shift[None]).astype(LOWER)
+
+
+def middle_stage(joint, weight, bias, mods, image, text):
+    devices, slots, total, share = joint.shape
+    width = image.shape[-1]
+    outs = []
+    for item in (image, text):
+        outs += [
+            jax.ShapeDtypeStruct(item.shape, WIDE),
+            jax.ShapeDtypeStruct(item.shape, WIDE),
+            jax.ShapeDtypeStruct(item.shape, LOWER),
+        ]
+
+    def whole(array):
+        return pl.BlockSpec(array.shape, lambda item: (0,) * len(array.shape))
+
+    return pl.pallas_call(
+        lambda *refs: middle_kernel(width, *refs),
+        out_shape=outs,
+        grid=(devices,),
+        in_specs=[
+            pl.BlockSpec((1, slots, total, share), lambda item: (item, 0, 0, 0)),
+            pl.BlockSpec((1, 2, share, width), lambda item: (item, 0, 0, 0)),
+            whole(bias),
+            whole(mods),
+            whole(image),
+            whole(text),
+        ],
+        out_specs=[whole(item) for item in outs],
+        cost_estimate=cost(2 * slots * total * width * width, 4 * width * width + 4000000),
+        name="middle",
+    )(joint, weight, bias, mods, image, text)
+
+
+def back_kernel(width, weight_ref, mods_ref, live_ref, *refs):
+    inputs, outs, joint_ref = refs[:10], refs[10:16], refs[16]
+    at = pl.program_id(0)
+    low = 0
+    for which in range(2):
+        own_ref, other_ref, middle_ref, branch_ref, cotangent_ref = inputs[
+            5 * which : 5 * which + 5
+        ]
+        d_middle_ref, d_branch_ref, sums_ref = outs[3 * which : 3 * which + 3]
+        slots, rows, _ = d_branch_ref.shape
+
+        @pl.when(at == 0)
+        def _(
+            own_ref=own_ref,
+            other_ref=other_ref,
+            middle_ref=middle_ref,
+            branch_ref=branch_ref,
+            cotangent_ref=cotangent_ref,
+            d_middle_ref=d_middle_ref,
+            d_branch_ref=d_branch_ref,
+            sums_ref=sums_ref,
+            which=which,
+        ):
+            for slot in range(slots):
+                mods = mods_ref[slot, which]
+                gate = mods[2 * width : 3 * width]
+                scale = mods[4 * width : 5 * width]
+                d_hidden = own_ref[slot].astype(WIDE) + other_ref[slot].astype(WIDE)
+                normal, spread_of = normal_parts(middle_ref[slot])
+                d_normal = d_hidden * (1.0 + scale[None])
+                pull = d_normal - jnp.mean(d_normal, axis=-1, keepdims=True)
+                pull = pull - normal * jnp.mean(d_normal * normal, axis=-1, keepdims=True)
+                cotangent = cotangent_ref[slot].astype(WIDE) * live_ref[slot]
+                d_middle = cotangent + spread_of * pull
+                d_middle_ref[slot] = d_middle
+                d_branch_ref[slot] = (d_middle * gate[None]).astype(LOWER)
+                sums_ref[slot, 0] = jnp.sum(d_middle * branch_ref[slot], axis=0)
+                sums_ref[slot, 1] = jnp.sum(d_hidden, axis=0)
+                sums_ref[slot, 2] = jnp.sum(d_hidden * normal, axis=0)
+
+        left = d_branch_ref[...].reshape(slots * rows, width)
+        piece = contract(left, weight_ref[0, which], ((1,), (1,))).astype(LOWER)
+        joint_ref[0, :, low : low + rows] = piece.reshape(slots, rows, -1)
+        low += rows
+
+
+def back_stage(weight, mods, live, pairs):
+    devices, _, share, width = weight.shape
+    flat_inputs = [item for group in pairs for item in group]
+    slots = mods.shape[0]
+    outs = []
+    total = 0
+    for group in pairs:
+        shape = group[2].shape
+        total += shape[1]
+        outs += [
+            jax.ShapeDtypeStruct(shape, WIDE),
+            jax.ShapeDtypeStruct(shape, LOWER),
+            jax.ShapeDtypeStruct((slots, 3, width), WIDE),
+        ]
+
+    def whole(array):
+        return pl.BlockSpec(array.shape, lambda item: (0,) * len(array.shape))
+
+    return pl.pallas_call(
+        lambda *refs: back_kernel(width, *refs),
+        out_shape=[*outs, jax.ShapeDtypeStruct((devices, slots, total, share), LOWER)],
+        grid=(devices,),
+        in_specs=[
+            pl.BlockSpec((1, 2, share, width), lambda item: (item, 0, 0, 0)),
+            whole(mods),
+            whole(live),
+            *[whole(item) for item in flat_inputs],
+        ],
+        out_specs=[
+            *[whole(item) for item in outs],
+            pl.BlockSpec((1, slots, total, share), lambda item: (item, 0, 0, 0)),
+        ],
+        cost_estimate=cost(2 * slots * total * width * width, 4 * width * width + 10000000),
+        name="back",
+    )(weight, mods, live, *flat_inputs)
+
+
+def split_body(
+    image,
+    text,
+    condition,
+    counts,
+    adaptive_weight,
+    adaptive_bias,
+    attend_weight,
+    attend_bias,
+    output_weight,
+    output_bias,
+    expand_weight,
+    expand_bias,
+    reduce_weight,
+    reduce_bias,
+    image_cotangent,
+    text_cotangent,
+):
+    slots, rows, width = image.shape
+    extra = text.shape[1]
+    me = lax.axis_index("shard")
+    me_array = me.astype(jnp.int32).reshape(1)
+    place = lax.axis_index("rep").astype(jnp.int32)
+    edge = ((place == 0) | (place == REPLICAS - 1)).astype(jnp.int32).reshape(1)
+    share = width // GROUP
+    size = width // HEADS
+    orders = (ORDER_ONE, ORDER_TWO)
+    spans = (rows, SPAN)
+
+    def padded(array):
+        return jnp.pad(array, ((0, 0), (0, SPAN - extra), (0, 0)))
+
+    alive = (jnp.arange(slots, dtype=jnp.int32) < counts[0]).astype(WIDE)[:, None, None]
+    sources = (image, padded(text))
+    streams = tuple(item.astype(WIDE) for item in sources)
+    pulls = (image_cotangent, padded(text_cotangent))
+    cotangents = tuple(item.astype(WIDE) * alive for item in pulls)
+    cond_value = condition.astype(WIDE)
+    cond_low = jax.nn.silu(cond_value).astype(LOWER)
+
+    small = jnp.concatenate(
+        [
+            cond_low,
+            *[
+                item.astype(LOWER)
+                for item in (adaptive_bias, attend_bias, output_bias, reduce_bias)
+            ],
+        ],
+        axis=1,
+    )
+    place_array = place.reshape(1)
+    packed_attend = pack(attend_weight, place_array, REPLICAS, 3, (0, 1))
+    packed_expand = pack(expand_weight, place_array, REPLICAS, 1, (0, 1))
+    output_low = output_weight.astype(LOWER)
+    small = after(small, packed_attend, packed_expand, output_low)
+    small_all = lax.all_gather(small, "shard", axis=0, tiled=False)
+    cond_cols = lax.dynamic_slice_in_dim(
+        pick(small_all[:, :, :width], [me ^ item for item in range(GROUP)]), me * share, share, 2
+    ).reshape(GROUP * slots, share)
+
+    def whole_bias(start, length):
+        piece = small_all[:, :, start : start + length]
+        return jnp.moveaxis(piece, 0, 1).reshape(2, GROUP * length).astype(WIDE)
+
+    at = width
+    biases = []
+    for item in (adaptive_bias, attend_bias, output_bias, reduce_bias):
+        biases.append(whole_bias(at, item.shape[1]))
+        at += item.shape[1]
+    adaptive_bias_full, attend_bias_full, output_bias_full, reduce_bias_full = biases
+    expand_bias_own = expand_bias.astype(LOWER).astype(WIDE)
+
+    adaptive_local = adaptive_weight.astype(LOWER)
+    partial_terms = project("gd,sde->gse", cond_cols, adaptive_local)
+    quarter = spread(packed_attend)
+    partial_terms = after(partial_terms, quarter).reshape(GROUP, slots, 2, 6 * width)
+    modulation = adaptive_bias_full[None] + partial_terms[0]
+    for item in range(1, GROUP):
+        modulation = modulation + swap(partial_terms[item], item)
+    parts = [
+        [modulation[:, which, piece * width : (piece + 1) * width] for piece in range(6)]
+        for which in range(2)
+    ]
+
+    turns = ring(quarter)
+    output_full = lax.all_gather(output_low, "shard", axis=0, tiled=False)
+    quarter = spread(after(packed_expand, turns[1]))
+    quarters = lax.all_gather(after(quarter, output_full, turns[3]), "rep", axis=0, tiled=False)
+    expand_own = [
+        jnp.moveaxis(quarters[:, :, which], 0, 1).reshape(width, 4 * share) for which in range(2)
+    ]
+    reduce_own = reduce_weight.astype(LOWER)
+
+    fronts = []
+    triples = []
+    query_bias = lax.dynamic_slice_in_dim(attend_bias_full, me * share, share, 1)
+    value_bias = lax.dynamic_slice_in_dim(attend_bias_full, width + me * share, share, 1)
+    triple_bias = jnp.concatenate([query_bias, jnp.zeros_like(query_bias), value_bias], axis=1)
+    hiddens = [
+        modulate(streams[which], parts[which][0], parts[which][1]).astype(LOWER)
+        for which in range(2)
+    ]
+    for stage in range(3):
+        hiddens = [after(item, turns[stage + 1]) for item in hiddens]
+        hiddens = [grow(hiddens[which], orders[which][stage]) for which in range(2)]
+    attend_own = arrange(turns, place_array)
+    for which in range(2):
+        front = hiddens[which].reshape(GROUP * slots * spans[which], width)
+        fronts.append(front)
+        triple = (project("rd,de->re", front, attend_own[which]) + triple_bias[which]).astype(LOWER)
+        triples.append(triple.reshape(GROUP, slots, spans[which], 3 * share))
+    d_seconds = []
+    for which in range(2):
+        d_second = (cotangents[which] * parts[which][5][:, None, :]).astype(LOWER)
+        d_seconds.append(grow(after(d_second, *fronts), orders[which][0]))
+    triples, d_seconds = together(triples, d_seconds)
+    d_seconds = [grow(d_seconds[which], orders[which][1]) for which in range(2)]
+    attended = attend_forward(triples[0], triples[1], me_array, size, rows + extra)
+    joint = spread(after(attended, *d_seconds))
+    d_seconds = [flat(grow(d_seconds[which], orders[which][2])) for which in range(2)]
+
+    branch_one, middle_one, hidden_one, branch_two, middle_two, hidden_two = middle_stage(
+        joint, output_full, output_bias_full, modulation, sources[0], sources[1]
+    )
+    branches = (branch_one, branch_two)
+    middles = (middle_one, middle_two)
+    feeds = []
+    for which, hidden in enumerate((hidden_one, hidden_two)):
+        feeds.append(flat(collect(hidden, orders[which])))
+
+    befores = []
+    actives = []
+    reduce_grads = []
+    for which in range(2):
+        before = project("rd,df->rf", feeds[which], expand_own[which]) + expand_bias_own[which]
+        befores.append(before)
+        active = smooth_gelu(before).astype(LOWER)
+        actives.append(active)
+        reduce_grads.append(project("rf,rd->fd", active, d_seconds[which]).astype(LOWER))
+    reduce_totals = lax.psum(tuple(reduce_grads), "rep")
+
+    pairs = []
+    expand_grads = []
+    expand_bias_grads = []
+    reduce_bias_grads = []
+    for which in range(2):
+        d_active = project("rd,fd->rf", d_seconds[which], reduce_own[which])
+        d_before = jax.vjp(smooth_gelu, befores[which])[1](d_active)[0].astype(LOWER)
+        d_hidden = project("rf,df->rd", d_before, expand_own[which]).astype(LOWER)
+        d_hidden = d_hidden.reshape(GROUP * slots, spans[which], width)
+        own, other = scatter_halves(d_hidden, orders[which])
+        pairs.append((own, other, middles[which], branches[which], pulls[which]))
+        expand_grads.append(project("rd,rf->df", feeds[which], d_before).astype(LOWER))
+        expand_bias_grads.append(jnp.sum(d_before, axis=0, dtype=WIDE))
+        d_cols = lax.dynamic_slice_in_dim(d_seconds[which], me * share, share, 1)
+        reduce_bias_grads.append(jnp.sum(d_cols, axis=0, dtype=WIDE))
+    live = jnp.broadcast_to(alive, (slots, 1, width))
+    d_middle_one, d_branch_one, sums_one, d_middle_two, d_branch_two, sums_two, d_joint = (
+        back_stage(output_full, modulation, live, pairs)
+    )
+    d_middles = (d_middle_one, d_middle_two)
+    d_branches = (d_branch_one, d_branch_two)
+    sums = (sums_one, sums_two)
+    d_attended = spread(d_joint)
+    d_attended, grown, expand_grads = together([d_attended], list(d_branches), expand_grads)
+    (d_attended,) = d_attended
+    expand_grads = [item.reshape(GROUP, share, 4 * share) for item in expand_grads]
+    grown = [grow(grown[which], orders[which][0]) for which in range(2)]
+    d_triples = attend_backward(
+        triples[0], triples[1], d_attended, me_array, size, rows + extra
+    )
+    expand_one = spread(expand_grads[0])
+    (expand_one,), d_triples, grown = together([expand_one], list(d_triples), grown)
+
+    d_triples = [flat(item) for item in d_triples]
+    attend_grads = [
+        project("rd,re->de", fronts[which], d_triples[which]).astype(LOWER) for which in range(2)
+    ]
+    expand_two = spread(expand_grads[1])
+    grown = [grow(grown[which], orders[which][1]) for which in range(2)]
+    d_fronts = [
+        project("re,de->rd", d_triples[which], attend_own[which])
+        .astype(LOWER)
+        .reshape(GROUP * slots, spans[which], width)
+        for which in range(2)
+    ]
+    (expand_two,), attend_grads, grown, d_fronts = together(
+        [expand_two], attend_grads, grown, d_fronts
+    )
+    attend_grads = [item.reshape(GROUP, share, 3 * share) for item in attend_grads]
+
+    def halved(arrays, stage):
+        found = []
+        for which, array in enumerate(arrays):
+            half = array.shape[0] // 2
+            found += [array[:half], swap(array[half:], orders[which][2 - stage])]
+        return found
+
+    def summed(pairs, kind=LOWER):
+        return [
+            (pairs[2 * which].astype(WIDE) + pairs[2 * which + 1].astype(WIDE)).astype(kind)
+            for which in range(2)
+        ]
+
+    def halves(array):
+        middle = array.shape[1] // 2
+        return array[:, :middle], array[:, middle:]
+
+    tree = ReplicaSum()
+    handles = []
+    reduce_totals, (expand_one, expand_two) = together(
+        list(reduce_totals), [expand_one, expand_two]
+    )
+    expand_parts = [*halves(expand_one), *halves(expand_two)]
+
+    handles.append(tree.add(expand_parts[0]))
+    grown = [grow(grown[which], orders[which][2]) for which in range(2)]
+    attend_one = spread(attend_grads[0])
+    (attend_one,), grown, pairs = tree.step([attend_one], grown, halved(d_fronts, 0))
+
+    handles.append(tree.add(expand_parts[1]))
+    d_fronts = summed(pairs)
+    attend_two = spread(attend_grads[1])
+    ordered = pick(attended, [me ^ item for item in distances(ORDER_ONE)])
+    output_grads = []
+    output_bias_grads = []
+    for which in range(2):
+        d_branch_all = flat(grown[which])
+        pieces = ordered[:, :, :rows] if which == 0 else ordered[:, :, rows:]
+        if which == 1:
+            turned = [distances(ORDER_ONE).index(item) for item in distances(ORDER_TWO)]
+            pieces = jnp.concatenate([pieces[item : item + 1] for item in turned], axis=0)
+        output_grads.append(project("rd,re->de", flat(pieces), d_branch_all).astype(LOWER))
+        d_cols = lax.dynamic_slice_in_dim(d_branch_all, me * share, share, 1)
+        output_bias_grads.append(jnp.sum(d_cols, axis=0, dtype=WIDE))
+    (attend_two,), pairs, output_grads = tree.step(
+        [attend_two], halved(d_fronts, 1), output_grads
+    )
+
+    handles.append(tree.add(expand_parts[2]))
+    d_fronts = summed(pairs)
+    seconds = [
+        project("rf,fd->rd", actives[which], reduce_own[which])
+        .astype(LOWER)
+        .reshape(GROUP * slots, spans[which], width)
+        for which in range(2)
+    ]
+    pairs, seconds = tree.step(halved(d_fronts, 2), seconds)
+
+    handles.append(tree.add(expand_parts[3]))
+    d_fronts = summed(pairs, WIDE)
+    input_grads = []
+    front_mods = []
+    for which in range(2):
+        d_stream, d_shift_front, d_scale_front = jax.vjp(
+            modulate, streams[which], parts[which][0], parts[which][1]
+        )[1](d_fronts[which])
+        input_grads.append((d_middles[which] + d_stream).astype(LOWER))
+        front_mods += [d_shift_front, d_scale_front]
+    pairs, front_mods, input_grads = tree.step(halved(seconds, 0), front_mods, input_grads)
+
+    handles.append(tree.add(jnp.stack(output_grads)))
+    (pairs,) = tree.step(halved(summed(pairs), 1))
+
+    attend_parts = [*halves(attend_one), *halves(attend_two)]
+    handles.append(tree.add(attend_parts[0]))
+    (pairs,) = tree.step(halved(summed(pairs), 2))
+
+    seconds = summed(pairs, WIDE)
+    outputs = []
+    d_mods = []
+    attend_bias_grads = []
+    for which in range(2):
+        second = seconds[which] + reduce_bias_full[which]
+        gate = parts[which][5][:, None, :]
+        outputs.append(((middles[which] + gate * second) * alive).astype(LOWER))
+        gate_feed = jnp.sum(cotangents[which] * second, axis=1)
+        column_sums = jnp.sum(d_triples[which], axis=0, dtype=WIDE)
+        attend_bias_grads.append(
+            jnp.concatenate([column_sums[:share], column_sums[2 * share :]]).astype(LOWER)
+        )
+        d_mods.append(
+            jnp.concatenate(
+                [
+                    *front_mods[2 * which : 2 * which + 2],
+                    sums[which][:, 0],
+                    sums[which][:, 1],
+                    sums[which][:, 2],
+                    gate_feed,
+                ],
+                axis=-1,
+            )
+        )
+
+    d_modulation = jnp.stack(d_mods, axis=1).astype(LOWER)
+    packed = jnp.concatenate(
+        [
+            d_modulation.reshape(-1),
+            cond_low.reshape(-1),
+            *[item for item in attend_bias_grads],
+            *[item.astype(LOWER) for item in output_bias_grads],
+            *[item.astype(LOWER) for item in expand_bias_grads],
+            *[item.astype(LOWER) for item in reduce_bias_grads],
+        ]
+    )
+    handles.append(tree.add(attend_parts[1]))
+    ((across,),) = tree.step([around(packed)])
+    modulation_size = d_modulation.size
+    cond_size = cond_low.size
+    keep = modulation_size + cond_size + 4 * share
+    rest = jnp.sum(across[:, keep:], axis=0, dtype=WIDE)
+    output_bias_total = rest[: 2 * share].reshape(2, share)
+    expand_bias_total = rest[2 * share : 10 * share].reshape(2, 4 * share)
+    reduce_bias_total = rest[10 * share :].reshape(2, share)
+    apart = [me ^ item for item in range(GROUP)]
+    places = [((item >> 1) & 1) + 2 * (item >> 2) + 4 * (item & 1) for item in apart]
+    every = across[None, :, :keep]
+    for stage in range(3):
+        if stage < 2:
+            handles.append(tree.add(attend_parts[2 + stage]))
+        ((every,),) = tree.step([grow(every, ORDER_ONE[stage])])
+    modulation_all = every[:, :, :modulation_size].reshape(
+        GROUP, REPLICAS, slots, 2, 6 * width
+    )
+    cond_all = every[:, :, modulation_size : modulation_size + cond_size].reshape(
+        GROUP * REPLICAS * slots, width
+    )
+    bias_all = jnp.sum(every[:, :, modulation_size + cond_size :], axis=1, dtype=WIDE)
+    bias_all = pick(bias_all, places)
+    bias_all = bias_all.reshape(GROUP, 2, 2, share).transpose(1, 2, 0, 3).reshape(2, 2 * width)
+    attend_bias_total = lax.dynamic_slice_in_dim(bias_all, me * 2 * share, 2 * share, 1)
+    group_modulation = lax.dynamic_index_in_dim(
+        modulation_all, place, 1, keepdims=False
+    ).reshape(GROUP * slots, 2, 6 * width)
+    modulation_all = modulation_all.reshape(GROUP * REPLICAS * slots, 2, 6 * width)
+    adaptive_total = project(
+        "gd,gse->sde",
+        lax.dynamic_slice_in_dim(cond_all, me * share, share, 1),
+        modulation_all,
+    )
+    own_cols = lax.dynamic_slice_in_dim(modulation_all, me * 6 * share, 6 * share, 2)
+    adaptive_bias_total = jnp.sum(own_cols, axis=0, dtype=WIDE)
+    cond_parts = project("gse,sde->gd", group_modulation, adaptive_local)
+    cond_parts = pick(cond_parts.reshape(GROUP, slots, share), places)
+    d_cond_act = lax.all_to_all(cond_parts, "shard", split_axis=0, concat_axis=2, tiled=True)
+    condition_grad = (
+        jax.vjp(jax.nn.silu, cond_value)[1](d_cond_act[0])[0].astype(LOWER)
+    )
+    tree.step()
+    done = [tuple(item[:2]) for item in handles]
+    reduce_parts = [[(item.reshape(1, 4 * share, width),)] for item in reduce_totals]
+    reduce_total = unpack(reduce_parts, edge, 1)
+    expand_total = unpack([done[0:2], done[2:4]], edge, 1)
+    output_parts = [[tuple(item[at : at + 1] for item in done[4])] for at in range(2)]
+    output_total = unpack(output_parts, edge, 1)
+    attend_total = unpack([done[5:7], done[7:9]], edge, 3)
+    return (
+        outputs[0],
+        outputs[1][:, :extra],
+        input_grads[0],
+        input_grads[1][:, :extra],
+        condition_grad,
+        adaptive_total,
+        adaptive_bias_total,
+        attend_total,
+        attend_bias_total,
+        output_total,
+        output_bias_total,
+        expand_total,
+        expand_bias_total,
+        reduce_total,
+        reduce_bias_total,
+    )
+
+
 def solution(mesh):
     in_specs = (
         P(("shard", "rep"), None, None),
@@ -361,4 +1257,6 @@
         P(None, "shard", None),
         P(None, "shard"),
     )
+    fits = mesh.shape["shard"] == GROUP and mesh.shape["rep"] == REPLICAS
+    body = split_body if fits else gathered_body
     return jax.shard_map(body, mesh=mesh, in_specs=in_specs, out_specs=out_specs, check_vma=False)

time: 2350 us -> 987 us (0.42)
  waiting for transfers between devices: 1840 us -> 388 us
  matrix products: 258 us -> 108 us
  starting transfers between devices: 4.21 us -> 144 us
  Pallas kernels: 0 us -> 111 us
  blocking collectives: 86.8 us -> 12.4 us
  local copies, waits for them, and re-layouts: 42.8 us -> 98.5 us
    psum x1, waiting for transfers between devices: 684 us -> 38 us  [split_body(): reduce_totals = lax.psum(tuple(reduce_grads), 'rep')]
    reduce_scatter x8 -> x0, waiting for transfers between devices: 617 us -> none  [the longest x2 256 us: body(): lax.psum_scatter(expand_grad.astype(jnp.bfloat16), 'shard', scatter_dimen...]
    all_gather x4 -> x2, waiting for transfers between devices: 500 us -> 0.02 us  [the longest x1 0.02 us: split_body(): output_full = lax.all_gather(output_low, 'shard', axis=0, tiled=False)]
    ppermute x0 -> x85, waiting for transfers between devices: none -> 329 us  [the longest x52 175 us: swap(): lax.ppermute(array, 'shard', [(item, item ^ step) for item in range(GROUP)])]
    dot_general x33 -> x23, matrix products: 258 us -> 108 us  [project(): return jnp.einsum(form, left, right, preferred_element_type=WIDE)]
    pallas_call x0 -> x11, Pallas kernels: none -> 111 us  [the longest x4 34.7 us: unpack(): pl.pallas_call(kernel, out_shape=jax.ShapeDtypeStruct((2, total, pieces *...]
    ppermute x0 -> x85, starting transfers between devices: none -> 105 us  [the longest x27 55.6 us: step(): entry[1] = lax.ppermute(entry[0], 'rep', HOPS[entry[2]])]
    all_gather x7 -> x1, blocking collectives: 66.5 us -> 12.4 us  [split_body(): small_all = lax.all_gather(small, 'shard', axis=0, tiled=False)]
  transfers between devices with their start and end apart: 16 -> 97, of which waited for: 12 -> 43; matrix products, arithmetic and copies ran while one was open for 13% -> 26% of each run, Pallas kernels for 0% -> 9%
where the time goes in v2:
time: 987 us; the launch traced here: 975 us
  waiting for transfers between devices  388 us (39%)
  starting transfers between devices  144 us (15%)
  Pallas kernels  111 us (11%)
  matrix products  108 us (11%)
  local copies, waits for them, and re-layouts  98.5 us (10%)
  other arithmetic  96.3 us (10%)
  between operations  17.4 us (2%)
  blocking collectives  12.4 us (1%)
    ppermute x52, waiting for transfers between devices, swap(): lax.ppermute(array, 'shard', [(item, item ^ step) for item in range(GROUP)])  175 us
    ppermute x27, waiting for transfers between devices, step(): entry[1] = lax.ppermute(entry[0], 'rep', HOPS[entry[2]])  121 us
    dot_general x23, matrix products, project(): return jnp.einsum(form, left, right, preferred_element_type=WIDE)  108 us
    ppermute x27, starting transfers between devices, step(): entry[1] = lax.ppermute(entry[0], 'rep', HOPS[entry[2]])  55.6 us
    ppermute x52, starting transfers between devices, swap(): lax.ppermute(array, 'shard', [(item, item ^ step) for item in range(GROUP)])  44.1 us
    psum x1, waiting for transfers between devices, split_body(): reduce_totals = lax.psum(tuple(reduce_grads), 'rep')  38 us
    concatenate x25, other arithmetic, grow(): return jnp.concatenate([array, swap(array, step)], axis=0)  37.5 us
    all_to_all x8, starting transfers between devices, spread(): lax.all_to_all(array, 'shard', split_axis=0, concat_axis=0, tiled=True)  34.7 us
  transfers between devices with their start and end apart: 97, of which 43 were waited for; matrix products, arithmetic and copies ran while one was open for 26% of the time, Pallas kernels for 9%

profile of v2, /device:TPU:0, one launch (start us, length us, event | category | flops | bytes accessed | tf_op | source)
XLA Modules:
  0.0 974.8 jit_solution(16346204239772767156)
XLA Ops:
  9.6 5.2 all-to-all-start
  20.5 12.4 %all-gather.3 = bf16[8,2,3456]{2,1,0:T(2,128)(2,1)S(1)} all-gather(bf16[1,2,3456]{2,1,0:T(2,128)(2,1)S(1)} %bitcast.229), channel_id=2, replica_groups=mesh['shard'=8,'rep'=4] {'shard'}, dimensions={0}, use_global_device_ids=true | all-gather | bytes 124416 | tf_op jit(solution)/shard_map/all_gather | solution.py:904
  34.2 6.1 fusion.11
  51.6 8.7 collective-permute-done.4
  63.1 12.2 %collective-permute-done.7.refs_1_ = bf16[8,2,48,576]{3,2,1,0:T(8,128)(2,1)S(1)} collective-permute-done((bf16[8,2,48,576]{3,2,1,0:T(8,128)(2,1)S(1)}, bf16[8,2,48,576]{3,2,1,0:T(8,128)(2,1)S(1)}, u32[]{:S(2)}, u32[]{:S(2)}) %collective-permute-start.7) | collective-permute-done | bytes 884768 | tf_op jit(solution)/shard_map/ppermute | solution.py:506
  78.0 12.8 %collective-permute-done.8 = bf16[2,64,1536]{2,1,0:T(8,128)(2,1)S(1)} collective-permute-done((bf16[2,64,1536]{2,1,0:T(8,128)(2,1)S(1)}, bf16[2,64,1536]{2,1,0:T(8,128)(2,1)S(1)}, u32[]{:S(2)}, u32[]{:S(2)}) %collective-permute-start.8) | collective-permute-done | bytes 393248 | tf_op jit(solution)/shard_map/ppermute | solution.py:346
  90.9 4.2 collective-permute-done.13
  95.3 7.3 collective-permute-done.9.refs_2_
  106.3 16.4 %collective-permute-done.10 = bf16[4,64,1536]{2,1,0:T(8,128)(2,1)} collective-permute-done((bf16[4,64,1536]{2,1,0:T(8,128)(2,1)S(1)}, bf16[4,64,1536]{2,1,0:T(8,128)(2,1)}, u32[]{:S(2)}, u32[]{:S(2)}) %collective-permute-start.10) | collective-permute-done | bytes 786464 | tf_op jit(solution)/shard_map/ppermute | solution.py:346
  124.2 4.7 collective-permute-done.11.refs_3_
  132.9 4.3 all-to-all-start.2
  168.9 10.9 %attend.1 = bf16[8,2,144,192]{3,2,1,0:T(8,128)(2,1)} custom-call(s32[1]{0:T(128)} %bitcast.refs_0_, bf16[8,2,64,576]{3,2,1,0:T(8,128)(2,1)} %bitcast.177, bf16[8,2,80,576]{3,2,1,0:T(8,128)(2,1)} %bitcast.175), custom_call_target="tpu_custom_call" | custom-call | flops 254803968 | bytes 3538944 | tf_op jit(solution)/shard_map/attend/pallas_call | solution.py:637
  184.8 5.4 collective-permute-done.19
  192.5 4.4 all-to-all-start.1
  199.3 14.5 %all-to-all-done.1.refs_0_ = bf16[8,2,144,192]{3,2,1,0:T(8,128)(2,1)} async-done(((bf16[8,2,144,192]{3,2,1,0:T(8,128)(2,1)}), bf16[8,2,144,192]{3,2,1,0:T(8,128)(2,1)}, u32[]{:S(2)}, u32[]{:S(2)}) %all-to-all-start.1) | async-done | bytes 884768 | tf_op jit(solution)/shard_map/all_to_all | solution.py:374
  213.7 12.3 %middle.1 = (f32[2,64,1536]{2,1,0:T(8,128)}, f32[2,64,1536]{2,1,0:T(8,128)}, bf16[2,64,1536]{2,1,0:T(8,128)(2,1)}, f32[2,80,1536]{2,1,0:T(8,128)}, f32[2,80,1536]{2,1,0:T(8,128)}, /*index=5*/bf16[2,80,1536]{2,1,0:T(8,128)(2,1)}) custom-call(bf16[8,2,144,192]{3,2,1,0:T(8,128)(2,1)} %all-to-all-done.1.refs_0_, bf16[8,2,192,1536]{3,2,1,0:T(8,128)(2,1)} %bitcast.171, ...), custom_call_target="tpu_custom_call" | custom-call | flops 1358954496 | bytes 13437184 | tf_op jit(solution)/shard_map/middle/pallas_call | solution.py:748
  228.7 6.5 convert_element_type.547
  239.4 11.2 %collective-permute-done.24 = bf16[2,80,1536]{2,1,0:T(8,128)(2,1)S(1)} collective-permute-done((bf16[2,80,1536]{2,1,0:T(8,128)(2,1)S(1)}, bf16[2,80,1536]{2,1,0:T(8,128)(2,1)S(1)}, u32[]{:S(2)}, u32[]{:S(2)}) %collective-permute-start.24) | collective-permute-done | bytes 491552 | tf_op jit(solution)/shard_map/ppermute | solution.py:346
  259.5 6.8 collective-permute-done.21
  266.5 5.8 collective-permute-done.25
  297.1 6.6 fusion.105
  306.3 4.8 fusion.104
  318.7 4.7 convolution_convert_fusion.9
  324.0 5.1 convolution_convert_fusion
  330.0 13.8 %collective-permute-done.29 = bf16[4,64,1536]{2,1,0:T(8,128)(2,1)S(1)} collective-permute-done((bf16[4,64,1536]{2,1,0:T(8,128)(2,1)S(1)}, bf16[4,64,1536]{2,1,0:T(8,128)(2,1)S(1)}, u32[]{:S(2)}, u32[]{:S(2)}) %collective-permute-start.29) | collective-permute-done | bytes 786464 | tf_op jit(solution)/shard_map/ppermute | solution.py:346
  345.1 9.2 collective-permute-done.32
  362.3 5.5 collective-permute-done.33.refs_9_
  368.5 15.2 %back.1 = (f32[2,64,1536]{2,1,0:T(8,128)}, bf16[2,64,1536]{2,1,0:T(8,128)(2,1)}, f32[2,3,1536]{2,1,0:T(4,128)}, f32[2,80,1536]{2,1,0:T(8,128)}, bf16[2,80,1536]{...) custom-call(bf16[8,2,192,1536]{3,2,1,0:T(8,128)(2,1)} %bitcast.172, ...), custom_call_target="tpu_custom_call" | custom-call | flops 1358954496 | bytes 19437184 | tf_op jit(solution)/shard_map/back/pallas_call | solution.py:830
  387.5 6.0 convolution_convert_fusion.6
  395.0 6.9 convolution_convert_fusion.8
  408.8 7.3 convolution_convert_fusion.4
  419.7 29.0 %attend_back.1 = (bf16[8,2,64,576]{3,2,1,0:T(8,128)(2,1)}, bf16[8,2,80,576]{3,2,1,0:T(8,128)(2,1)}) custom-call(s32[1]{0:T(128)} %bitcast.refs_0_, bf16[8,2,64,576]{3,2,1,0:T(8,128)(2,1)} %bitcast.178, bf16[8,2,80,576]{3,2,1,0:T(8,128)(2,1)} %bitcast.176, bf16[8,2,144,192]{3,2,1,0:T(8,128)(2,1)} %copy-done.15), custom_call_target="tpu_custom_call" | custom-call | flops 637009920 | bytes 6193152 | tf_op jit(solution)/shard_map/attend_back/pallas_call | solution.py:665
  451.9 4.8 all-to-all-start.5
  460.3 7.4 convolution_convert_fusion.1
  476.8 6.5 convolution_convert_fusion.11
  483.3 18.8 %collective-permute-done.36 = bf16[4,64,1536]{2,1,0:T(8,128)(2,1)} collective-permute-done((bf16[4,64,1536]{2,1,0:T(8,128)(2,1)}, bf16[4,64,1536]{2,1,0:T(8,128)(2,1)}, u32[]{:S(2)}, u32[]{:S(2)}) %collective-permute-start.36) | collective-permute-done | bytes 786464 | tf_op jit(solution)/shard_map/ppermute | solution.py:346
  509.6 4.6 fusion.76
  520.5 4.3 all-to-all-start.6
  526.5 38.0 %all-reduce.5.cloned.1.call-done = (bf16[768,1536]{1,0:T(8,128)(2,1)}, bf16[768,1536]{1,0:T(8,128)(2,1)}) async-done(((bf16[768,1536]{1,0:T(8,128)(2,1)}, bf16[768,1536]{1,0:T(8,128)(2,1)}), (bf16[768,1536]{1,0:T(8,128)(2,1)}, bf16[768,1536]{1,0:T(8,128)(2,1)})) %all-reduce.5.cloned.1.call-update) | async-done | bytes 4718608 | tf_op jit(solution)/shard_map/psum | solution.py:988
  572.4 8.0 unpack.7
  594.2 4.3 all-to-all-start.7
  624.3 15.4 %collective-permute-done.45 = bf16[4,64,1536]{2,1,0:T(8,128)(2,1)} collective-permute-done((bf16[4,64,1536]{2,1,0:T(8,128)(2,1)}, bf16[4,64,1536]{2,1,0:T(8,128)(2,1)}, u32[]{:S(2)}, u32[]{:S(2)}) %collective-permute-start.45) | collective-permute-done | bytes 786464 | tf_op jit(solution)/shard_map/ppermute | solution.py:346
  639.7 4.3 collective-permute-done.46
  658.6 4.8 collective-permute-start.54
  665.1 15.9 %collective-permute-done.47.refs_1_ = bf16[8,96,768]{2,1,0:T(8,128)(2,1)S(1)} collective-permute-done((bf16[8,96,768]{2,1,0:T(8,128)(2,1)S(1)}, bf16[8,96,768]{2,1,0:T(8,128)(2,1)S(1)}, u32[]{:S(2)}, u32[]{:S(2)}) %collective-permute-start.47) | collective-permute-done | bytes 1179680 | tf_op jit(solution)/shard_map/ppermute | solution.py:420
  690.3 5.3 collective-permute-start.59
  695.6 22.6 %collective-permute-done.52.refs_3_ = bf16[8,96,768]{2,1,0:T(8,128)(2,1)S(1)} collective-permute-done((bf16[8,96,768]{2,1,0:T(8,128)(2,1)S(1)}, bf16[8,96,768]{2,1,0:T(8,128)(2,1)S(1)}, u32[]{:S(2)}, u32[]{:S(2)}) %collective-permute-start.52) | collective-permute-done | bytes 1179680 | tf_op jit(solution)/shard_map/ppermute | solution.py:420
  725.5 4.7 collective-permute-start.64
  730.2 9.5 collective-permute-done.60
  743.0 8.8 collective-permute-done.57.refs_5_
  759.0 5.6 collective-permute-start.69
  766.6 5.3 collective-permute-start.75
  771.9 11.8 %collective-permute-done.62.refs_7_ = bf16[8,96,768]{2,1,0:T(8,128)(2,1)S(1)} collective-permute-done((bf16[8,96,768]{2,1,0:T(8,128)(2,1)S(1)}, bf16[8,96,768]{2,1,0:T(8,128)(2,1)S(1)}, u32[]{:S(2)}, u32[]{:S(2)}) %collective-permute-start.62) | collective-permute-done | bytes 1179680 | tf_op jit(solution)/shard_map/ppermute | solution.py:420
  792.9 10.7 %unpack.6 = f32[2,192,6144]{2,1,0:T(8,128)} custom-call(s32[1]{0:T(128)} %bitcast.64.edge_ref, bf16[8,96,768]{2,1,0:T(8,128)(2,1)} %copy-done.16, bf16[8,96,768]{2,1,0:T(8,128)(2,1)} %copy-done.62, bf16[8,96,768]{2,1,0:T(8,128)(2,1)} %copy-done.17, bf16[8,96,768]{2,1,0:T(8,128)(2,1)} %copy-done.63, bf16[8,96,768]{2,1,0:T(8,128)(2,1)} %copy-done.18, ...), custom_call_target="tpu_custom_call" | custom-call | bytes 18874368 | tf_op jit(solution)/shard_map/unpack/pallas_call | solution.py:551
  803.7 7.8 collective-permute-done.70
  819.8 19.1 %collective-permute-done.67 = bf16[2,192,1536]{2,1,0:T(8,128)(2,1)S(1)} collective-permute-done((bf16[2,192,1536]{2,1,0:T(8,128)(2,1)S(1)}, bf16[2,192,1536]{2,1,0:T(8,128)(2,1)S(1)}, u32[]{:S(2)}, u32[]{:S(2)}) %collective-permute-start.67) | collective-permute-done | bytes 1179680 | tf_op jit(solution)/shard_map/ppermute | solution.py:420
  847.4 12.9 %collective-permute-done.73.refs_1_ = bf16[8,96,576]{2,1,0:T(8,128)(2,1)S(1)} collective-permute-done((bf16[8,96,576]{2,1,0:T(8,128)(2,1)S(1)}, bf16[8,96,576]{2,1,0:T(8,128)(2,1)S(1)}, u32[]{:S(2)}, u32[]{:S(2)}) %collective-permute-start.73) | collective-permute-done | bytes 884768 | tf_op jit(solution)/shard_map/ppermute | solution.py:420
  866.1 5.1 collective-permute-done.80
  873.4 8.7 collective-permute-done.77.refs_3_
  885.4 6.2 unpack.5
  899.0 21.5 %collective-permute-done.81.refs_5_ = bf16[8,96,576]{2,1,0:T(8,128)(2,1)S(1)} collective-permute-done((bf16[8,96,576]{2,1,0:T(8,128)(2,1)S(1)}, bf16[8,96,576]{2,1,0:T(8,128)(2,1)S(1)}, u32[]{:S(2)}, u32[]{:S(2)}) %collective-permute-start.81) | collective-permute-done | bytes 884768 | tf_op jit(solution)/shard_map/ppermute | solution.py:420
  934.9 7.1 fusion.31
  948.7 7.4 convolution_bitcast_fusion
  958.3 9.8 %unpack.4 = f32[2,192,4608]{2,1,0:T(8,128)} custom-call(s32[1]{0:T(128)} %bitcast.64.edge_ref, bf16[8,96,576]{2,1,0:T(8,128)(2,1)} %copy-done.27, bf16[8,96,576]{2,1,0:T(8,128)(2,1)} %copy-done.67, bf16[8,96,576]{2,1,0:T(8,128)(2,1)} %copy-done.28, bf16[8,96,576]{2,1,0:T(8,128)(2,1)} %copy-done.68, bf16[8,96,576]{2,1,0:T(8,128)(2,1)} %copy-done.29, ...), custom_call_target="tpu_custom_call" | custom-call | bytes 14155776 | tf_op jit(solution)/shard_map/unpack/pallas_call | solution.py:551
  (692 shorter events, 344.3 us)
Async XLA Ops:
  9.6 30.7 %all-to-all-start = ((bf16[8,2,48,576]{3,2,1,0:T(8,128)(2,1)}), bf16[8,2,48,576]{3,2,1,0:T(8,128)(2,1)S(1)}, u32[]{:S(2)}, u32[]{:S(2)}) async-start(bf16[8,2,48,576]{3,2,1,0:T(8,128)(2,1)} %pack.2), calls=%async_computation | async-start | bytes 1966080 | tf_op jit(solution)/shard_map/all_to_all | solution.py:374
  14.7 150.2 %all-gather.7.cloned.1.call-start = ((), (), s32[]{:S(2)}) async-start(), calls=%async_computation.9 | async-start | bytes 10616832 | tf_op jit(solution)/shard_map/all_gather | solution.py:934
  50.0 25.3 %collective-permute-start.7 = (bf16[8,2,48,576]{3,2,1,0:T(8,128)(2,1)S(1)}, bf16[8,2,48,576]{3,2,1,0:T(8,128)(2,1)S(1)}, u32[]{:S(2)}, u32[]{:S(2)}) collective-permute-start(bf16[8,2,48,576]{3,2,1,0:T(8,128)(2,1)S(1)} %all-to-all-done.refs_0_), channel_id=1, source_target_pairs={{0,1},{1,2},{2,3},{3,0},{4,5},{5,6},{6,7},{7,4},{8,9},{9,10},{10,1... | collective-permute-start | bytes 2654216 | tf_op jit(solution)/shard_map/ppermute | solution.py:506
  77.0 25.6 %collective-permute-start.9 = (bf16[8,2,48,576]{3,2,1,0:T(8,128)(2,1)S(1)}, bf16[8,2,48,576]{3,2,1,0:T(8,128)(2,1)}, u32[]{:S(2)}, u32[]{:S(2)}) collective-permute-start(bf16[8,2,48,576]{3,2,1,0:T(8,128)(2,1)S(1)} %collective-permute-done.7.refs_1_), channel_id=1, source_target_pairs={{0,1},{1,2},{2,3},{3,0},{4,5},{5,6},{6,7},{7,4},{8,9},{9,10},{10,1... | collective-permute-start | bytes 2654216 | tf_op jit(solution)/shard_map/ppermute | solution.py:506
  77.5 17.7 %collective-permute-start.13 = (bf16[2,80,1536]{2,1,0:T(8,128)(2,1)S(1)}, bf16[2,80,1536]{2,1,0:T(8,128)(2,1)S(1)}, u32[]{:S(2)}, u32[]{:S(2)}) collective-permute-start(bf16[2,80,1536]{2,1,0:T(8,128)(2,1)S(1)} %fusion.35), channel_id=1, source_target_pairs={{0,16},{4,20},{8,24},{12,28},{16,0},{20,4},{24,8},{28,12},{1,17},{... | collective-permute-start | bytes 1474568 | tf_op jit(solution)/shard_map/ppermute | solution.py:346
  102.6 26.3 %collective-permute-start.14 = (bf16[4,80,1536]{2,1,0:T(8,128)(2,1)S(1)}, bf16[4,80,1536]{2,1,0:T(8,128)(2,1)}, u32[]{:S(2)}, u32[]{:S(2)}) collective-permute-start(bf16[4,80,1536]{2,1,0:T(8,128)(2,1)S(1)} %pad_maximum_fusion.17), channel_id=1, source_target_pairs={{0,8},{4,12},{8,0},{12,4},{16,24},{20,28},{24,16},{28,20},{1,9},{5... | collective-permute-start | bytes 2949128 | tf_op jit(solution)/shard_map/ppermute | solution.py:346
  103.6 19.1 %collective-permute-start.10 = (bf16[4,64,1536]{2,1,0:T(8,128)(2,1)S(1)}, bf16[4,64,1536]{2,1,0:T(8,128)(2,1)}, u32[]{:S(2)}, u32[]{:S(2)}) collective-permute-start(bf16[4,64,1536]{2,1,0:T(8,128)(2,1)S(1)} %pad_maximum_fusion.21), channel_id=1, source_target_pairs={{0,16},{4,20},{8,24},{12,28},{16,0},{20,4},{24,8},{28,12},{1,17},{... | collective-permute-start | bytes 2359304 | tf_op jit(solution)/shard_map/ppermute | solution.py:346
  104.7 24.2 %collective-permute-start.11 = (bf16[8,2,48,576]{3,2,1,0:T(8,128)(2,1)}, bf16[8,2,48,576]{3,2,1,0:T(8,128)(2,1)}, u32[]{:S(2)}, u32[]{:S(2)}) collective-permute-start(bf16[8,2,48,576]{3,2,1,0:T(8,128)(2,1)} %collective-permute-done.9.refs_2_), channel_id=1, source_target_pairs={{0,1},{1,2},{2,3},{3,0},{4,5},{5,6},{6,7},{7,4},{8,9},{9,10},{10,1... | collective-permute-start | bytes 2654216 | tf_op jit(solution)/shard_map/ppermute | solution.py:506
  132.9 32.1 %all-to-all-start.2 = ((bf16[8,2,48,768]{3,2,1,0:T(8,128)(2,1)}), bf16[8,2,48,768]{3,2,1,0:T(8,128)(2,1)}, u32[]{:S(2)}, u32[]{:S(2)}) async-start(bf16[8,2,48,768]{3,2,1,0:T(8,128)(2,1)} %pack.3), calls=%async_computation.2 | async-start | bytes 2359296 | tf_op jit(solution)/shard_map/all_to_all | solution.py:374
  137.1 151.6 %all-gather.9.cloned.1.call-start = ((), (), s32[]{:S(2)}) async-start(), calls=%async_computation.10 | async-start | bytes 5898240 | tf_op jit(solution)/shard_map/all_gather | solution.py:936
  166.1 18.6 %collective-permute-start.18 = (bf16[4,64,1536]{2,1,0:T(8,128)(2,1)S(1)}, bf16[4,64,1536]{2,1,0:T(8,128)(2,1)S(1)}, u32[]{:S(2)}, u32[]{:S(2)}) collective-permute-start(bf16[4,64,1536]{2,1,0:T(8,128)(2,1)S(1)} %pad_maximum_fusion.22), channel_id=1, source_target_pairs={{0,16},{4,20},{8,24},{12,28},{16,0},{20,4},{24,8},{28,12},{1,17},{... | collective-permute-start | bytes 2359304 | tf_op jit(solution)/shard_map/ppermute | solution.py:346
  167.4 22.8 %collective-permute-start.19 = (bf16[4,80,1536]{2,1,0:T(8,128)(2,1)S(1)}, bf16[4,80,1536]{2,1,0:T(8,128)(2,1)}, u32[]{:S(2)}, u32[]{:S(2)}) collective-permute-start(bf16[4,80,1536]{2,1,0:T(8,128)(2,1)S(1)} %pad_maximum_fusion.18), channel_id=1, source_target_pairs={{0,8},{4,12},{8,0},{12,4},{16,24},{20,28},{24,16},{28,20},{1,9},{5... | collective-permute-start | bytes 2949128 | tf_op jit(solution)/shard_map/ppermute | solution.py:346
  192.5 21.3 %all-to-all-start.1 = ((bf16[8,2,144,192]{3,2,1,0:T(8,128)(2,1)}), bf16[8,2,144,192]{3,2,1,0:T(8,128)(2,1)}, u32[]{:S(2)}, u32[]{:S(2)}) async-start(bf16[8,2,144,192]{3,2,1,0:T(8,128)(2,1)} %attend.1), calls=%async_computation.1 | async-start | bytes 2359296 | tf_op jit(solution)/shard_map/all_to_all | solution.py:374
  238.0 28.3 %collective-permute-start.21 = (bf16[4,64,1536]{2,1,0:T(8,128)(2,1)S(1)}, bf16[4,64,1536]{2,1,0:T(8,128)(2,1)S(1)}, u32[]{:S(2)}, u32[]{:S(2)}) collective-permute-start(bf16[4,64,1536]{2,1,0:T(8,128)(2,1)S(1)} %pad_maximum_fusion.23), channel_id=1, source_target_pairs={{0,16},{4,20},{8,24},{12,28},{16,0},{20,4},{24,8},{28,12},{1,17},{... | collective-permute-start | bytes 2359304 | tf_op jit(solution)/shard_map/ppermute | solution.py:346
  250.7 21.6 %collective-permute-start.25 = (bf16[4,80,1536]{2,1,0:T(8,128)(2,1)S(1)}, bf16[4,80,1536]{2,1,0:T(8,128)(2,1)S(1)}, u32[]{:S(2)}, u32[]{:S(2)}) collective-permute-start(bf16[4,80,1536]{2,1,0:T(8,128)(2,1)S(1)} %pad_maximum_fusion.19), channel_id=1, source_target_pairs={{0,8},{4,12},{8,0},{12,4},{16,24},{20,28},{24,16},{28,20},{1,9},{5... | collective-permute-start | bytes 2949128 | tf_op jit(solution)/shard_map/ppermute | solution.py:346
  257.0 25.0 %collective-permute-start.27 = (bf16[8,80,1536]{2,1,0:T(8,128)(2,1)}, bf16[8,80,1536]{2,1,0:T(8,128)(2,1)S(1)}, u32[]{:S(2)}, u32[]{:S(2)}) collective-permute-start(bf16[8,80,1536]{2,1,0:T(8,128)(2,1)} %constant_dynamic-update-slice_fusion.10), channel_id=1, source_target_pairs={{0,4},{4,0},{8,12},{12,8},{16,20},{20,16},{24,28},{28,24},{1,5},{5... | collective-permute-start | bytes 5898248 | tf_op jit(solution)/shard_map/ppermute | solution.py:346
  258.1 22.6 %collective-permute-start.23 = (bf16[8,64,1536]{2,1,0:T(8,128)(2,1)S(1)}, bf16[8,64,1536]{2,1,0:T(8,128)(2,1)S(1)}, u32[]{:S(2)}, u32[]{:S(2)}) collective-permute-start(bf16[8,64,1536]{2,1,0:T(8,128)(2,1)S(1)} %copy-done.85), channel_id=1, source_target_pairs={{0,4},{4,0},{8,12},{12,8},{16,20},{20,16},{24,28},{28,24},{1,5},{5... | collective-permute-start | bytes 4718600 | tf_op jit(solution)/shard_map/ppermute | solution.py:346
  266.5 18.2 %collective-permute-start.22 = (bf16[8,64,1536]{2,1,0:T(8,128)(2,1)S(1)}, bf16[8,64,1536]{2,1,0:T(8,128)(2,1)S(1)}, u32[]{:S(2)}, u32[]{:S(2)}) collective-permute-start(bf16[8,64,1536]{2,1,0:T(8,128)(2,1)S(1)} %pad_maximum_fusion.13), channel_id=1, source_target_pairs={{0,4},{4,0},{8,12},{12,8},{16,20},{20,16},{24,28},{28,24},{1,5},{5... | collective-permute-start | bytes 4718600 | tf_op jit(solution)/shard_map/ppermute | solution.py:346
  323.9 20.0 %collective-permute-start.29 = (bf16[4,64,1536]{2,1,0:T(8,128)(2,1)S(1)}, bf16[4,64,1536]{2,1,0:T(8,128)(2,1)S(1)}, u32[]{:S(2)}, u32[]{:S(2)}) collective-permute-start(bf16[4,64,1536]{2,1,0:T(8,128)(2,1)S(1)} %slice.514), channel_id=1, source_target_pairs={{0,16},{4,20},{8,24},{12,28},{16,0},{20,4},{24,8},{28,12},{1,17},{... | collective-permute-start | bytes 2359304 | tf_op jit(solution)/shard_map/ppermute | solution.py:346
  329.7 24.6 %collective-permute-start.32 = (bf16[4,80,1536]{2,1,0:T(8,128)(2,1)S(1)}, bf16[4,80,1536]{2,1,0:T(8,128)(2,1)S(1)}, u32[]{:S(2)}, u32[]{:S(2)}) collective-permute-start(bf16[4,80,1536]{2,1,0:T(8,128)(2,1)S(1)} %slice.521), channel_id=1, source_target_pairs={{0,8},{4,12},{8,0},{12,4},{16,24},{20,28},{24,16},{28,20},{1,9},{5... | collective-permute-start | bytes 2949128 | tf_op jit(solution)/shard_map/ppermute | solution.py:346
  383.7 20.5 %all-to-all-start.3 = ((bf16[8,2,144,192]{3,2,1,0:T(8,128)(2,1)}), bf16[8,2,144,192]{3,2,1,0:T(8,128)(2,1)S(1)}, u32[]{:S(2)}, u32[]{:S(2)}) async-start(bf16[8,2,144,192]{3,2,1,0:T(8,128)(2,1)} %get-tuple-element.191), calls=%async_computation.3 | async-start | bytes 2359296 | tf_op jit(solution)/shard_map/all_to_all | solution.py:374
  387.4 177.1 %all-reduce.5.cloned.1.call-start = ((), (), s32[]{:S(2)}) async-start(), calls=%async_computation.11 | async-start | bytes 9437184 | tf_op jit(solution)/shard_map/psum | solution.py:988
  405.2 46.8 %all-to-all-start.4 = ((bf16[8,192,768]{2,1,0:T(8,128)(2,1)}), bf16[8,192,768]{2,1,0:T(8,128)(2,1)S(1)}, u32[]{:S(2)}, u32[]{:S(2)}) async-start(bf16[8,192,768]{2,1,0:T(8,128)(2,1)} %bitcast.207), calls=%async_computation.4 | async-start | bytes 4718592 | tf_op jit(solution)/shard_map/all_to_all | solution.py:374
  416.2 34.4 %collective-permute-start.35 = (bf16[2,80,1536]{2,1,0:T(8,128)(2,1)S(1)}, bf16[2,80,1536]{2,1,0:T(8,128)(2,1)}, u32[]{:S(2)}, u32[]{:S(2)}) collective-permute-start(bf16[2,80,1536]{2,1,0:T(8,128)(2,1)S(1)} %copy-done.80), channel_id=1, source_target_pairs={{0,16},{4,20},{8,24},{12,28},{16,0},{20,4},{24,8},{28,12},{1,17},{... | collective-permute-start | bytes 1474568 | tf_op jit(solution)/shard_map/ppermute | solution.py:346
  418.2 30.5 %collective-permute-start.34 = (bf16[2,64,1536]{2,1,0:T(8,128)(2,1)S(1)}, bf16[2,64,1536]{2,1,0:T(8,128)(2,1)}, u32[]{:S(2)}, u32[]{:S(2)}) collective-permute-start(bf16[2,64,1536]{2,1,0:T(8,128)(2,1)S(1)} %copy-done.86), channel_id=1, source_target_pairs={{0,8},{4,12},{8,0},{12,4},{16,24},{20,28},{24,16},{28,20},{1,9},{5... | collective-permute-start | bytes 1179656 | tf_op jit(solution)/shard_map/ppermute | solution.py:346
  451.9 57.1 %all-to-all-start.5 = ((bf16[8,192,768]{2,1,0:T(8,128)(2,1)}), bf16[8,192,768]{2,1,0:T(8,128)(2,1)}, u32[]{:S(2)}, u32[]{:S(2)}) async-start(bf16[8,192,768]{2,1,0:T(8,128)(2,1)} %bitcast.206), calls=%async_computation.5 | async-start | bytes 4718592 | tf_op jit(solution)/shard_map/all_to_all | solution.py:374
  456.8 49.7 %collective-permute-start.37 = (bf16[4,80,1536]{2,1,0:T(8,128)(2,1)S(1)}, bf16[4,80,1536]{2,1,0:T(8,128)(2,1)}, u32[]{:S(2)}, u32[]{:S(2)}) collective-permute-start(bf16[4,80,1536]{2,1,0:T(8,128)(2,1)S(1)} %pad_maximum_fusion.20), channel_id=1, source_target_pairs={{0,8},{4,12},{8,0},{12,4},{16,24},{20,28},{24,16},{28,20},{1,9},{5... | collective-permute-start | bytes 2949128 | tf_op jit(solution)/shard_map/ppermute | solution.py:346
  458.8 43.3 %collective-permute-start.36 = (bf16[4,64,1536]{2,1,0:T(8,128)(2,1)}, bf16[4,64,1536]{2,1,0:T(8,128)(2,1)}, u32[]{:S(2)}, u32[]{:S(2)}) collective-permute-start(bf16[4,64,1536]{2,1,0:T(8,128)(2,1)} %pad_maximum_fusion.24), channel_id=1, source_target_pairs={{0,16},{4,20},{8,24},{12,28},{16,0},{20,4},{24,8},{28,12},{1,17},{... | collective-permute-start | bytes 2359304 | tf_op jit(solution)/shard_map/ppermute | solution.py:346
  509.1 79.0 %collective-permute-start.40 = (bf16[8,80,1536]{2,1,0:T(8,128)(2,1)}, bf16[8,80,1536]{2,1,0:T(8,128)(2,1)}, u32[]{:S(2)}, u32[]{:S(2)}) collective-permute-start(bf16[8,80,1536]{2,1,0:T(8,128)(2,1)} %pad_maximum_fusion.11), channel_id=1, source_target_pairs={{0,4},{4,0},{8,12},{12,8},{16,20},{20,16},{24,28},{28,24},{1,5},{5... | collective-permute-start | bytes 5898248 | tf_op jit(solution)/shard_map/ppermute | solution.py:346
  509.1 74.6 %collective-permute-start.39 = (bf16[8,64,1536]{2,1,0:T(8,128)(2,1)}, bf16[8,64,1536]{2,1,0:T(8,128)(2,1)}, u32[]{:S(2)}, u32[]{:S(2)}) collective-permute-start(bf16[8,64,1536]{2,1,0:T(8,128)(2,1)} %pad_maximum_fusion.14), channel_id=1, source_target_pairs={{0,4},{4,0},{8,12},{12,8},{16,20},{20,16},{24,28},{28,24},{1,5},{5... | collective-permute-start | bytes 4718600 | tf_op jit(solution)/shard_map/ppermute | solution.py:346
  514.2 84.3 %collective-permute-start.42 = (bf16[8,80,1536]{2,1,0:T(8,128)(2,1)}, bf16[8,80,1536]{2,1,0:T(8,128)(2,1)}, u32[]{:S(2)}, u32[]{:S(2)}) collective-permute-start(bf16[8,80,1536]{2,1,0:T(8,128)(2,1)} %get-tuple-element.476), channel_id=1, source_target_pairs={{0,4},{4,0},{8,12},{12,8},{16,20},{20,16},{24,28},{28,24},{1,5},{5... | collective-permute-start | bytes 5898248 | tf_op jit(solution)/shard_map/ppermute | solution.py:346
  516.1 82.4 %collective-permute-start.41 = (bf16[8,64,1536]{2,1,0:T(8,128)(2,1)}, bf16[8,64,1536]{2,1,0:T(8,128)(2,1)}, u32[]{:S(2)}, u32[]{:S(2)}) collective-permute-start(bf16[8,64,1536]{2,1,0:T(8,128)(2,1)} %get-tuple-element.482), channel_id=1, source_target_pairs={{0,4},{4,0},{8,12},{12,8},{16,20},{20,16},{24,28},{28,24},{1,5},{5... | collective-permute-start | bytes 4718600 | tf_op jit(solution)/shard_map/ppermute | solution.py:346
  520.5 73.7 %all-to-all-start.6 = ((bf16[8,192,576]{2,1,0:T(8,128)(2,1)}), bf16[8,192,576]{2,1,0:T(8,128)(2,1)}, u32[]{:S(2)}, u32[]{:S(2)}) async-start(bf16[8,192,576]{2,1,0:T(8,128)(2,1)} %bitcast.180), calls=%async_computation.6 | async-start | bytes 3932160 | tf_op jit(solution)/shard_map/all_to_all | solution.py:374
  566.1 32.5 %collective-permute-start.38 = (bf16[8,96,768]{2,1,0:T(8,128)(2,1)}, bf16[8,96,768]{2,1,0:T(8,128)(2,1)}, u32[]{:S(2)}, u32[]{:S(2)}) collective-permute-start(bf16[8,96,768]{2,1,0:T(8,128)(2,1)} %get-tuple-element.213), channel_id=1, source_target_pairs={{0,1},{3,2},{4,5},{7,6},{8,9},{11,10},{12,13},{15,14},{16,17},{19,... | collective-permute-start | bytes 3538952 | tf_op jit(solution)/shard_map/ppermute | solution.py:420
  583.7 36.3 %collective-permute-start.44 = (bf16[8,96,768]{2,1,0:T(8,128)(2,1)}, bf16[8,96,768]{2,1,0:T(8,128)(2,1)}, u32[]{:S(2)}, u32[]{:S(2)}) collective-permute-start(bf16[8,96,768]{2,1,0:T(8,128)(2,1)} %get-tuple-element.224), channel_id=1, source_target_pairs={{0,1},{3,2},{4,5},{7,6},{8,9},{11,10},{12,13},{15,14},{16,17},{19,... | collective-permute-start | bytes 3538952 | tf_op jit(solution)/shard_map/ppermute | solution.py:420
  588.0 70.5 %collective-permute-start.49 = (bf16[8,96,768]{2,1,0:T(8,128)(2,1)}, bf16[8,96,768]{2,1,0:T(8,128)(2,1)}, u32[]{:S(2)}, u32[]{:S(2)}) collective-permute-start(bf16[8,96,768]{2,1,0:T(8,128)(2,1)} %get-tuple-element.233), channel_id=1, source_target_pairs={{0,1},{3,2},{4,5},{7,6},{8,9},{11,10},{12,13},{15,14},{16,17},{19,... | collective-permute-start | bytes 3538952 | tf_op jit(solution)/shard_map/ppermute | solution.py:420
  594.2 30.1 %all-to-all-start.7 = ((bf16[8,192,576]{2,1,0:T(8,128)(2,1)}), bf16[8,192,576]{2,1,0:T(8,128)(2,1)}, u32[]{:S(2)}, u32[]{:S(2)}) async-start(bf16[8,192,576]{2,1,0:T(8,128)(2,1)} %bitcast.179), calls=%async_computation.7 | async-start | bytes 3932160 | tf_op jit(solution)/shard_map/all_to_all | solution.py:374
  602.7 41.3 %collective-permute-start.46 = (bf16[4,80,1536]{2,1,0:T(8,128)(2,1)}, bf16[4,80,1536]{2,1,0:T(8,128)(2,1)}, u32[]{:S(2)}, u32[]{:S(2)}) collective-permute-start(bf16[4,80,1536]{2,1,0:T(8,128)(2,1)} %get-tuple-element.496), channel_id=1, source_target_pairs={{0,8},{4,12},{8,0},{12,4},{16,24},{20,28},{24,16},{28,20},{1,9},{5... | collective-permute-start | bytes 2949128 | tf_op jit(solution)/shard_map/ppermute | solution.py:346
  607.5 36.5 %collective-permute-start.43 = (bf16[8,96,768]{2,1,0:T(8,128)(2,1)}, bf16[8,96,768]{2,1,0:T(8,128)(2,1)}, u32[]{:S(2)}, u32[]{:S(2)}) collective-permute-start(bf16[8,96,768]{2,1,0:T(8,128)(2,1)} %add_convert_fusion.13), channel_id=1, source_target_pairs={{1,2},{2,1},{5,6},{6,5},{9,10},{10,9},{13,14},{14,13},{17,18},{18,... | collective-permute-start | bytes 3538952 | tf_op jit(solution)/shard_map/ppermute | solution.py:420
  612.4 27.3 %collective-permute-start.45 = (bf16[4,64,1536]{2,1,0:T(8,128)(2,1)}, bf16[4,64,1536]{2,1,0:T(8,128)(2,1)}, u32[]{:S(2)}, u32[]{:S(2)}) collective-permute-start(bf16[4,64,1536]{2,1,0:T(8,128)(2,1)} %get-tuple-element.500), channel_id=1, source_target_pairs={{0,16},{4,20},{8,24},{12,28},{16,0},{20,4},{24,8},{28,12},{1,17},{... | collective-permute-start | bytes 2359304 | tf_op jit(solution)/shard_map/ppermute | solution.py:346
  645.5 19.6 %collective-permute-start.51 = (bf16[2,80,1536]{2,1,0:T(8,128)(2,1)S(1)}, bf16[2,80,1536]{2,1,0:T(8,128)(2,1)S(1)}, u32[]{:S(2)}, u32[]{:S(2)}) collective-permute-start(bf16[2,80,1536]{2,1,0:T(8,128)(2,1)S(1)} %get-tuple-element.515), channel_id=1, source_target_pairs={{0,16},{4,20},{8,24},{12,28},{16,0},{20,4},{24,8},{28,12},{1,17},{... | collective-permute-start | bytes 1474568 | tf_op jit(solution)/shard_map/ppermute | solution.py:346
  651.8 29.3 %collective-permute-start.47 = (bf16[8,96,768]{2,1,0:T(8,128)(2,1)S(1)}, bf16[8,96,768]{2,1,0:T(8,128)(2,1)S(1)}, u32[]{:S(2)}, u32[]{:S(2)}) collective-permute-start(bf16[8,96,768]{2,1,0:T(8,128)(2,1)S(1)} %add_convert_fusion.12.refs_0_), channel_id=1, source_target_pairs={{1,0},{2,3},{5,4},{6,7},{9,8},{10,11},{13,12},{14,15},{17,16},{18,... | collective-permute-start | bytes 3538952 | tf_op jit(solution)/shard_map/ppermute | solution.py:420
  658.6 31.7 %collective-permute-start.54 = (bf16[8,96,768]{2,1,0:T(8,128)(2,1)S(1)}, bf16[8,96,768]{2,1,0:T(8,128)(2,1)S(1)}, u32[]{:S(2)}, u32[]{:S(2)}) collective-permute-start(bf16[8,96,768]{2,1,0:T(8,128)(2,1)S(1)} %copy-done.14), channel_id=1, source_target_pairs={{0,1},{3,2},{4,5},{7,6},{8,9},{11,10},{12,13},{15,14},{16,17},{19,... | collective-permute-start | bytes 3538952 | tf_op jit(solution)/shard_map/ppermute | solution.py:420
  682.8 35.4 %collective-permute-start.56 = (bf16[8,80,1536]{2,1,0:T(8,128)(2,1)S(1)}, bf16[8,80,1536]{2,1,0:T(8,128)(2,1)S(1)}, u32[]{:S(2)}, u32[]{:S(2)}) collective-permute-start(bf16[8,80,1536]{2,1,0:T(8,128)(2,1)S(1)} %get-tuple-element.474), channel_id=1, source_target_pairs={{0,4},{4,0},{8,12},{12,8},{16,20},{20,16},{24,28},{28,24},{1,5},{5... | collective-permute-start | bytes 5898248 | tf_op jit(solution)/shard_map/ppermute | solution.py:346
  686.0 32.2 %collective-permute-start.55 = (bf16[8,64,1536]{2,1,0:T(8,128)(2,1)S(1)}, bf16[8,64,1536]{2,1,0:T(8,128)(2,1)S(1)}, u32[]{:S(2)}, u32[]{:S(2)}) collective-permute-start(bf16[8,64,1536]{2,1,0:T(8,128)(2,1)S(1)} %get-tuple-element.480), channel_id=1, source_target_pairs={{0,4},{4,0},{8,12},{12,8},{16,20},{20,16},{24,28},{28,24},{1,5},{5... | collective-permute-start | bytes 4718600 | tf_op jit(solution)/shard_map/ppermute | solution.py:346
  687.4 30.9 %collective-permute-start.52 = (bf16[8,96,768]{2,1,0:T(8,128)(2,1)S(1)}, bf16[8,96,768]{2,1,0:T(8,128)(2,1)S(1)}, u32[]{:S(2)}, u32[]{:S(2)}) collective-permute-start(bf16[8,96,768]{2,1,0:T(8,128)(2,1)S(1)} %add_convert_fusion.10.refs_2_), channel_id=1, source_target_pairs={{1,0},{2,3},{5,4},{6,7},{9,8},{10,11},{13,12},{14,15},{17,16},{18,... | collective-permute-start | bytes 3538952 | tf_op jit(solution)/shard_map/ppermute | solution.py:420
  690.3 35.2 %collective-permute-start.59 = (bf16[2,192,1536]{2,1,0:T(8,128)(2,1)S(1)}, bf16[2,192,1536]{2,1,0:T(8,128)(2,1)S(1)}, u32[]{:S(2)}, u32[]{:S(2)}) collective-permute-start(bf16[2,192,1536]{2,1,0:T(8,128)(2,1)S(1)} %pad_maximum_fusion.16), channel_id=1, source_target_pairs={{0,1},{3,2},{4,5},{7,6},{8,9},{11,10},{12,13},{15,14},{16,17},{19,... | collective-permute-start | bytes 3538952 | tf_op jit(solution)/shard_map/ppermute | solution.py:420
  719.4 23.6 %collective-permute-start.61 = (bf16[4,80,1536]{2,1,0:T(8,128)(2,1)S(1)}, bf16[4,80,1536]{2,1,0:T(8,128)(2,1)S(1)}, u32[]{:S(2)}, u32[]{:S(2)}) collective-permute-start(bf16[4,80,1536]{2,1,0:T(8,128)(2,1)S(1)} %get-tuple-element.494), channel_id=1, source_target_pairs={{0,8},{4,12},{8,0},{12,4},{16,24},{20,28},{24,16},{28,20},{1,9},{5... | collective-permute-start | bytes 2949128 | tf_op jit(solution)/shard_map/ppermute | solution.py:346
  720.6 19.1 %collective-permute-start.60 = (bf16[4,64,1536]{2,1,0:T(8,128)(2,1)S(1)}, bf16[4,64,1536]{2,1,0:T(8,128)(2,1)S(1)}, u32[]{:S(2)}, u32[]{:S(2)}) collective-permute-start(bf16[4,64,1536]{2,1,0:T(8,128)(2,1)S(1)} %get-tuple-element.498), channel_id=1, source_target_pairs={{0,16},{4,20},{8,24},{12,28},{16,0},{20,4},{24,8},{28,12},{1,17},{... | collective-permute-start | bytes 2359304 | tf_op jit(solution)/shard_map/ppermute | solution.py:346
  721.6 21.5 %collective-permute-start.58 = (bf16[8,96,768]{2,1,0:T(8,128)(2,1)S(1)}, bf16[8,96,768]{2,1,0:T(8,128)(2,1)S(1)}, u32[]{:S(2)}, u32[]{:S(2)}) collective-permute-start(bf16[8,96,768]{2,1,0:T(8,128)(2,1)S(1)} %add_convert_fusion.7), channel_id=1, source_target_pairs={{1,2},{2,1},{5,6},{6,5},{9,10},{10,9},{13,14},{14,13},{17,18},{18,... | collective-permute-start | bytes 3538952 | tf_op jit(solution)/shard_map/ppermute | solution.py:420
  722.8 29.1 %collective-permute-start.57 = (bf16[8,96,768]{2,1,0:T(8,128)(2,1)S(1)}, bf16[8,96,768]{2,1,0:T(8,128)(2,1)S(1)}, u32[]{:S(2)}, u32[]{:S(2)}) collective-permute-start(bf16[8,96,768]{2,1,0:T(8,128)(2,1)S(1)} %add_convert_fusion.8.refs_4_), channel_id=1, source_target_pairs={{1,0},{2,3},{5,4},{6,7},{9,8},{10,11},{13,12},{14,15},{17,16},{18,... | collective-permute-start | bytes 3538952 | tf_op jit(solution)/shard_map/ppermute | solution.py:420
  725.5 33.5 %collective-permute-start.64 = (bf16[8,96,576]{2,1,0:T(8,128)(2,1)S(1)}, bf16[8,96,576]{2,1,0:T(8,128)(2,1)S(1)}, u32[]{:S(2)}, u32[]{:S(2)}) collective-permute-start(bf16[8,96,576]{2,1,0:T(8,128)(2,1)S(1)} %copy-done.36), channel_id=1, source_target_pairs={{0,1},{3,2},{4,5},{7,6},{8,9},{11,10},{12,13},{15,14},{16,17},{19,... | collective-permute-start | bytes 2654216 | tf_op jit(solution)/shard_map/ppermute | solution.py:420
  752.8 19.0 %collective-permute-start.66 = (bf16[2,80,1536]{2,1,0:T(8,128)(2,1)S(1)}, bf16[2,80,1536]{2,1,0:T(8,128)(2,1)S(1)}, u32[]{:S(2)}, u32[]{:S(2)}) collective-permute-start(bf16[2,80,1536]{2,1,0:T(8,128)(2,1)S(1)} %get-tuple-element.513), channel_id=1, source_target_pairs={{0,16},{4,20},{8,24},{12,28},{16,0},{20,4},{24,8},{28,12},{1,17},{... | collective-permute-start | bytes 1474568 | tf_op jit(solution)/shard_map/ppermute | solution.py:346
  755.7 28.0 %collective-permute-start.62 = (bf16[8,96,768]{2,1,0:T(8,128)(2,1)S(1)}, bf16[8,96,768]{2,1,0:T(8,128)(2,1)S(1)}, u32[]{:S(2)}, u32[]{:S(2)}) collective-permute-start(bf16[8,96,768]{2,1,0:T(8,128)(2,1)S(1)} %add_convert_fusion.6.refs_6_), channel_id=1, source_target_pairs={{1,0},{2,3},{5,4},{6,7},{9,8},{10,11},{13,12},{14,15},{17,16},{18,... | collective-permute-start | bytes 3538952 | tf_op jit(solution)/shard_map/ppermute | solution.py:420
  759.0 60.8 %collective-permute-start.69 = (bf16[8,96,576]{2,1,0:T(8,128)(2,1)}, bf16[8,96,576]{2,1,0:T(8,128)(2,1)}, u32[]{:S(2)}, u32[]{:S(2)}) collective-permute-start(bf16[8,96,576]{2,1,0:T(8,128)(2,1)} %get-tuple-element.280), channel_id=1, source_target_pairs={{0,1},{3,2},{4,5},{7,6},{8,9},{11,10},{12,13},{15,14},{16,17},{19,... | collective-permute-start | bytes 2654216 | tf_op jit(solution)/shard_map/ppermute | solution.py:420
  766.6 80.8 %collective-permute-start.75 = (bf16[8,96,576]{2,1,0:T(8,128)(2,1)}, bf16[8,96,576]{2,1,0:T(8,128)(2,1)}, u32[]{:S(2)}, u32[]{:S(2)}) collective-permute-start(bf16[8,96,576]{2,1,0:T(8,128)(2,1)} %get-tuple-element.286), channel_id=1, source_target_pairs={{0,1},{3,2},{4,5},{7,6},{8,9},{11,10},{12,13},{15,14},{16,17},{19,... | collective-permute-start | bytes 2654216 | tf_op jit(solution)/shard_map/ppermute | solution.py:420
  785.7 25.8 %collective-permute-start.70 = (bf16[43008]{0:T(1024)(128)(2,1)S(1)}, bf16[43008]{0:T(1024)(128)(2,1)}, u32[]{:S(2)}, u32[]{:S(2)}) collective-permute-start(bf16[43008]{0:T(1024)(128)(2,1)S(1)} %concatenate.163), channel_id=1, source_target_pairs={{0,1},{1,2},{2,3},{3,0},{4,5},{5,6},{6,7},{7,4},{8,9},{9,10},{10,1... | collective-permute-start | bytes 258056 | tf_op jit(solution)/shard_map/ppermute | solution.py:387
  785.7 29.0 %collective-permute-start.71 = (bf16[43008]{0:T(1024)(128)(2,1)S(1)}, bf16[43008]{0:T(1024)(128)(2,1)S(1)}, u32[]{:S(2)}, u32[]{:S(2)}) collective-permute-start(bf16[43008]{0:T(1024)(128)(2,1)S(1)} %concatenate.163), channel_id=1, source_target_pairs={{0,2},{1,3},{2,0},{3,1},{4,6},{5,7},{6,4},{7,5},{8,10},{9,11},{10,... | collective-permute-start | bytes 258056 | tf_op jit(solution)/shard_map/ppermute | solution.py:387
  787.8 27.8 %collective-permute-start.72 = (bf16[43008]{0:T(1024)(128)(2,1)S(1)}, bf16[43008]{0:T(1024)(128)(2,1)S(1)}, u32[]{:S(2)}, u32[]{:S(2)}) collective-permute-start(bf16[43008]{0:T(1024)(128)(2,1)S(1)} %concatenate.163), channel_id=1, source_target_pairs={{0,3},{1,0},{2,1},{3,2},{4,7},{5,4},{6,5},{7,6},{8,11},{9,8},{10,9... | collective-permute-start | bytes 258056 | tf_op jit(solution)/shard_map/ppermute | solution.py:387
  811.5 61.8 %collective-permute-start.79 = (bf16[8,96,576]{2,1,0:T(8,128)(2,1)}, bf16[8,96,576]{2,1,0:T(8,128)(2,1)}, u32[]{:S(2)}, u32[]{:S(2)}) collective-permute-start(bf16[8,96,576]{2,1,0:T(8,128)(2,1)} %get-tuple-element.291), channel_id=1, source_target_pairs={{0,1},{3,2},{4,5},{7,6},{8,9},{11,10},{12,13},{15,14},{16,17},{19,... | collective-permute-start | bytes 2654216 | tf_op jit(solution)/shard_map/ppermute | solution.py:420
  815.6 23.3 %collective-permute-start.67 = (bf16[2,192,1536]{2,1,0:T(8,128)(2,1)S(1)}, bf16[2,192,1536]{2,1,0:T(8,128)(2,1)S(1)}, u32[]{:S(2)}, u32[]{:S(2)}) collective-permute-start(bf16[2,192,1536]{2,1,0:T(8,128)(2,1)S(1)} %add_convert_fusion.4), channel_id=1, source_target_pairs={{1,0},{2,3},{5,4},{6,7},{9,8},{10,11},{13,12},{14,15},{17,16},{18,... | collective-permute-start | bytes 3538952 | tf_op jit(solution)/shard_map/ppermute | solution.py:420
  842.3 18.0 %collective-permute-start.73 = (bf16[8,96,576]{2,1,0:T(8,128)(2,1)S(1)}, bf16[8,96,576]{2,1,0:T(8,128)(2,1)S(1)}, u32[]{:S(2)}, u32[]{:S(2)}) collective-permute-start(bf16[8,96,576]{2,1,0:T(8,128)(2,1)S(1)} %add_convert_fusion.21.refs_0_), channel_id=1, source_target_pairs={{1,0},{2,3},{5,4},{6,7},{9,8},{10,11},{13,12},{14,15},{17,16},{18,... | collective-permute-start | bytes 2654216 | tf_op jit(solution)/shard_map/ppermute | solution.py:420
  894.5 26.1 %collective-permute-start.81 = (bf16[8,96,576]{2,1,0:T(8,128)(2,1)S(1)}, bf16[8,96,576]{2,1,0:T(8,128)(2,1)S(1)}, u32[]{:S(2)}, u32[]{:S(2)}) collective-permute-start(bf16[8,96,576]{2,1,0:T(8,128)(2,1)S(1)} %add_convert_fusion.17.refs_4_), channel_id=1, source_target_pairs={{1,0},{2,3},{5,4},{6,7},{9,8},{10,11},{13,12},{14,15},{17,16},{18,... | collective-permute-start | bytes 2654216 | tf_op jit(solution)/shard_map/ppermute | solution.py:420
  932.1 26.3 %collective-permute-start.84 = (bf16[8,96,576]{2,1,0:T(8,128)(2,1)S(1)}, bf16[8,96,576]{2,1,0:T(8,128)(2,1)}, u32[]{:S(2)}, u32[]{:S(2)}) collective-permute-start(bf16[8,96,576]{2,1,0:T(8,128)(2,1)S(1)} %add_convert_fusion.15.refs_6_), channel_id=1, source_target_pairs={{1,0},{2,3},{5,4},{6,7},{9,8},{10,11},{13,12},{14,15},{17,16},{18,... | collective-permute-start | bytes 2654216 | tf_op jit(solution)/shard_map/ppermute | solution.py:420
  (173 other events, 2320.3 us)
Sparse Core Ops, SparseCore 0:
  18.0 72.9 all-gather.6
  165.1 86.6 all-gather.8
  393.6 170.8 all-reduce.4

commit v3 on v2

--- a/solution.py
+++ b/solution.py
@@ -393,9 +393,6 @@
     return lax.optimization_barrier((array, *others))[0]
 
 
-HOPS = ([(0, 1), (3, 2)], [(1, 2), (2, 1)], [(1, 0), (2, 3)])
-
-
 def together(*groups):
     items = [item for group in groups for item in group]
     items = list(lax.optimization_barrier(tuple(items)))
@@ -406,26 +403,16 @@
     return found
 
 
-class ReplicaSum:
-    def __init__(self):
-        self.entries = []
-
-    def add(self, array):
-        self.entries.append([array, None, 0])
-        return self.entries[-1]
-
-    def step(self, *groups):
-        moving = [entry for entry in self.entries if entry[2] < 3]
-        for entry in moving:
-            entry[1] = lax.ppermute(entry[0], "rep", HOPS[entry[2]])
-        pairs = [item for entry in moving for item in entry[:2]]
-        pairs, *groups = together(pairs, *groups)
-        for at, entry in enumerate(moving):
-            entry[0], entry[1] = pairs[2 * at : 2 * at + 2]
-            if entry[2] < 2:
-                entry[0] = (entry[0].astype(WIDE) + entry[1].astype(WIDE)).astype(LOWER)
-            entry[2] += 1
-        return groups
+def once(trips, stage, *inputs):
+    shapes = jax.eval_shape(stage, *inputs)
+    zeros = jax.tree.map(lambda item: jnp.zeros(item.shape, item.dtype), shapes)
+
+    def body(index, state):
+        held = jax.tree.leaves(inputs)
+        held = lax.optimization_barrier((index, *held))[1:]
+        return stage(*jax.tree.unflatten(jax.tree.structure(inputs), held))
+
+    return lax.fori_loop(0, trips, body, zeros)
 
 
 def cost(flops, moved, transcendentals=0):
@@ -574,7 +561,10 @@
     return raised / jnp.sum(raised, axis=-1, keepdims=True)
 
 
-def attend_kernel(size, length, me_ref, image_ref, text_ref, out_ref):
+def attend_kernel(
+    size, length, me_ref, image_ref, text_ref, out_ref, image_out_ref, text_out_ref
+):
+    split_at = image_ref.shape[2]
     for slot in range(image_ref.shape[1]):
         joint = jnp.concatenate([image_ref[0, slot], text_ref[0, slot]], axis=0)
         width = joint.shape[1] // 3
@@ -585,7 +575,10 @@
             value = joint[:, 2 * width + at : 2 * width + at + size]
             probs = head_softmax(query, key, length)
             found.append(contract(probs.astype(LOWER), value, ((1,), (0,))).astype(LOWER))
-        out_ref[0, slot] = jnp.concatenate(found, axis=1)
+        whole = jnp.concatenate(found, axis=1)
+        out_ref[0, slot] = whole
+        image_out_ref[0, slot] = whole[:split_at]
+        text_out_ref[0, slot] = whole[split_at:]
 
 
 def attend_back_kernel(
@@ -636,7 +629,10 @@
     share = columns // 3
     return pl.pallas_call(
         lambda *refs: attend_kernel(size, length, *refs),
-        out_shape=jax.ShapeDtypeStruct((devices, slots, rows + more, share), LOWER),
+        out_shape=[
+            jax.ShapeDtypeStruct((devices, slots, item, share), LOWER)
+            for item in (rows + more, rows, more)
+        ],
         grid_spec=pltpu.PrefetchScalarGridSpec(
             num_scalar_prefetch=1,
             grid=(devices,),
@@ -644,7 +640,11 @@
                 pl.BlockSpec((1, slots, rows, columns), image_place),
                 pl.BlockSpec((1, slots, more, columns), text_place),
             ],
-            out_specs=pl.BlockSpec((1, slots, rows + more, share), joint_place),
+            out_specs=[
+                pl.BlockSpec((1, slots, rows + more, share), joint_place),
+                pl.BlockSpec((1, slots, rows, share), image_place),
+                pl.BlockSpec((1, slots, more, share), text_place),
+            ],
         ),
         cost_estimate=cost(
             4 * count * (rows + more) ** 2 * share,
@@ -900,11 +900,9 @@
     packed_attend = pack(attend_weight, place_array, REPLICAS, 3, (0, 1))
     packed_expand = pack(expand_weight, place_array, REPLICAS, 1, (0, 1))
     output_low = output_weight.astype(LOWER)
-    small = after(small, packed_attend, packed_expand, output_low)
     small_all = lax.all_gather(small, "shard", axis=0, tiled=False)
-    cond_cols = lax.dynamic_slice_in_dim(
-        pick(small_all[:, :, :width], [me ^ item for item in range(GROUP)]), me * share, share, 2
-    ).reshape(GROUP * slots, share)
+    cond_group = small_all[:, :, :width].reshape(GROUP * slots, width)
+    cond_cols = lax.dynamic_slice_in_dim(cond_group, me * share, share, 1)
 
     def whole_bias(start, length):
         piece = small_all[:, :, start : start + length]
@@ -920,17 +918,17 @@
 
     adaptive_local = adaptive_weight.astype(LOWER)
     partial_terms = project("gd,sde->gse", cond_cols, adaptive_local)
-    quarter = spread(packed_attend)
+    quarter = spread(after(packed_attend, small_all))
     partial_terms = after(partial_terms, quarter).reshape(GROUP, slots, 2, 6 * width)
-    modulation = adaptive_bias_full[None] + partial_terms[0]
-    for item in range(1, GROUP):
-        modulation = modulation + swap(partial_terms[item], item)
+    turns = ring(quarter)
+    arrived = spread(partial_terms)
+    (arrived,), turns[:2] = together([arrived], turns[:2])
+    modulation = jnp.sum(arrived, axis=0) + adaptive_bias_full[None]
     parts = [
         [modulation[:, which, piece * width : (piece + 1) * width] for piece in range(6)]
         for which in range(2)
     ]
 
-    turns = ring(quarter)
     output_full = lax.all_gather(output_low, "shard", axis=0, tiled=False)
     quarter = spread(after(packed_expand, turns[1]))
     quarters = lax.all_gather(after(quarter, output_full, turns[3]), "rep", axis=0, tiled=False)
@@ -963,8 +961,9 @@
         d_seconds.append(grow(after(d_second, *fronts), orders[which][0]))
     triples, d_seconds = together(triples, d_seconds)
     d_seconds = [grow(d_seconds[which], orders[which][1]) for which in range(2)]
-    attended = attend_forward(triples[0], triples[1], me_array, size, rows + extra)
-    joint = spread(after(attended, *d_seconds))
+    attended, *pieces = attend_forward(triples[0], triples[1], me_array, size, rows + extra)
+    joint = spread(attended)
+    (joint, reduce_own), d_seconds = together([joint, reduce_own], d_seconds)
     d_seconds = [flat(grow(d_seconds[which], orders[which][2])) for which in range(2)]
 
     branch_one, middle_one, hidden_one, branch_two, middle_two, hidden_two = middle_stage(
@@ -975,67 +974,6 @@
     feeds = []
     for which, hidden in enumerate((hidden_one, hidden_two)):
         feeds.append(flat(collect(hidden, orders[which])))
-
-    befores = []
-    actives = []
-    reduce_grads = []
-    for which in range(2):
-        before = project("rd,df->rf", feeds[which], expand_own[which]) + expand_bias_own[which]
-        befores.append(before)
-        active = smooth_gelu(before).astype(LOWER)
-        actives.append(active)
-        reduce_grads.append(project("rf,rd->fd", active, d_seconds[which]).astype(LOWER))
-    reduce_totals = lax.psum(tuple(reduce_grads), "rep")
-
-    pairs = []
-    expand_grads = []
-    expand_bias_grads = []
-    reduce_bias_grads = []
-    for which in range(2):
-        d_active = project("rd,fd->rf", d_seconds[which], reduce_own[which])
-        d_before = jax.vjp(smooth_gelu, befores[which])[1](d_active)[0].astype(LOWER)
-        d_hidden = project("rf,df->rd", d_before, expand_own[which]).astype(LOWER)
-        d_hidden = d_hidden.reshape(GROUP * slots, spans[which], width)
-        own, other = scatter_halves(d_hidden, orders[which])
-        pairs.append((own, other, middles[which], branches[which], pulls[which]))
-        expand_grads.append(project("rd,rf->df", feeds[which], d_before).astype(LOWER))
-        expand_bias_grads.append(jnp.sum(d_before, axis=0, dtype=WIDE))
-        d_cols = lax.dynamic_slice_in_dim(d_seconds[which], me * share, share, 1)
-        reduce_bias_grads.append(jnp.sum(d_cols, axis=0, dtype=WIDE))
-    live = jnp.broadcast_to(alive, (slots, 1, width))
-    d_middle_one, d_branch_one, sums_one, d_middle_two, d_branch_two, sums_two, d_joint = (
-        back_stage(output_full, modulation, live, pairs)
-    )
-    d_middles = (d_middle_one, d_middle_two)
-    d_branches = (d_branch_one, d_branch_two)
-    sums = (sums_one, sums_two)
-    d_attended = spread(d_joint)
-    d_attended, grown, expand_grads = together([d_attended], list(d_branches), expand_grads)
-    (d_attended,) = d_attended
-    expand_grads = [item.reshape(GROUP, share, 4 * share) for item in expand_grads]
-    grown = [grow(grown[which], orders[which][0]) for which in range(2)]
-    d_triples = attend_backward(
-        triples[0], triples[1], d_attended, me_array, size, rows + extra
-    )
-    expand_one = spread(expand_grads[0])
-    (expand_one,), d_triples, grown = together([expand_one], list(d_triples), grown)
-
-    d_triples = [flat(item) for item in d_triples]
-    attend_grads = [
-        project("rd,re->de", fronts[which], d_triples[which]).astype(LOWER) for which in range(2)
-    ]
-    expand_two = spread(expand_grads[1])
-    grown = [grow(grown[which], orders[which][1]) for which in range(2)]
-    d_fronts = [
-        project("re,de->rd", d_triples[which], attend_own[which])
-        .astype(LOWER)
-        .reshape(GROUP * slots, spans[which], width)
-        for which in range(2)
-    ]
-    (expand_two,), attend_grads, grown, d_fronts = together(
-        [expand_two], attend_grads, grown, d_fronts
-    )
-    attend_grads = [item.reshape(GROUP, share, 3 * share) for item in attend_grads]
 
     def halved(arrays, stage):
         found = []
@@ -1054,119 +992,190 @@
         middle = array.shape[1] // 2
         return array[:, :middle], array[:, middle:]
 
-    tree = ReplicaSum()
-    handles = []
-    reduce_totals, (expand_one, expand_two) = together(
-        list(reduce_totals), [expand_one, expand_two]
-    )
-    expand_parts = [*halves(expand_one), *halves(expand_two)]
-
-    handles.append(tree.add(expand_parts[0]))
-    grown = [grow(grown[which], orders[which][2]) for which in range(2)]
-    attend_one = spread(attend_grads[0])
-    (attend_one,), grown, pairs = tree.step([attend_one], grown, halved(d_fronts, 0))
-
-    handles.append(tree.add(expand_parts[1]))
-    d_fronts = summed(pairs)
-    attend_two = spread(attend_grads[1])
-    ordered = pick(attended, [me ^ item for item in distances(ORDER_ONE)])
-    output_grads = []
-    output_bias_grads = []
+    def by_device(array, which):
+        return array.reshape(GROUP * slots, spans[which], width)
+
+    def feed_forward(which):
+        before = project("rd,df->rf", feeds[which], expand_own[which]) + expand_bias_own[which]
+        active = smooth_gelu(before).astype(LOWER)
+        d_active = project("rd,fd->rf", d_seconds[which], reduce_own[which])
+        d_before = jax.vjp(smooth_gelu, before)[1](d_active)[0].astype(LOWER)
+        d_hidden = project("rf,df->rd", d_before, expand_own[which]).astype(LOWER)
+        return active, d_before, by_device(d_hidden, which)
+
+    actives = []
+    d_befores = []
+    d_hiddens = []
     for which in range(2):
-        d_branch_all = flat(grown[which])
-        pieces = ordered[:, :, :rows] if which == 0 else ordered[:, :, rows:]
-        if which == 1:
-            turned = [distances(ORDER_ONE).index(item) for item in distances(ORDER_TWO)]
-            pieces = jnp.concatenate([pieces[item : item + 1] for item in turned], axis=0)
-        output_grads.append(project("rd,re->de", flat(pieces), d_branch_all).astype(LOWER))
-        d_cols = lax.dynamic_slice_in_dim(d_branch_all, me * share, share, 1)
-        output_bias_grads.append(jnp.sum(d_cols, axis=0, dtype=WIDE))
-    (attend_two,), pairs, output_grads = tree.step(
-        [attend_two], halved(d_fronts, 1), output_grads
-    )
-
-    handles.append(tree.add(expand_parts[2]))
-    d_fronts = summed(pairs)
-    seconds = [
-        project("rf,fd->rd", actives[which], reduce_own[which])
+        active, d_before, d_hidden = feed_forward(which)
+        actives.append(active)
+        d_befores.append(d_before)
+        d_hiddens.append(d_hidden)
+    d_hiddens, actives, d_befores = together(d_hiddens, actives, d_befores)
+    expand_grads = [
+        project("rd,rf->df", feeds[which], d_befores[which])
         .astype(LOWER)
-        .reshape(GROUP * slots, spans[which], width)
+        .reshape(GROUP, share, 4 * share)
         for which in range(2)
     ]
-    pairs, seconds = tree.step(halved(d_fronts, 2), seconds)
-
-    handles.append(tree.add(expand_parts[3]))
-    d_fronts = summed(pairs, WIDE)
-    input_grads = []
-    front_mods = []
-    for which in range(2):
-        d_stream, d_shift_front, d_scale_front = jax.vjp(
-            modulate, streams[which], parts[which][0], parts[which][1]
-        )[1](d_fronts[which])
-        input_grads.append((d_middles[which] + d_stream).astype(LOWER))
-        front_mods += [d_shift_front, d_scale_front]
-    pairs, front_mods, input_grads = tree.step(halved(seconds, 0), front_mods, input_grads)
-
-    handles.append(tree.add(jnp.stack(output_grads)))
-    (pairs,) = tree.step(halved(summed(pairs), 1))
-
-    attend_parts = [*halves(attend_one), *halves(attend_two)]
-    handles.append(tree.add(attend_parts[0]))
-    (pairs,) = tree.step(halved(summed(pairs), 2))
-
-    seconds = summed(pairs, WIDE)
-    outputs = []
-    d_mods = []
-    attend_bias_grads = []
-    for which in range(2):
-        second = seconds[which] + reduce_bias_full[which]
-        gate = parts[which][5][:, None, :]
-        outputs.append(((middles[which] + gate * second) * alive).astype(LOWER))
-        gate_feed = jnp.sum(cotangents[which] * second, axis=1)
-        column_sums = jnp.sum(d_triples[which], axis=0, dtype=WIDE)
-        attend_bias_grads.append(
-            jnp.concatenate([column_sums[:share], column_sums[2 * share :]]).astype(LOWER)
-        )
-        d_mods.append(
-            jnp.concatenate(
+    reduce_grads = [
+        project("rf,rd->fd", actives[which], d_seconds[which])
+        .astype(LOWER)
+        .reshape(1, 4 * share, width)
+        for which in range(2)
+    ]
+    pairs, expand_grads, reduce_grads = together(halved(d_hiddens, 0), expand_grads, reduce_grads)
+    early_totals = lax.psum((*expand_grads, *reduce_grads), "rep")
+    trips = jnp.minimum(jnp.abs(counts[0]) + 1, 1)
+
+    def chain(pairs, actives, d_befores):
+        pairs = halved(summed(pairs), 1)
+        pairs = halved(summed(pairs), 2)
+        live = jnp.broadcast_to(alive, (slots, 1, width))
+        d_middle_one, d_branch_one, sums_one, d_middle_two, d_branch_two, sums_two, d_joint = (
+            back_stage(
+                output_full,
+                modulation,
+                live,
                 [
-                    *front_mods[2 * which : 2 * which + 2],
-                    sums[which][:, 0],
-                    sums[which][:, 1],
-                    sums[which][:, 2],
-                    gate_feed,
+                    (*pairs[2 * which : 2 * which + 2], middles[which], branches[which], pulls[which])
+                    for which in range(2)
                 ],
-                axis=-1,
             )
         )
-
-    d_modulation = jnp.stack(d_mods, axis=1).astype(LOWER)
-    packed = jnp.concatenate(
-        [
-            d_modulation.reshape(-1),
-            cond_low.reshape(-1),
-            *[item for item in attend_bias_grads],
-            *[item.astype(LOWER) for item in output_bias_grads],
-            *[item.astype(LOWER) for item in expand_bias_grads],
-            *[item.astype(LOWER) for item in reduce_bias_grads],
+        d_middles = (d_middle_one, d_middle_two)
+        d_branches = (d_branch_one, d_branch_two)
+        sums = (sums_one, sums_two)
+        d_attended = spread(d_joint)
+        (d_attended,), grown = together([d_attended], list(d_branches))
+        seconds = [
+            by_device(project("rf,fd->rd", actives[which], reduce_own[which]).astype(LOWER), which)
+            for which in range(2)
         ]
-    )
-    handles.append(tree.add(attend_parts[1]))
-    ((across,),) = tree.step([around(packed)])
-    modulation_size = d_modulation.size
+        grown = [grow(grown[which], orders[which][0]) for which in range(2)]
+        d_triples = attend_backward(
+            triples[0], triples[1], d_attended, me_array, size, rows + extra
+        )
+        d_triples, grown = together(list(d_triples), grown)
+
+        d_triples = [flat(item) for item in d_triples]
+        attend_grads = [
+            project("rd,re->de", fronts[which], d_triples[which]).astype(LOWER) for which in range(2)
+        ]
+        grown = [grow(grown[which], orders[which][1]) for which in range(2)]
+        d_fronts = [
+            project("re,de->rd", d_triples[which], attend_own[which])
+            .astype(LOWER)
+            .reshape(GROUP * slots, spans[which], width)
+            for which in range(2)
+        ]
+        attend_grads, grown, d_fronts = together(attend_grads, grown, d_fronts)
+        attend_grads = [item.reshape(GROUP, share, 3 * share) for item in attend_grads]
+
+
+        grown = [grow(grown[which], orders[which][2]) for which in range(2)]
+        attend_one = spread(attend_grads[0])
+        (attend_one,), grown, pairs = together([attend_one], grown, halved(d_fronts, 0))
+
+        d_fronts = summed(pairs)
+        attend_two = spread(attend_grads[1])
+        output_grads = []
+        output_bias_grads = []
+        for which in range(2):
+            d_branch_all = flat(grown[which])
+            output_grads.append(project("rd,re->de", flat(pieces[which]), d_branch_all).astype(LOWER))
+            d_cols = lax.dynamic_slice_in_dim(d_branch_all, me * share, share, 1)
+            output_bias_grads.append(jnp.sum(d_cols, axis=0, dtype=WIDE))
+        (attend_one, attend_two), pairs, output_grads = together(
+            [attend_one, attend_two], halved(d_fronts, 1), output_grads
+        )
+
+        d_fronts = summed(pairs)
+        pairs, seconds = together(halved(d_fronts, 2), halved(seconds, 0))
+
+        d_fronts = summed(pairs, WIDE)
+        input_grads = []
+        front_mods = []
+        for which in range(2):
+            d_stream, d_shift_front, d_scale_front = jax.vjp(
+                modulate, streams[which], parts[which][0], parts[which][1]
+            )[1](d_fronts[which])
+            input_grads.append((d_middles[which] + d_stream).astype(LOWER))
+            front_mods += [d_shift_front, d_scale_front]
+        pairs, front_mods, input_grads = together(
+            halved(summed(seconds), 1), front_mods, input_grads
+        )
+
+        pairs = halved(summed(pairs), 2)
+        seconds = summed(pairs, WIDE)
+        outputs = []
+        d_mods = []
+        attend_bias_grads = []
+        expand_bias_grads = []
+        reduce_bias_grads = []
+        for which in range(2):
+            second = seconds[which] + reduce_bias_full[which]
+            gate = parts[which][5][:, None, :]
+            outputs.append(((middles[which] + gate * second) * alive).astype(LOWER))
+            gate_feed = jnp.sum(cotangents[which] * second, axis=1)
+            column_sums = jnp.sum(d_triples[which], axis=0, dtype=WIDE)
+            attend_bias_grads.append(
+                jnp.concatenate([column_sums[:share], column_sums[2 * share :]]).astype(LOWER)
+            )
+            expand_bias_grads.append(jnp.sum(d_befores[which], axis=0, dtype=WIDE))
+            d_cols = lax.dynamic_slice_in_dim(d_seconds[which], me * share, share, 1)
+            reduce_bias_grads.append(jnp.sum(d_cols, axis=0, dtype=WIDE))
+            d_mods.append(
+                jnp.concatenate(
+                    [
+                        *front_mods[2 * which : 2 * which + 2],
+                        sums[which][:, 0],
+                        sums[which][:, 1],
+                        sums[which][:, 2],
+                        gate_feed,
+                    ],
+                    axis=-1,
+                )
+            )
+        d_modulation = jnp.stack(d_mods, axis=1).astype(LOWER)
+        packed = jnp.concatenate(
+            [
+                d_modulation.reshape(-1),
+                cond_low.reshape(-1),
+                *[item for item in attend_bias_grads],
+                *[item.astype(LOWER) for item in output_bias_grads],
+                *[item.astype(LOWER) for item in expand_bias_grads],
+                *[item.astype(LOWER) for item in reduce_bias_grads],
+            ]
+        )
+        return (attend_one, attend_two, *output_grads), packed, outputs, input_grads
+
+    late, packed, outputs, input_grads = once(trips, chain, pairs, actives, d_befores)
+    late, packed, early_totals = together(list(late), [packed], list(early_totals))
+    late_totals = lax.psum(tuple(late), "rep")
+
+    keep = slots * 12 * width + cond_low.size + 4 * share
+
+    def finish(packed, totals):
+        across = around(packed)
+        every = across[None, :, :keep]
+        expand_parts = []
+        for stage in range(3):
+            every = grow(every, ORDER_ONE[stage])
+            if stage < 2:
+                expand_parts.append(spread(totals[stage]))
+        return across[:, keep:], every, expand_parts
+
+    rest, every, expand_parts = once(trips, finish, packed[0], early_totals[:2])
+    modulation_size = slots * 12 * width
     cond_size = cond_low.size
     keep = modulation_size + cond_size + 4 * share
-    rest = jnp.sum(across[:, keep:], axis=0, dtype=WIDE)
+    rest = jnp.sum(rest, axis=0, dtype=WIDE)
     output_bias_total = rest[: 2 * share].reshape(2, share)
     expand_bias_total = rest[2 * share : 10 * share].reshape(2, 4 * share)
     reduce_bias_total = rest[10 * share :].reshape(2, share)
     apart = [me ^ item for item in range(GROUP)]
     places = [((item >> 1) & 1) + 2 * (item >> 2) + 4 * (item & 1) for item in apart]
-    every = across[None, :, :keep]
-    for stage in range(3):
-        if stage < 2:
-            handles.append(tree.add(attend_parts[2 + stage]))
-        ((every,),) = tree.step([grow(every, ORDER_ONE[stage])])
     modulation_all = every[:, :, :modulation_size].reshape(
         GROUP, REPLICAS, slots, 2, 6 * width
     )
@@ -1194,14 +1203,15 @@
     condition_grad = (
         jax.vjp(jax.nn.silu, cond_value)[1](d_cond_act[0])[0].astype(LOWER)
     )
-    tree.step()
-    done = [tuple(item[:2]) for item in handles]
-    reduce_parts = [[(item.reshape(1, 4 * share, width),)] for item in reduce_totals]
-    reduce_total = unpack(reduce_parts, edge, 1)
-    expand_total = unpack([done[0:2], done[2:4]], edge, 1)
-    output_parts = [[tuple(item[at : at + 1] for item in done[4])] for at in range(2)]
-    output_total = unpack(output_parts, edge, 1)
-    attend_total = unpack([done[5:7], done[7:9]], edge, 3)
+    reduce_total = unpack([[(item,)] for item in early_totals[2:]], edge, 1)
+    expand_total = unpack([[(item,)] for item in expand_parts], edge, 1)
+    late_totals, held = together(
+        list(late_totals),
+        [condition_grad, adaptive_total, adaptive_bias_total, reduce_total, expand_total],
+    )
+    condition_grad, adaptive_total, adaptive_bias_total, reduce_total, expand_total = held
+    output_total = unpack([[(item.reshape(1, share, width),)] for item in late_totals[2:]], edge, 1)
+    attend_total = unpack([[(item,)] for item in late_totals[:2]], edge, 3)
     return (
         outputs[0],
         outputs[1][:, :extra],

time: 987 us -> 904 us (0.916)
  waiting for transfers between devices: 388 us -> 311 us
  starting transfers between devices: 144 us -> 84.5 us
  loops' own time: 0 us -> 28.3 us
  other arithmetic: 96.3 us -> 122 us
  local copies, waits for them, and re-layouts: 98.5 us -> 112 us
    ppermute x27 -> x0, waiting for transfers between devices: 121 us -> none  [step(): entry[1] = lax.ppermute(entry[0], 'rep', HOPS[entry[2]])]
    all_to_all x8 -> x9, waiting for transfers between devices: 21 us -> 92.4 us  [spread(): lax.all_to_all(array, 'shard', split_axis=0, concat_axis=0, tiled=True)]
    ppermute x27 -> x0, starting transfers between devices: 55.6 us -> none  [step(): entry[1] = lax.ppermute(entry[0], 'rep', HOPS[entry[2]])]
    ppermute x52 -> x45, waiting for transfers between devices: 175 us -> 143 us  [swap(): lax.ppermute(array, 'shard', [(item, item ^ step) for item in range(GROUP)])]
    another operation x0 -> x2, loops' own time: none -> 28.3 us  [once(): return lax.fori_loop(0, trips, body, zeros)]
    concatenate x25 -> x27, other arithmetic: 37.5 us -> 56.3 us  [grow(): return jnp.concatenate([array, swap(array, step)], axis=0)]
    unnamed x317 -> x113, local copies, waits for them, and re-layouts: 27.5 us -> 10.9 us
    convert_element_type x27 -> x6, other arithmetic: 22.3 us -> 6.49 us  [the longest x2 2.34 us: chain(): input_grads.append((d_middles[which] + d_stream).astype(LOWER))]
  transfers between devices with their start and end apart: 97 -> 65, of which waited for: 43 -> 33; matrix products, arithmetic and copies ran while one was open for 26% -> 33% of each run, Pallas kernels for 9% -> 10%
where the time goes in v3:
time: 904 us; the launch traced here: 895 us
  waiting for transfers between devices  311 us (34%)
  other arithmetic  122 us (13%)
  local copies, waits for them, and re-layouts  112 us (12%)
  matrix products  106 us (12%)
  Pallas kernels  103 us (11%)
  starting transfers between devices  84.5 us (9%)
  loops' own time  28.3 us (3%)
  between operations  15.6 us (2%)
  blocking collectives  10.7 us (1%)
    ppermute x45, waiting for transfers between devices, swap(): lax.ppermute(array, 'shard', [(item, item ^ step) for item in range(GROUP)])  143 us
    dot_general x23, matrix products, project(): return jnp.einsum(form, left, right, preferred_element_type=WIDE)  106 us
    all_to_all x9, waiting for transfers between devices, spread(): lax.all_to_all(array, 'shard', split_axis=0, concat_axis=0, tiled=True)  92.4 us
    concatenate x27, other arithmetic, grow(): return jnp.concatenate([array, swap(array, step)], axis=0)  56.3 us
    ppermute x45, starting transfers between devices, swap(): lax.ppermute(array, 'shard', [(item, item ^ step) for item in range(GROUP)])  40.1 us
    all_to_all x9, starting transfers between devices, spread(): lax.all_to_all(array, 'shard', split_axis=0, concat_axis=0, tiled=True)  36.5 us
    ppermute x3, waiting for transfers between devices, ring(): found.append(lax.ppermute(found[-1], 'rep', pairs))  33.8 us
    pallas_call x4, Pallas kernels, unpack(): pl.pallas_call(kernel, out_shape=jax.ShapeDtypeStruct((2, total, pieces *...  29.3 us
  transfers between devices with their start and end apart: 65, of which 33 were waited for; matrix products, arithmetic and copies ran while one was open for 33% of the time, Pallas kernels for 10%

profile of v3, /device:TPU:0, one launch (start us, length us, event | category | flops | bytes accessed | tf_op | source)
XLA Modules:
  0.0 894.5 jit_solution(5334435672761990491)
XLA Ops:
  10.4 10.7 %all-gather.3 = bf16[8,2,3456]{2,1,0:T(2,128)(2,1)S(1)} all-gather(bf16[1,2,3456]{2,1,0:T(2,128)(2,1)S(1)} %bitcast.400), channel_id=2, replica_groups=mesh['shard'=8,'rep'=4] {'shard'}, dimensions={0}, use_global_device_ids=true | all-gather | bytes 124416 | tf_op jit(solution)/shard_map/all_gather | solution.py:903
  24.1 4.3 all-to-all-start.5
  28.6 6.1 fusion.28
  34.7 13.4 %all-to-all-done.5.refs_0_ = bf16[8,2,48,576]{3,2,1,0:T(8,128)(2,1)} async-done(((bf16[8,2,48,576]{3,2,1,0:T(8,128)(2,1)}), bf16[8,2,48,576]{3,2,1,0:T(8,128)(2,1)}, u32[]{:S(2)}, u32[]{:S(2)}) %all-to-all-start.5) | async-done | bytes 884768 | tf_op jit(solution)/shard_map/all_to_all | solution.py:374
  57.7 24.6 %collective-permute-done.28.refs_1_ = bf16[8,2,48,576]{3,2,1,0:T(8,128)(2,1)} collective-permute-done((bf16[8,2,48,576]{3,2,1,0:T(8,128)(2,1)}, bf16[8,2,48,576]{3,2,1,0:T(8,128)(2,1)}, u32[]{:S(2)}, u32[]{:S(2)}) %collective-permute-start.28) | collective-permute-done | bytes 884768 | tf_op jit(solution)/shard_map/ppermute | solution.py:493
  88.7 12.9 %collective-permute-done.29 = bf16[2,64,1536]{2,1,0:T(8,128)(2,1)S(1)} collective-permute-done((bf16[2,64,1536]{2,1,0:T(8,128)(2,1)S(1)}, bf16[2,64,1536]{2,1,0:T(8,128)(2,1)S(1)}, u32[]{:S(2)}, u32[]{:S(2)}) %collective-permute-start.29) | collective-permute-done | bytes 393248 | tf_op jit(solution)/shard_map/ppermute | solution.py:346
  114.1 12.4 %collective-permute-done.31 = bf16[4,64,1536]{2,1,0:T(8,128)(2,1)S(1)} collective-permute-done((bf16[4,64,1536]{2,1,0:T(8,128)(2,1)S(1)}, bf16[4,64,1536]{2,1,0:T(8,128)(2,1)S(1)}, u32[]{:S(2)}, u32[]{:S(2)}) %collective-permute-start.31) | collective-permute-done | bytes 786464 | tf_op jit(solution)/shard_map/ppermute | solution.py:346
  127.9 6.3 collective-permute-done.32.refs_3_
  156.8 4.9 pad_maximum_fusion.15
  166.1 6.4 fusion.37
  181.0 6.5 convert_element_type.636
  188.3 9.8 %attend.1 = (bf16[8,2,144,192]{3,2,1,0:T(8,128)(2,1)}, bf16[8,2,64,192]{3,2,1,0:T(8,128)(2,1)}, bf16[8,2,80,192]{3,2,1,0:T(8,128)(2,1)}) custom-call(s32[1]{0:T(128)} %bitcast.2.refs_0_, bf16[8,2,64,576]{3,2,1,0:T(8,128)(2,1)S(1)} %bitcast.355, bf16[8,2,80,576]{3,2,1,0:T(8,128)(2,1)S(1)} %bitcast.352), custom_call_target="tpu_custom_call" | custom-call | flops 254803968 | bytes 3538944 | tf_op jit(solution)/shard_map/attend/pallas_call | solution.py:630
  208.6 9.9 %all-to-all-done.7.refs_0_ = bf16[8,2,144,192]{3,2,1,0:T(8,128)(2,1)S(1)} async-done(((bf16[8,2,144,192]{3,2,1,0:T(8,128)(2,1)}), bf16[8,2,144,192]{3,2,1,0:T(8,128)(2,1)S(1)}, u32[]{:S(2)}, u32[]{:S(2)}) %all-to-all-start.7) | async-done | bytes 884768 | tf_op jit(solution)/shard_map/all_to_all | solution.py:374
  219.6 11.7 %middle.1 = (f32[2,64,1536]{2,1,0:T(8,128)}, f32[2,64,1536]{2,1,0:T(8,128)S(1)}, bf16[2,64,1536]{2,1,0:T(8,128)(2,1)}, f32[2,80,1536]{2,1,0:T(8,128)}, f32[2,80,...) custom-call(bf16[8,2,144,192]{3,2,1,0:T(8,128)(2,1)} %copy-done.34, bf16[8,2,192,1536]{3,2,1,0:T(8,128)(2,1)} %bitcast.341, ...), custom_call_target="tpu_custom_call" | custom-call | flops 1358954496 | bytes 13437184 | tf_op jit(solution)/shard_map/middle/pallas_call | solution.py:748
  232.4 9.2 %collective-permute-done.46 = bf16[2,80,1536]{2,1,0:T(8,128)(2,1)S(1)} collective-permute-done((bf16[2,80,1536]{2,1,0:T(8,128)(2,1)}, bf16[2,80,1536]{2,1,0:T(8,128)(2,1)S(1)}, u32[]{:S(2)}, u32[]{:S(2)}) %collective-permute-start.46) | collective-permute-done | bytes 491552 | tf_op jit(solution)/shard_map/ppermute | solution.py:346
  248.8 19.2 %collective-permute-done.47 = bf16[4,80,1536]{2,1,0:T(8,128)(2,1)S(1)} collective-permute-done((bf16[4,80,1536]{2,1,0:T(8,128)(2,1)S(1)}, bf16[4,80,1536]{2,1,0:T(8,128)(2,1)S(1)}, u32[]{:S(2)}, u32[]{:S(2)}) %collective-permute-start.47) | collective-permute-done | bytes 983072 | tf_op jit(solution)/shard_map/ppermute | solution.py:346
  298.3 5.3 multiply_convert_fusion.2
  303.7 5.5 fusion.26
  315.8 4.7 multiply_convert_fusion.3
  320.5 6.4 fusion.36
  329.8 4.0 fusion.38
  337.2 3.9 convolution_convert_fusion.11
  341.1 4.6 fusion.39
  345.8 4.6 convolution_convert_fusion.13
  359.0 320.7 %while.50 = (s32[]{:T(128)}, bf16[8,192,576]{2,1,0:T(8,128)(2,1)}, bf16[8,192,576]{2,1,0:T(8,128)(2,1)}, bf16[192,1536]{1,0:T(8,128)(2,1)}, bf16[192,1536]{1,0:T...) while((s32[]{:T(128)}, bf16[8,192,576]{2,1,0:T(8,128)(2,1)}, ...), condition=%wide.wide.region_26.27_spmd.clone, body=%wide.wide.region_7.26_spmd.clone.sunk | while | flops 17015431168 | bytes 515612192 | solution.py:415
  387.1 15.3 %collective-permute-done.6 = bf16[4,64,1536]{2,1,0:T(8,128)(2,1)S(1)} collective-permute-done((bf16[4,64,1536]{2,1,0:T(8,128)(2,1)S(1)}, bf16[4,64,1536]{2,1,0:T(8,128)(2,1)S(1)}, u32[]{:S(2)}, u32[]{:S(2)}) %collective-permute-start.6) | collective-permute-done | bytes 786464 | tf_op jit(solution)/shard_map/while/body/ppermute | solution.py:346
  405.1 4.8 collective-permute-done.8
  413.1 4.7 convolution_convert_fusion.25
  418.5 4.1 collective-permute-done.9.refs_9_
  423.3 14.8 %back.5 = (f32[2,64,1536]{2,1,0:T(8,128)}, bf16[2,64,1536]{2,1,0:T(8,128)(2,1)}, f32[2,3,1536]{2,1,0:T(4,128)}, f32[2,80,1536]{2,1,0:T(8,128)}, bf16[2,80,1536]{...) custom-call(bf16[8,2,192,1536]{3,2,1,0:T(8,128)(2,1)} %get-tuple-element.3036.refs_0_, ...), custom_call_target="tpu_custom_call" | custom-call | flops 1358954496 | bytes 19437184 | tf_op jit(solution)/shard_map/while/body/back/pallas_call | solution.py:830
  442.0 4.4 fusion.238
  446.9 5.7 convolution_convert_fusion.24
  452.6 6.2 all-to-all-done.2.refs_3_
  460.6 29.0 %attend_back.5 = (bf16[8,2,64,576]{3,2,1,0:T(8,128)(2,1)}, bf16[8,2,80,576]{3,2,1,0:T(8,128)(2,1)}) custom-call(s32[1]{0:T(128)} %get-tuple-element.3044.refs_0_, bf16[8,2,64,576]{3,2,1,0:T(8,128)(2,1)} %get-tuple-element.3045.refs_1_, bf16[8,2,80,576]{3,2,1,0:T(8,128)(2,1)} %get-tuple-element.3046.refs_2_, bf16[8,2,144,192]{3,2,1,0:T(8,128)(2,1)} %copy-done.4), custom_call_target="tpu_custom_call" | custom-call | flops 637009920 | bytes 6193152 | tf_op jit(solution)/shard_map/while/body/attend_back/pallas_call | solution.py:665
  495.0 5.2 convolution_convert_fusion.23
  525.6 4.5 all-to-all-start.3
  540.4 3.9 copy.283
  548.1 4.4 pad_maximum_fusion.63
  555.3 4.3 all-to-all-start.4
  575.7 9.8 %all-to-all-done.4 = bf16[8,192,576]{2,1,0:T(8,128)(2,1)} async-done(((bf16[8,192,576]{2,1,0:T(8,128)(2,1)}), bf16[8,192,576]{2,1,0:T(8,128)(2,1)}, u32[]{:S(2)}, u32[]{:S(2)}) %all-to-all-start.4) | async-done | bytes 1769504 | tf_op jit(solution)/shard_map/while/body/all_to_all | solution.py:374
  585.5 15.3 %collective-permute-done.18 = bf16[4,64,1536]{2,1,0:T(8,128)(2,1)S(1)} collective-permute-done((bf16[4,64,1536]{2,1,0:T(8,128)(2,1)}, bf16[4,64,1536]{2,1,0:T(8,128)(2,1)S(1)}, u32[]{:S(2)}, u32[]{:S(2)}) %collective-permute-start.18) | collective-permute-done | bytes 786464 | tf_op jit(solution)/shard_map/while/body/ppermute | solution.py:346
  600.7 4.4 collective-permute-done.19
  633.7 14.3 %collective-permute-done.24 = bf16[4,64,1536]{2,1,0:T(8,128)(2,1)S(1)} collective-permute-done((bf16[4,64,1536]{2,1,0:T(8,128)(2,1)S(1)}, bf16[4,64,1536]{2,1,0:T(8,128)(2,1)S(1)}, u32[]{:S(2)}, u32[]{:S(2)}) %collective-permute-start.24) | collective-permute-done | bytes 786464 | tf_op jit(solution)/shard_map/while/body/ppermute | solution.py:346
  651.8 6.9 collective-permute-done.27
  664.4 8.8 concatenate.207
  690.9 97.5 %while.49 = (s32[]{:T(128)}, bf16[4,2304]{1,0:T(4,128)(2,1)}, bf16[8,4,40704]{2,1,0:T(4,128)(2,1)}, bf16[8,192,768]{2,1,0:T(8,128)(2,1)}, bf16[8,192,768]{2,1,0:...) while((s32[]{:T(128)}, bf16[4,2304]{1,0:T(4,128)(2,1)}, ...), condition=%wide.region_36.37_spmd, body=%wide.region_35.36_spmd.sunk | while | flops 8288319 | bytes 36521040 | solution.py:415
  693.1 6.5 collective-permute-done
  699.6 8.6 collective-permute-done.1
  712.0 5.9 collective-permute-done.3
  719.5 4.4 all-to-all-start
  723.9 7.0 collective-permute-done.4
  733.6 20.8 %all-to-all-done = bf16[8,192,768]{2,1,0:T(8,128)(2,1)} async-done(((bf16[8,192,768]{2,1,0:T(8,128)(2,1)}), bf16[8,192,768]{2,1,0:T(8,128)(2,1)}, u32[]{:S(2)}, u32[]{:S(2)}) %all-to-all-start) | async-done | bytes 2359328 | tf_op jit(solution)/shard_map/while/body/all_to_all | solution.py:374
  754.4 4.4 all-to-all-start.1
  761.8 26.4 %all-to-all-done.1 = bf16[8,192,768]{2,1,0:T(8,128)(2,1)} async-done(((bf16[8,192,768]{2,1,0:T(8,128)(2,1)}), bf16[8,192,768]{2,1,0:T(8,128)(2,1)}, u32[]{:S(2)}, u32[]{:S(2)}) %all-to-all-start.1) | async-done | bytes 2359328 | tf_op jit(solution)/shard_map/while/body/all_to_all | solution.py:374
  788.4 4.2 slice.482
  793.6 5.0 reshape_reshape.3
  798.6 5.0 reshape.423
  805.1 7.0 fusion.51
  818.0 9.1 %convolution_bitcast_fusion = f32[2,192,9216]{2,1,0:T(8,128)} fusion(bf16[64,2,9216]{2,1,0:T(2,128)(2,1)} %reshape_reshape.3, bf16[64,1536]{1,0:T(8,128)(2,1)S(1)} %reshape.425, s32[]{:T(128)} %select_n.115), kind=kOutput, calls=%fused_computation.102 | convolution fusion | flops 452984832 | bytes 16547844 | tf_op jit(solution)/shard_map/gd,gse->sde/dot_general | solution.py:28
  830.8 8.0 unpack.5
  838.9 8.1 unpack.4
  847.7 26.9 %all-reduce.7.cloned.1.call-done = (bf16[8,192,576]{2,1,0:T(8,128)(2,1)}, bf16[8,192,576]{2,1,0:T(8,128)(2,1)}, bf16[192,1536]{1,0:T(8,128)(2,1)}, bf16[192,1536]{1,0:T(8,128)(2,1)}) async-done(((bf16[8,192,576]{2,1,0:T(8,128)(2,1)}, bf16[8,192,576]{2,1,0:T(8,128)(2,1)}, bf16[192,1536]{1,0:T(8,128)(2,1)}, bf16[192,1536]{1,0:T(8,128)(2,1)}), (bf16[8,192,576]{2,1,0:T(8,128)(2,1)}, ...) | async-done | bytes 4718608 | tf_op jit(solution)/shard_map/psum | solution.py:1155
  874.6 5.7 unpack.7
  880.3 7.5 unpack.6
  (538 shorter events, 302.2 us)
Async XLA Ops:
  7.2 157.8 %all-gather.7.cloned.1.call-start = ((), (), s32[]{:S(2)}) async-start(), calls=%async_computation.10 | async-start | bytes 10616832 | tf_op jit(solution)/shard_map/all_gather | solution.py:932
  24.1 24.0 %all-to-all-start.5 = ((bf16[8,2,48,576]{3,2,1,0:T(8,128)(2,1)}), bf16[8,2,48,576]{3,2,1,0:T(8,128)(2,1)}, u32[]{:S(2)}, u32[]{:S(2)}) async-start(bf16[8,2,48,576]{3,2,1,0:T(8,128)(2,1)} %pack.2), calls=%async_computation.5 | async-start | bytes 1966080 | tf_op jit(solution)/shard_map/all_to_all | solution.py:374
  52.2 33.2 %all-to-all-start.6 = ((f32[8,2,2,9216]{3,1,2,0:T(2,128)}), f32[8,2,2,9216]{3,1,2,0:T(2,128)S(1)}, u32[]{:S(2)}, u32[]{:S(2)}) async-start(f32[8,2,2,9216]{3,1,2,0:T(2,128)} %copy.198), calls=%async_computation.6 | async-start | bytes 2359296 | tf_op jit(solution)/shard_map/all_to_all | solution.py:374
  56.0 26.3 %collective-permute-start.28 = (bf16[8,2,48,576]{3,2,1,0:T(8,128)(2,1)}, bf16[8,2,48,576]{3,2,1,0:T(8,128)(2,1)}, u32[]{:S(2)}, u32[]{:S(2)}) collective-permute-start(bf16[8,2,48,576]{3,2,1,0:T(8,128)(2,1)} %all-to-all-done.5.refs_0_), channel_id=1, source_target_pairs={{0,1},{1,2},{2,3},{3,0},{4,5},{5,6},{6,7},{7,4},{8,9},{9,10},{10,1... | collective-permute-start | bytes 2654216 | tf_op jit(solution)/shard_map/ppermute | solution.py:493
  82.3 25.4 %collective-permute-start.30 = (bf16[8,2,48,576]{3,2,1,0:T(8,128)(2,1)}, bf16[8,2,48,576]{3,2,1,0:T(8,128)(2,1)}, u32[]{:S(2)}, u32[]{:S(2)}) collective-permute-start(bf16[8,2,48,576]{3,2,1,0:T(8,128)(2,1)} %collective-permute-done.28.refs_1_), channel_id=1, source_target_pairs={{0,1},{1,2},{2,3},{3,0},{4,5},{5,6},{6,7},{7,4},{8,9},{9,10},{10,1... | collective-permute-start | bytes 2654216 | tf_op jit(solution)/shard_map/ppermute | solution.py:493
  87.0 14.6 %collective-permute-start.29 = (bf16[2,64,1536]{2,1,0:T(8,128)(2,1)S(1)}, bf16[2,64,1536]{2,1,0:T(8,128)(2,1)S(1)}, u32[]{:S(2)}, u32[]{:S(2)}) collective-permute-start(bf16[2,64,1536]{2,1,0:T(8,128)(2,1)S(1)} %add_convert_fusion.16), channel_id=1, source_target_pairs={{0,8},{4,12},{8,0},{12,4},{16,24},{20,28},{24,16},{28,20},{1,9},{5... | collective-permute-start | bytes 1179656 | tf_op jit(solution)/shard_map/ppermute | solution.py:346
  87.5 16.2 %collective-permute-start.34 = (bf16[2,80,1536]{2,1,0:T(8,128)(2,1)S(1)}, bf16[2,80,1536]{2,1,0:T(8,128)(2,1)S(1)}, u32[]{:S(2)}, u32[]{:S(2)}) collective-permute-start(bf16[2,80,1536]{2,1,0:T(8,128)(2,1)S(1)} %add_convert_fusion.15), channel_id=1, source_target_pairs={{0,16},{4,20},{8,24},{12,28},{16,0},{20,4},{24,8},{28,12},{1,17},{... | collective-permute-start | bytes 1474568 | tf_op jit(solution)/shard_map/ppermute | solution.py:346
  107.7 26.4 %collective-permute-start.35 = (bf16[4,80,1536]{2,1,0:T(8,128)(2,1)}, bf16[4,80,1536]{2,1,0:T(8,128)(2,1)}, u32[]{:S(2)}, u32[]{:S(2)}) collective-permute-start(bf16[4,80,1536]{2,1,0:T(8,128)(2,1)} %pad_maximum_fusion.27), channel_id=1, source_target_pairs={{0,8},{4,12},{8,0},{12,4},{16,24},{20,28},{24,16},{28,20},{1,9},{5... | collective-permute-start | bytes 2949128 | tf_op jit(solution)/shard_map/ppermute | solution.py:346
  109.0 17.6 %collective-permute-start.31 = (bf16[4,64,1536]{2,1,0:T(8,128)(2,1)S(1)}, bf16[4,64,1536]{2,1,0:T(8,128)(2,1)S(1)}, u32[]{:S(2)}, u32[]{:S(2)}) collective-permute-start(bf16[4,64,1536]{2,1,0:T(8,128)(2,1)S(1)} %pad_maximum_fusion.30), channel_id=1, source_target_pairs={{0,16},{4,20},{8,24},{12,28},{16,0},{20,4},{24,8},{28,12},{1,17},{... | collective-permute-start | bytes 2359304 | tf_op jit(solution)/shard_map/ppermute | solution.py:346
  110.5 23.6 %collective-permute-start.32 = (bf16[8,2,48,576]{3,2,1,0:T(8,128)(2,1)}, bf16[8,2,48,576]{3,2,1,0:T(8,128)(2,1)}, u32[]{:S(2)}, u32[]{:S(2)}) collective-permute-start(bf16[8,2,48,576]{3,2,1,0:T(8,128)(2,1)} %collective-permute-done.30.refs_2_), channel_id=1, source_target_pairs={{0,1},{1,2},{2,3},{3,0},{4,5},{5,6},{6,7},{7,4},{8,9},{9,10},{10,1... | collective-permute-start | bytes 2654216 | tf_op jit(solution)/shard_map/ppermute | solution.py:493
  134.1 14.3 %collective-permute-start.33 = (bf16[8,64,1536]{2,1,0:T(8,128)(2,1)S(1)}, bf16[8,64,1536]{2,1,0:T(8,128)(2,1)}, u32[]{:S(2)}, u32[]{:S(2)}) collective-permute-start(bf16[8,64,1536]{2,1,0:T(8,128)(2,1)S(1)} %pad_maximum_fusion.24), channel_id=1, source_target_pairs={{0,4},{4,0},{8,12},{12,8},{16,20},{20,16},{24,28},{28,24},{1,5},{5... | collective-permute-start | bytes 4718600 | tf_op jit(solution)/shard_map/ppermute | solution.py:346
  137.1 19.7 %collective-permute-start.36 = (bf16[8,80,1536]{2,1,0:T(8,128)(2,1)}, bf16[8,80,1536]{2,1,0:T(8,128)(2,1)}, u32[]{:S(2)}, u32[]{:S(2)}) collective-permute-start(bf16[8,80,1536]{2,1,0:T(8,128)(2,1)} %pad_maximum_fusion.21), channel_id=1, source_target_pairs={{0,4},{4,0},{8,12},{12,8},{16,20},{20,16},{24,28},{28,24},{1,5},{5... | collective-permute-start | bytes 5898248 | tf_op jit(solution)/shard_map/ppermute | solution.py:346
  144.3 20.7 %all-to-all-start.8 = ((bf16[8,2,48,768]{3,2,1,0:T(8,128)(2,1)}), bf16[8,2,48,768]{3,2,1,0:T(8,128)(2,1)S(1)}, u32[]{:S(2)}, u32[]{:S(2)}) async-start(bf16[8,2,48,768]{3,2,1,0:T(8,128)(2,1)} %pack.3), calls=%async_computation.8 | async-start | bytes 2359296 | tf_op jit(solution)/shard_map/all_to_all | solution.py:374
  147.9 146.9 %all-gather.9.cloned.1.call-start = ((), (), s32[]{:S(2)}) async-start(), calls=%async_computation.11 | async-start | bytes 5898240 | tf_op jit(solution)/shard_map/all_gather | solution.py:934
  161.6 15.4 %collective-permute-start.38 = (bf16[2,80,1536]{2,1,0:T(8,128)(2,1)}, bf16[2,80,1536]{2,1,0:T(8,128)(2,1)}, u32[]{:S(2)}, u32[]{:S(2)}) collective-permute-start(bf16[2,80,1536]{2,1,0:T(8,128)(2,1)} %get-tuple-element.1014), channel_id=1, source_target_pairs={{0,16},{4,20},{8,24},{12,28},{16,0},{20,4},{24,8},{28,12},{1,17},{... | collective-permute-start | bytes 1474568 | tf_op jit(solution)/shard_map/ppermute | solution.py:346
  163.5 11.2 %collective-permute-start.37 = (bf16[2,64,1536]{2,1,0:T(8,128)(2,1)}, bf16[2,64,1536]{2,1,0:T(8,128)(2,1)}, u32[]{:S(2)}, u32[]{:S(2)}) collective-permute-start(bf16[2,64,1536]{2,1,0:T(8,128)(2,1)} %get-tuple-element.1013), channel_id=1, source_target_pairs={{0,8},{4,12},{8,0},{12,4},{16,24},{20,28},{24,16},{28,20},{1,9},{5... | collective-permute-start | bytes 1179656 | tf_op jit(solution)/shard_map/ppermute | solution.py:346
  179.3 23.7 %collective-permute-start.39 = (bf16[4,64,1536]{2,1,0:T(8,128)(2,1)}, bf16[4,64,1536]{2,1,0:T(8,128)(2,1)}, u32[]{:S(2)}, u32[]{:S(2)}) collective-permute-start(bf16[4,64,1536]{2,1,0:T(8,128)(2,1)} %pad_maximum_fusion.31), channel_id=1, source_target_pairs={{0,16},{4,20},{8,24},{12,28},{16,0},{20,4},{24,8},{28,12},{1,17},{... | collective-permute-start | bytes 2359304 | tf_op jit(solution)/shard_map/ppermute | solution.py:346
  179.8 25.8 %collective-permute-start.40 = (bf16[4,80,1536]{2,1,0:T(8,128)(2,1)}, bf16[4,80,1536]{2,1,0:T(8,128)(2,1)}, u32[]{:S(2)}, u32[]{:S(2)}) collective-permute-start(bf16[4,80,1536]{2,1,0:T(8,128)(2,1)} %pad_maximum_fusion.28), channel_id=1, source_target_pairs={{0,8},{4,12},{8,0},{12,4},{16,24},{20,28},{24,16},{28,20},{1,9},{5... | collective-permute-start | bytes 2949128 | tf_op jit(solution)/shard_map/ppermute | solution.py:346
  198.1 20.4 %all-to-all-start.7 = ((bf16[8,2,144,192]{3,2,1,0:T(8,128)(2,1)}), bf16[8,2,144,192]{3,2,1,0:T(8,128)(2,1)S(1)}, u32[]{:S(2)}, u32[]{:S(2)}) async-start(bf16[8,2,144,192]{3,2,1,0:T(8,128)(2,1)} %get-tuple-element.1017), calls=%async_computation.7 | async-start | bytes 2359296 | tf_op jit(solution)/shard_map/all_to_all | solution.py:374
  201.8 483.2 %all-reduce.9.cloned.1.call-start = ((), (), s32[]{:S(2)}) async-start(), calls=%async_computation.13 | async-start | bytes 18874368 | tf_op jit(solution)/shard_map/psum | solution.py:1028
  231.3 10.3 %collective-permute-start.46 = (bf16[2,80,1536]{2,1,0:T(8,128)(2,1)}, bf16[2,80,1536]{2,1,0:T(8,128)(2,1)S(1)}, u32[]{:S(2)}, u32[]{:S(2)}) collective-permute-start(bf16[2,80,1536]{2,1,0:T(8,128)(2,1)} %get-tuple-element.1027), channel_id=1, source_target_pairs={{0,16},{4,20},{8,24},{12,28},{16,0},{20,4},{24,8},{28,12},{1,17},{... | collective-permute-start | bytes 1474568 | tf_op jit(solution)/shard_map/ppermute | solution.py:346
  231.8 14.8 %collective-permute-start.42 = (bf16[2,64,1536]{2,1,0:T(8,128)(2,1)}, bf16[2,64,1536]{2,1,0:T(8,128)(2,1)S(1)}, u32[]{:S(2)}, u32[]{:S(2)}) collective-permute-start(bf16[2,64,1536]{2,1,0:T(8,128)(2,1)} %get-tuple-element.1023), channel_id=1, source_target_pairs={{0,8},{4,12},{8,0},{12,4},{16,24},{20,28},{24,16},{28,20},{1,9},{5... | collective-permute-start | bytes 1179656 | tf_op jit(solution)/shard_map/ppermute | solution.py:346
  242.9 25.1 %collective-permute-start.47 = (bf16[4,80,1536]{2,1,0:T(8,128)(2,1)S(1)}, bf16[4,80,1536]{2,1,0:T(8,128)(2,1)S(1)}, u32[]{:S(2)}, u32[]{:S(2)}) collective-permute-start(bf16[4,80,1536]{2,1,0:T(8,128)(2,1)S(1)} %pad_maximum_fusion.29), channel_id=1, source_target_pairs={{0,8},{4,12},{8,0},{12,4},{16,24},{20,28},{24,16},{28,20},{1,9},{5... | collective-permute-start | bytes 2949128 | tf_op jit(solution)/shard_map/ppermute | solution.py:346
  247.9 21.7 %collective-permute-start.43 = (bf16[4,64,1536]{2,1,0:T(8,128)(2,1)S(1)}, bf16[4,64,1536]{2,1,0:T(8,128)(2,1)S(1)}, u32[]{:S(2)}, u32[]{:S(2)}) collective-permute-start(bf16[4,64,1536]{2,1,0:T(8,128)(2,1)S(1)} %pad_maximum_fusion.32), channel_id=1, source_target_pairs={{0,16},{4,20},{8,24},{12,28},{16,0},{20,4},{24,8},{28,12},{1,17},{... | collective-permute-start | bytes 2359304 | tf_op jit(solution)/shard_map/ppermute | solution.py:346
  248.3 36.1 %collective-permute-start.45 = (bf16[8,80,1536]{2,1,0:T(8,128)(2,1)}, bf16[8,80,1536]{2,1,0:T(8,128)(2,1)}, u32[]{:S(2)}, u32[]{:S(2)}) collective-permute-start(bf16[8,80,1536]{2,1,0:T(8,128)(2,1)} %pad_maximum_fusion.22), channel_id=1, source_target_pairs={{0,4},{4,0},{8,12},{12,8},{16,20},{20,16},{24,28},{28,24},{1,5},{5... | collective-permute-start | bytes 5898248 | tf_op jit(solution)/shard_map/ppermute | solution.py:346
  248.3 32.3 %collective-permute-start.41 = (bf16[8,64,1536]{2,1,0:T(8,128)(2,1)}, bf16[8,64,1536]{2,1,0:T(8,128)(2,1)}, u32[]{:S(2)}, u32[]{:S(2)}) collective-permute-start(bf16[8,64,1536]{2,1,0:T(8,128)(2,1)} %pad_maximum_fusion.25), channel_id=1, source_target_pairs={{0,4},{4,0},{8,12},{12,8},{16,20},{20,16},{24,28},{28,24},{1,5},{5... | collective-permute-start | bytes 4718600 | tf_op jit(solution)/shard_map/ppermute | solution.py:346
  269.6 21.8 %collective-permute-start.48 = (bf16[8,80,1536]{2,1,0:T(8,128)(2,1)}, bf16[8,80,1536]{2,1,0:T(8,128)(2,1)}, u32[]{:S(2)}, u32[]{:S(2)}) collective-permute-start(bf16[8,80,1536]{2,1,0:T(8,128)(2,1)} %pad_maximum_fusion.23), channel_id=1, source_target_pairs={{0,4},{4,0},{8,12},{12,8},{16,20},{20,16},{24,28},{28,24},{1,5},{5... | collective-permute-start | bytes 5898248 | tf_op jit(solution)/shard_map/ppermute | solution.py:346
  271.1 17.1 %collective-permute-start.44 = (bf16[8,64,1536]{2,1,0:T(8,128)(2,1)}, bf16[8,64,1536]{2,1,0:T(8,128)(2,1)}, u32[]{:S(2)}, u32[]{:S(2)}) collective-permute-start(bf16[8,64,1536]{2,1,0:T(8,128)(2,1)} %pad_maximum_fusion.26), channel_id=1, source_target_pairs={{0,4},{4,0},{8,12},{12,8},{16,20},{20,16},{24,28},{28,24},{1,5},{5... | collective-permute-start | bytes 4718600 | tf_op jit(solution)/shard_map/ppermute | solution.py:346
  335.3 15.1 %collective-permute-start.50 = (bf16[8,80,1536]{2,1,0:T(8,128)(2,1)S(1)}, bf16[8,80,1536]{2,1,0:T(8,128)(2,1)}, u32[]{:S(2)}, u32[]{:S(2)}) collective-permute-start(bf16[8,80,1536]{2,1,0:T(8,128)(2,1)S(1)} %get-tuple-element.1920), channel_id=1, source_target_pairs={{0,4},{4,0},{8,12},{12,8},{16,20},{20,16},{24,28},{28,24},{1,5},{5... | collective-permute-start | bytes 5898248 | tf_op jit(solution)/shard_map/ppermute | solution.py:346
  336.7 13.7 %collective-permute-start.49 = (bf16[8,64,1536]{2,1,0:T(8,128)(2,1)S(1)}, bf16[8,64,1536]{2,1,0:T(8,128)(2,1)}, u32[]{:S(2)}, u32[]{:S(2)}) collective-permute-start(bf16[8,64,1536]{2,1,0:T(8,128)(2,1)S(1)} %get-tuple-element.1922), channel_id=1, source_target_pairs={{0,4},{4,0},{8,12},{12,8},{16,20},{20,16},{24,28},{28,24},{1,5},{5... | collective-permute-start | bytes 4718600 | tf_op jit(solution)/shard_map/ppermute | solution.py:346
  350.4 524.2 %all-reduce.7.cloned.1.call-start = ((), (), s32[]{:S(2)}) async-start(), calls=%async_computation.12 | async-start | bytes 10223616 | tf_op jit(solution)/shard_map/psum | solution.py:1155
  382.8 19.5 %collective-permute-start.6 = (bf16[4,64,1536]{2,1,0:T(8,128)(2,1)S(1)}, bf16[4,64,1536]{2,1,0:T(8,128)(2,1)S(1)}, u32[]{:S(2)}, u32[]{:S(2)}) collective-permute-start(bf16[4,64,1536]{2,1,0:T(8,128)(2,1)S(1)} %slice.802), channel_id=1, source_target_pairs={{0,16},{4,20},{8,24},{12,28},{16,0},{20,4},{24,8},{28,12},{1,17},{... | collective-permute-start | bytes 2359304 | tf_op jit(solution)/shard_map/while/body/ppermute | solution.py:346
  385.2 24.7 %collective-permute-start.8 = (bf16[4,80,1536]{2,1,0:T(8,128)(2,1)S(1)}, bf16[4,80,1536]{2,1,0:T(8,128)(2,1)S(1)}, u32[]{:S(2)}, u32[]{:S(2)}) collective-permute-start(bf16[4,80,1536]{2,1,0:T(8,128)(2,1)S(1)} %slice.803), channel_id=1, source_target_pairs={{0,8},{4,12},{8,0},{12,4},{16,24},{20,28},{24,16},{28,20},{1,9},{5... | collective-permute-start | bytes 2949128 | tf_op jit(solution)/shard_map/while/body/ppermute | solution.py:346
  403.4 15.1 %collective-permute-start.7 = (bf16[2,64,1536]{2,1,0:T(8,128)(2,1)S(1)}, bf16[2,64,1536]{2,1,0:T(8,128)(2,1)S(1)}, u32[]{:S(2)}, u32[]{:S(2)}) collective-permute-start(bf16[2,64,1536]{2,1,0:T(8,128)(2,1)S(1)} %get-tuple-element.2789), channel_id=1, source_target_pairs={{0,8},{4,12},{8,0},{12,4},{16,24},{20,28},{24,16},{28,20},{1,9},{5... | collective-permute-start | bytes 1179656 | tf_op jit(solution)/shard_map/while/body/ppermute | solution.py:346
  411.1 11.6 %collective-permute-start.9 = (bf16[2,80,1536]{2,1,0:T(8,128)(2,1)S(1)}, bf16[2,80,1536]{2,1,0:T(8,128)(2,1)}, u32[]{:S(2)}, u32[]{:S(2)}) collective-permute-start(bf16[2,80,1536]{2,1,0:T(8,128)(2,1)S(1)} %get-tuple-element.2793), channel_id=1, source_target_pairs={{0,16},{4,20},{8,24},{12,28},{16,0},{20,4},{24,8},{28,12},{1,17},{... | collective-permute-start | bytes 1474568 | tf_op jit(solution)/shard_map/while/body/ppermute | solution.py:346
  438.1 20.6 %all-to-all-start.2 = ((bf16[8,2,144,192]{3,2,1,0:T(8,128)(2,1)}), bf16[8,2,144,192]{3,2,1,0:T(8,128)(2,1)S(1)}, u32[]{:S(2)}, u32[]{:S(2)}) async-start(bf16[8,2,144,192]{3,2,1,0:T(8,128)(2,1)} %get-tuple-element.2794), calls=%async_computation.2 | async-start | bytes 2359296 | tf_op jit(solution)/shard_map/while/body/all_to_all | solution.py:374
  446.4 175.9 %collective-permute-start.23 = (bf16[8,80,1536]{2,1,0:T(8,128)(2,1)}, bf16[8,80,1536]{2,1,0:T(8,128)(2,1)}, u32[]{:S(2)}, u32[]{:S(2)}) collective-permute-start(bf16[8,80,1536]{2,1,0:T(8,128)(2,1)} %bitcast.332), channel_id=1, source_target_pairs={{0,4},{4,0},{8,12},{12,8},{16,20},{20,16},{24,28},{28,24},{1,5},{5... | collective-permute-start | bytes 5898248 | tf_op jit(solution)/shard_map/while/body/ppermute | solution.py:346
  458.8 30.8 %collective-permute-start.10 = (bf16[2,64,1536]{2,1,0:T(8,128)(2,1)}, bf16[2,64,1536]{2,1,0:T(8,128)(2,1)}, u32[]{:S(2)}, u32[]{:S(2)}) collective-permute-start(bf16[2,64,1536]{2,1,0:T(8,128)(2,1)} %get-tuple-element.2800), channel_id=1, source_target_pairs={{0,8},{4,12},{8,0},{12,4},{16,24},{20,28},{24,16},{28,20},{1,9},{5... | collective-permute-start | bytes 1179656 | tf_op jit(solution)/shard_map/while/body/ppermute | solution.py:346
  459.9 31.0 %collective-permute-start.11 = (bf16[2,80,1536]{2,1,0:T(8,128)(2,1)S(1)}, bf16[2,80,1536]{2,1,0:T(8,128)(2,1)}, u32[]{:S(2)}, u32[]{:S(2)}) collective-permute-start(bf16[2,80,1536]{2,1,0:T(8,128)(2,1)S(1)} %copy-done.26), channel_id=1, source_target_pairs={{0,16},{4,20},{8,24},{12,28},{16,0},{20,4},{24,8},{28,12},{1,17},{... | collective-permute-start | bytes 1474568 | tf_op jit(solution)/shard_map/while/body/ppermute | solution.py:346
  492.0 23.0 %collective-permute-start.13 = (bf16[4,80,1536]{2,1,0:T(8,128)(2,1)S(1)}, bf16[4,80,1536]{2,1,0:T(8,128)(2,1)S(1)}, u32[]{:S(2)}, u32[]{:S(2)}) collective-permute-start(bf16[4,80,1536]{2,1,0:T(8,128)(2,1)S(1)} %pad_maximum_fusion.59), channel_id=1, source_target_pairs={{0,8},{4,12},{8,0},{12,4},{16,24},{20,28},{24,16},{28,20},{1,9},{5... | collective-permute-start | bytes 2949128 | tf_op jit(solution)/shard_map/while/body/ppermute | solution.py:346
  493.5 17.6 %collective-permute-start.12 = (bf16[4,64,1536]{2,1,0:T(8,128)(2,1)S(1)}, bf16[4,64,1536]{2,1,0:T(8,128)(2,1)S(1)}, u32[]{:S(2)}, u32[]{:S(2)}) collective-permute-start(bf16[4,64,1536]{2,1,0:T(8,128)(2,1)S(1)} %pad_maximum_fusion.58), channel_id=1, source_target_pairs={{0,16},{4,20},{8,24},{12,28},{16,0},{20,4},{24,8},{28,12},{1,17},{... | collective-permute-start | bytes 2359304 | tf_op jit(solution)/shard_map/while/body/ppermute | solution.py:346
  516.5 31.5 %collective-permute-start.15 = (bf16[8,80,1536]{2,1,0:T(8,128)(2,1)}, bf16[8,80,1536]{2,1,0:T(8,128)(2,1)}, u32[]{:S(2)}, u32[]{:S(2)}) collective-permute-start(bf16[8,80,1536]{2,1,0:T(8,128)(2,1)} %pad_maximum_fusion.61), channel_id=1, source_target_pairs={{0,4},{4,0},{8,12},{12,8},{16,20},{20,16},{24,28},{28,24},{1,5},{5... | collective-permute-start | bytes 5898248 | tf_op jit(solution)/shard_map/while/body/ppermute | solution.py:346
  516.5 27.8 %collective-permute-start.14 = (bf16[8,64,1536]{2,1,0:T(8,128)(2,1)S(1)}, bf16[8,64,1536]{2,1,0:T(8,128)(2,1)}, u32[]{:S(2)}, u32[]{:S(2)}) collective-permute-start(bf16[8,64,1536]{2,1,0:T(8,128)(2,1)S(1)} %pad_maximum_fusion.60), channel_id=1, source_target_pairs={{0,4},{4,0},{8,12},{12,8},{16,20},{20,16},{24,28},{28,24},{1,5},{5... | collective-permute-start | bytes 4718600 | tf_op jit(solution)/shard_map/while/body/ppermute | solution.py:346
  519.2 40.5 %collective-permute-start.17 = (bf16[8,80,1536]{2,1,0:T(8,128)(2,1)}, bf16[8,80,1536]{2,1,0:T(8,128)(2,1)}, u32[]{:S(2)}, u32[]{:S(2)}) collective-permute-start(bf16[8,80,1536]{2,1,0:T(8,128)(2,1)} %get-tuple-element.2814), channel_id=1, source_target_pairs={{0,4},{4,0},{8,12},{12,8},{16,20},{20,16},{24,28},{28,24},{1,5},{5... | collective-permute-start | bytes 5898248 | tf_op jit(solution)/shard_map/while/body/ppermute | solution.py:346
  521.2 38.5 %collective-permute-start.16 = (bf16[8,64,1536]{2,1,0:T(8,128)(2,1)}, bf16[8,64,1536]{2,1,0:T(8,128)(2,1)}, u32[]{:S(2)}, u32[]{:S(2)}) collective-permute-start(bf16[8,64,1536]{2,1,0:T(8,128)(2,1)} %get-tuple-element.2811), channel_id=1, source_target_pairs={{0,4},{4,0},{8,12},{12,8},{16,20},{20,16},{24,28},{28,24},{1,5},{5... | collective-permute-start | bytes 4718600 | tf_op jit(solution)/shard_map/while/body/ppermute | solution.py:346
  525.6 29.7 %all-to-all-start.3 = ((bf16[8,192,576]{2,1,0:T(8,128)(2,1)}), bf16[8,192,576]{2,1,0:T(8,128)(2,1)}, u32[]{:S(2)}, u32[]{:S(2)}) async-start(bf16[8,192,576]{2,1,0:T(8,128)(2,1)} %bitcast.344), calls=%async_computation.3 | async-start | bytes 3932160 | tf_op jit(solution)/shard_map/while/body/all_to_all | solution.py:374
  544.3 77.9 %collective-permute-start.22 = (bf16[8,64,1536]{2,1,0:T(8,128)(2,1)}, bf16[8,64,1536]{2,1,0:T(8,128)(2,1)}, u32[]{:S(2)}, u32[]{:S(2)}) collective-permute-start(bf16[8,64,1536]{2,1,0:T(8,128)(2,1)} %bitcast.359), channel_id=1, source_target_pairs={{0,4},{4,0},{8,12},{12,8},{16,20},{20,16},{24,28},{28,24},{1,5},{5... | collective-permute-start | bytes 4718600 | tf_op jit(solution)/shard_map/while/body/ppermute | solution.py:346
  555.3 30.1 %all-to-all-start.4 = ((bf16[8,192,576]{2,1,0:T(8,128)(2,1)}), bf16[8,192,576]{2,1,0:T(8,128)(2,1)}, u32[]{:S(2)}, u32[]{:S(2)}) async-start(bf16[8,192,576]{2,1,0:T(8,128)(2,1)} %bitcast.343), calls=%async_computation.4 | async-start | bytes 3932160 | tf_op jit(solution)/shard_map/while/body/all_to_all | solution.py:374
  563.5 41.7 %collective-permute-start.19 = (bf16[4,80,1536]{2,1,0:T(8,128)(2,1)}, bf16[4,80,1536]{2,1,0:T(8,128)(2,1)}, u32[]{:S(2)}, u32[]{:S(2)}) collective-permute-start(bf16[4,80,1536]{2,1,0:T(8,128)(2,1)} %get-tuple-element.2824), channel_id=1, source_target_pairs={{0,8},{4,12},{8,0},{12,4},{16,24},{20,28},{24,16},{28,20},{1,9},{5... | collective-permute-start | bytes 2949128 | tf_op jit(solution)/shard_map/while/body/ppermute | solution.py:346
  568.6 32.1 %collective-permute-start.18 = (bf16[4,64,1536]{2,1,0:T(8,128)(2,1)}, bf16[4,64,1536]{2,1,0:T(8,128)(2,1)S(1)}, u32[]{:S(2)}, u32[]{:S(2)}) collective-permute-start(bf16[4,64,1536]{2,1,0:T(8,128)(2,1)} %get-tuple-element.2820), channel_id=1, source_target_pairs={{0,16},{4,20},{8,24},{12,28},{16,0},{20,4},{24,8},{28,12},{1,17},{... | collective-permute-start | bytes 2359304 | tf_op jit(solution)/shard_map/while/body/ppermute | solution.py:346
  607.5 14.8 %collective-permute-start.21 = (bf16[2,80,1536]{2,1,0:T(8,128)(2,1)}, bf16[2,80,1536]{2,1,0:T(8,128)(2,1)S(1)}, u32[]{:S(2)}, u32[]{:S(2)}) collective-permute-start(bf16[2,80,1536]{2,1,0:T(8,128)(2,1)} %get-tuple-element.2838), channel_id=1, source_target_pairs={{0,16},{4,20},{8,24},{12,28},{16,0},{20,4},{24,8},{28,12},{1,17},{... | collective-permute-start | bytes 1474568 | tf_op jit(solution)/shard_map/while/body/ppermute | solution.py:346
  611.1 11.1 %collective-permute-start.20 = (bf16[2,64,1536]{2,1,0:T(8,128)(2,1)}, bf16[2,64,1536]{2,1,0:T(8,128)(2,1)S(1)}, u32[]{:S(2)}, u32[]{:S(2)}) collective-permute-start(bf16[2,64,1536]{2,1,0:T(8,128)(2,1)} %get-tuple-element.2834), channel_id=1, source_target_pairs={{0,8},{4,12},{8,0},{12,4},{16,24},{20,28},{24,16},{28,20},{1,9},{5... | collective-permute-start | bytes 1179656 | tf_op jit(solution)/shard_map/while/body/ppermute | solution.py:346
  626.1 22.8 %collective-permute-start.25 = (bf16[4,80,1536]{2,1,0:T(8,128)(2,1)S(1)}, bf16[4,80,1536]{2,1,0:T(8,128)(2,1)S(1)}, u32[]{:S(2)}, u32[]{:S(2)}) collective-permute-start(bf16[4,80,1536]{2,1,0:T(8,128)(2,1)S(1)} %get-tuple-element.2852), channel_id=1, source_target_pairs={{0,8},{4,12},{8,0},{12,4},{16,24},{20,28},{24,16},{28,20},{1,9},{5... | collective-permute-start | bytes 2949128 | tf_op jit(solution)/shard_map/while/body/ppermute | solution.py:346
  629.6 18.3 %collective-permute-start.24 = (bf16[4,64,1536]{2,1,0:T(8,128)(2,1)S(1)}, bf16[4,64,1536]{2,1,0:T(8,128)(2,1)S(1)}, u32[]{:S(2)}, u32[]{:S(2)}) collective-permute-start(bf16[4,64,1536]{2,1,0:T(8,128)(2,1)S(1)} %get-tuple-element.2848), channel_id=1, source_target_pairs={{0,16},{4,20},{8,24},{12,28},{16,0},{20,4},{24,8},{28,12},{1,17},{... | collective-permute-start | bytes 2359304 | tf_op jit(solution)/shard_map/while/body/ppermute | solution.py:346
  649.3 9.4 %collective-permute-start.27 = (bf16[2,64,1536]{2,1,0:T(8,128)(2,1)S(1)}, bf16[2,64,1536]{2,1,0:T(8,128)(2,1)S(1)}, u32[]{:S(2)}, u32[]{:S(2)}) collective-permute-start(bf16[2,64,1536]{2,1,0:T(8,128)(2,1)S(1)} %slice.805), channel_id=1, source_target_pairs={{0,8},{4,12},{8,0},{12,4},{16,24},{20,28},{24,16},{28,20},{1,9},{5... | collective-permute-start | bytes 1179656 | tf_op jit(solution)/shard_map/while/body/ppermute | solution.py:346
  651.2 11.2 %collective-permute-start.26 = (bf16[2,80,1536]{2,1,0:T(8,128)(2,1)S(1)}, bf16[2,80,1536]{2,1,0:T(8,128)(2,1)S(1)}, u32[]{:S(2)}, u32[]{:S(2)}) collective-permute-start(bf16[2,80,1536]{2,1,0:T(8,128)(2,1)S(1)} %slice.804), channel_id=1, source_target_pairs={{0,16},{4,20},{8,24},{12,28},{16,0},{20,4},{24,8},{28,12},{1,17},{... | collective-permute-start | bytes 1474568 | tf_op jit(solution)/shard_map/while/body/ppermute | solution.py:346
  690.9 8.6 collective-permute-start
  690.9 17.3 %collective-permute-start.1 = (bf16[43008]{0:T(1024)(128)(2,1)S(1)}, bf16[43008]{0:T(1024)(128)(2,1)S(1)}, u32[]{:S(2)}, u32[]{:S(2)}) collective-permute-start(bf16[43008]{0:T(1024)(128)(2,1)S(1)} %get-tuple-element.2734), channel_id=1, source_target_pairs={{0,2},{1,3},{2,0},{3,1},{4,6},{5,7},{6,4},{7,5},{8,10},{9,11},{10,... | collective-permute-start | bytes 258056 | tf_op jit(solution)/shard_map/while/body/ppermute | solution.py:387
  691.4 17.0 %collective-permute-start.2 = (bf16[43008]{0:T(1024)(128)(2,1)S(1)}, bf16[43008]{0:T(1024)(128)(2,1)S(1)}, u32[]{:S(2)}, u32[]{:S(2)}) collective-permute-start(bf16[43008]{0:T(1024)(128)(2,1)S(1)} %get-tuple-element.2734), channel_id=1, source_target_pairs={{0,1},{1,2},{2,3},{3,0},{4,5},{5,6},{6,7},{7,4},{8,9},{9,10},{10,1... | collective-permute-start | bytes 258056 | tf_op jit(solution)/shard_map/while/body/ppermute | solution.py:387
  718.4 12.5 %collective-permute-start.4 = (bf16[2,4,40704]{2,1,0:T(4,128)(2,1)S(1)}, bf16[2,4,40704]{2,1,0:T(4,128)(2,1)S(1)}, u32[]{:S(2)}, u32[]{:S(2)}) collective-permute-start(bf16[2,4,40704]{2,1,0:T(4,128)(2,1)S(1)} %pad_maximum_fusion.55), channel_id=1, source_target_pairs={{0,16},{4,20},{8,24},{12,28},{16,0},{20,4},{24,8},{28,12},{1,17},{... | collective-permute-start | bytes 1953800 | tf_op jit(solution)/shard_map/while/body/ppermute | solution.py:346
  719.5 34.9 %all-to-all-start = ((bf16[8,192,768]{2,1,0:T(8,128)(2,1)}), bf16[8,192,768]{2,1,0:T(8,128)(2,1)}, u32[]{:S(2)}, u32[]{:S(2)}) async-start(bf16[8,192,768]{2,1,0:T(8,128)(2,1)} %get-tuple-element.2739), calls=%async_computation | async-start | bytes 4718592 | tf_op jit(solution)/shard_map/while/body/all_to_all | solution.py:374
  732.9 25.9 %collective-permute-start.5 = (bf16[4,4,40704]{2,1,0:T(4,128)(2,1)}, bf16[4,4,40704]{2,1,0:T(4,128)(2,1)S(1)}, u32[]{:S(2)}, u32[]{:S(2)}) collective-permute-start(bf16[4,4,40704]{2,1,0:T(4,128)(2,1)} %pad_maximum_fusion.56), channel_id=1, source_target_pairs={{0,4},{4,0},{8,12},{12,8},{16,20},{20,16},{24,28},{28,24},{1,5},{5... | collective-permute-start | bytes 3907592 | tf_op jit(solution)/shard_map/while/body/ppermute | solution.py:346
  754.4 33.9 %all-to-all-start.1 = ((bf16[8,192,768]{2,1,0:T(8,128)(2,1)}), bf16[8,192,768]{2,1,0:T(8,128)(2,1)}, u32[]{:S(2)}, u32[]{:S(2)}) async-start(bf16[8,192,768]{2,1,0:T(8,128)(2,1)} %get-tuple-element.2740), calls=%async_computation.1 | async-start | bytes 4718592 | tf_op jit(solution)/shard_map/while/body/all_to_all | solution.py:374
  812.9 34.1 %all-to-all-start.9 = ((f32[8,2,192]{2,1,0:T(2,128)}), f32[8,2,192]{2,1,0:T(2,128)S(1)}, u32[]{:S(2)}, u32[]{:S(2)}) async-start(f32[8,2,192]{2,1,0:T(2,128)} %copy.216), calls=%async_computation.9 | async-start | bytes 32768 | tf_op jit(solution)/shard_map/all_to_all | solution.py:1202
  (108 other events, 1245.5 us)
Sparse Core Ops, SparseCore 0:
  10.5 89.9 all-gather.6
  166.2 85.7 all-gather.8
  350.5 324.2 all-reduce.8
  685.1 189.4 all-reduce.6

commit v4 on v3

--- a/solution.py
+++ b/solution.py
@@ -494,12 +494,12 @@
     return found
 
 
-def unpack(parts, edge, pieces):
+def unpack(parts, edge, pieces, most=STEPS):
     count, rows, columns = parts[0][0][0].shape
     each = len(parts[0][0])
     chunks = len(parts[0])
     total = rows * chunks
-    steps = max(1, min(STEPS, total // 48) // chunks)
+    steps = max(1, min(most, total // 48) // chunks)
     step = rows // steps
     share = columns // pieces
     width = share * count
@@ -935,7 +935,6 @@
     expand_own = [
         jnp.moveaxis(quarters[:, :, which], 0, 1).reshape(width, 4 * share) for which in range(2)
     ]
-    reduce_own = reduce_weight.astype(LOWER)
 
     fronts = []
     triples = []
@@ -947,7 +946,15 @@
         for which in range(2)
     ]
     for stage in range(3):
-        hiddens = [after(item, turns[stage + 1]) for item in hiddens]
+        waited = (turns[stage + 1], quarter) if stage else (turns[1],)
+        hiddens = [after(item, *waited) for item in hiddens]
+        if stage == 2:
+            d_seconds = [
+                (cotangents[which] * parts[which][5][:, None, :]).astype(LOWER)
+                for which in range(2)
+            ]
+            hiddens, d_seconds = together(hiddens, d_seconds)
+            d_seconds = [grow(d_seconds[which], orders[which][0]) for which in range(2)]
         hiddens = [grow(hiddens[which], orders[which][stage]) for which in range(2)]
     attend_own = arrange(turns, place_array)
     for which in range(2):
@@ -955,25 +962,23 @@
         fronts.append(front)
         triple = (project("rd,de->re", front, attend_own[which]) + triple_bias[which]).astype(LOWER)
         triples.append(triple.reshape(GROUP, slots, spans[which], 3 * share))
-    d_seconds = []
-    for which in range(2):
-        d_second = (cotangents[which] * parts[which][5][:, None, :]).astype(LOWER)
-        d_seconds.append(grow(after(d_second, *fronts), orders[which][0]))
     triples, d_seconds = together(triples, d_seconds)
     d_seconds = [grow(d_seconds[which], orders[which][1]) for which in range(2)]
     attended, *pieces = attend_forward(triples[0], triples[1], me_array, size, rows + extra)
     joint = spread(attended)
+    reduce_own = after(reduce_weight, attended).astype(LOWER)
     (joint, reduce_own), d_seconds = together([joint, reduce_own], d_seconds)
     d_seconds = [flat(grow(d_seconds[which], orders[which][2])) for which in range(2)]
-
     branch_one, middle_one, hidden_one, branch_two, middle_two, hidden_two = middle_stage(
         joint, output_full, output_bias_full, modulation, sources[0], sources[1]
     )
     branches = (branch_one, branch_two)
     middles = (middle_one, middle_two)
-    feeds = []
-    for which, hidden in enumerate((hidden_one, hidden_two)):
-        feeds.append(flat(collect(hidden, orders[which])))
+    feeds = [hidden_one, hidden_two]
+    for stage in range(2):
+        feeds = [grow(feeds[which], orders[which][stage]) for which in range(2)]
+    feeds, d_seconds, expand_own = together(feeds, d_seconds, expand_own)
+    feeds = [flat(grow(feeds[which], orders[which][2])) for which in range(2)]
 
     def halved(arrays, stage):
         found = []
@@ -1000,35 +1005,34 @@
         active = smooth_gelu(before).astype(LOWER)
         d_active = project("rd,fd->rf", d_seconds[which], reduce_own[which])
         d_before = jax.vjp(smooth_gelu, before)[1](d_active)[0].astype(LOWER)
-        d_hidden = project("rf,df->rd", d_before, expand_own[which]).astype(LOWER)
-        return active, d_before, by_device(d_hidden, which)
+        return active, d_before
 
     actives = []
     d_befores = []
-    d_hiddens = []
+    grads = []
     for which in range(2):
-        active, d_before, d_hidden = feed_forward(which)
+        active, d_before = feed_forward(which)
         actives.append(active)
         d_befores.append(d_before)
-        d_hiddens.append(d_hidden)
-    d_hiddens, actives, d_befores = together(d_hiddens, actives, d_befores)
-    expand_grads = [
-        project("rd,rf->df", feeds[which], d_befores[which])
-        .astype(LOWER)
-        .reshape(GROUP, share, 4 * share)
-        for which in range(2)
-    ]
-    reduce_grads = [
-        project("rf,rd->fd", actives[which], d_seconds[which])
-        .astype(LOWER)
-        .reshape(1, 4 * share, width)
-        for which in range(2)
-    ]
-    pairs, expand_grads, reduce_grads = together(halved(d_hiddens, 0), expand_grads, reduce_grads)
-    early_totals = lax.psum((*expand_grads, *reduce_grads), "rep")
+    for which in range(2):
+        grad = project("rd,rf->df", feeds[which], d_befores[which]).astype(LOWER)
+        grads.append(grad.reshape(GROUP, share, 4 * share))
+    for which in range(2):
+        grad = project("rf,rd->fd", actives[which], d_seconds[which]).astype(LOWER)
+        grads.append(grad.reshape(1, 4 * share, width))
+    grads, actives, d_befores = together(grads, actives, d_befores)
+    early_totals = lax.psum(tuple(grads), "rep")
     trips = jnp.minimum(jnp.abs(counts[0]) + 1, 1)
 
-    def chain(pairs, actives, d_befores):
+    def chain(actives, d_befores, d_seconds, raw):
+        pairs = []
+        for which in range(2):
+            d_hidden = project("rf,df->rd", d_befores[which], expand_own[which]).astype(LOWER)
+            pairs.append(by_device(d_hidden, which))
+        (pairs,) = together(halved(pairs, 0))
+        streams = (raw[0].astype(WIDE), padded(raw[1]).astype(WIDE))
+        pulls = (raw[2], padded(raw[3]))
+        cotangents = tuple(item.astype(WIDE) * alive for item in pulls)
         pairs = halved(summed(pairs), 1)
         pairs = halved(summed(pairs), 2)
         live = jnp.broadcast_to(alive, (slots, 1, width))
@@ -1137,26 +1141,34 @@
                     axis=-1,
                 )
             )
-        d_modulation = jnp.stack(d_mods, axis=1).astype(LOWER)
+        biases = (*attend_bias_grads, *output_bias_grads, *expand_bias_grads, *reduce_bias_grads)
+        biases = [item.astype(LOWER) for item in biases]
+        d_mods = [item.astype(LOWER) for item in d_mods]
+        return (attend_one, attend_two, *output_grads), d_mods, biases, outputs, input_grads
+
+    late, d_mods, biases, outputs, input_grads = once(
+        trips,
+        chain,
+        actives,
+        d_befores,
+        d_seconds,
+        (image, text, image_cotangent, text_cotangent),
+    )
+    late, d_mods, biases, early_totals = together(
+        list(late), list(d_mods), list(biases), list(early_totals)
+    )
+    late_totals = lax.psum(tuple(late), "rep")
+
+    keep = slots * 12 * width + cond_low.size + 4 * share
+
+    def finish(d_mods, biases, totals):
         packed = jnp.concatenate(
             [
-                d_modulation.reshape(-1),
+                jnp.stack(d_mods, axis=1).reshape(-1),
                 cond_low.reshape(-1),
-                *[item for item in attend_bias_grads],
-                *[item.astype(LOWER) for item in output_bias_grads],
-                *[item.astype(LOWER) for item in expand_bias_grads],
-                *[item.astype(LOWER) for item in reduce_bias_grads],
+                *biases,
             ]
         )
-        return (attend_one, attend_two, *output_grads), packed, outputs, input_grads
-
-    late, packed, outputs, input_grads = once(trips, chain, pairs, actives, d_befores)
-    late, packed, early_totals = together(list(late), [packed], list(early_totals))
-    late_totals = lax.psum(tuple(late), "rep")
-
-    keep = slots * 12 * width + cond_low.size + 4 * share
-
-    def finish(packed, totals):
         across = around(packed)
         every = across[None, :, :keep]
         expand_parts = []
@@ -1166,7 +1178,7 @@
                 expand_parts.append(spread(totals[stage]))
         return across[:, keep:], every, expand_parts
 
-    rest, every, expand_parts = once(trips, finish, packed[0], early_totals[:2])
+    rest, every, expand_parts = once(trips, finish, d_mods, biases, early_totals[:2])
     modulation_size = slots * 12 * width
     cond_size = cond_low.size
     keep = modulation_size + cond_size + 4 * share
@@ -1210,8 +1222,8 @@
         [condition_grad, adaptive_total, adaptive_bias_total, reduce_total, expand_total],
     )
     condition_grad, adaptive_total, adaptive_bias_total, reduce_total, expand_total = held
-    output_total = unpack([[(item.reshape(1, share, width),)] for item in late_totals[2:]], edge, 1)
-    attend_total = unpack([[(item,)] for item in late_totals[:2]], edge, 3)
+    output_total = jnp.stack(late_totals[2:]).astype(WIDE)
+    attend_total = unpack([[(item,)] for item in late_totals[:2]], edge, 3, 2)
     return (
         outputs[0],
         outputs[1][:, :extra],

time: 904 us -> 863 us (0.955)
  loops' own time: 28.3 us -> 9.17 us
  local copies, waits for them, and re-layouts: 112 us -> 97 us
    another operation x2, loops' own time: 28.3 us -> 9.17 us  [once(): return lax.fori_loop(0, trips, body, zeros)]
    pallas_call x4 -> x3, Pallas kernels: 29.3 us -> 21.8 us  [unpack(): pl.pallas_call(kernel, out_shape=jax.ShapeDtypeStruct((2, total, pieces *...]
  transfers between devices with their start and end apart: 65 -> 65, of which waited for: 33 -> 37; matrix products, arithmetic and copies ran while one was open for 33% -> 32% of each run, Pallas kernels for 10% -> 11%
where the time goes in v4:
time: 863 us; the launch traced here: 854 us
  waiting for transfers between devices  320 us (37%)
  other arithmetic  122 us (14%)
  matrix products  98.2 us (11%)
  Pallas kernels  97.9 us (11%)
  local copies, waits for them, and re-layouts  97 us (11%)
  starting transfers between devices  84.3 us (10%)
  between operations  15.9 us (2%)
  blocking collectives  10.7 us (1%)
  loops' own time  9.17 us (1%)
    ppermute x45, waiting for transfers between devices, swap(): lax.ppermute(array, 'shard', [(item, item ^ step) for item in range(GROUP)])  150 us
    dot_general x23, matrix products, project(): return jnp.einsum(form, left, right, preferred_element_type=WIDE)  98.2 us
    all_to_all x9, waiting for transfers between devices, spread(): lax.all_to_all(array, 'shard', split_axis=0, concat_axis=0, tiled=True)  90.5 us
    concatenate x27, other arithmetic, grow(): return jnp.concatenate([array, swap(array, step)], axis=0)  51 us
    all_to_all x9, starting transfers between devices, spread(): lax.all_to_all(array, 'shard', split_axis=0, concat_axis=0, tiled=True)  37.6 us
    ppermute x45, starting transfers between devices, swap(): lax.ppermute(array, 'shard', [(item, item ^ step) for item in range(GROUP)])  36.3 us
    psum x1, waiting for transfers between devices, split_body(): late_totals = lax.psum(tuple(late), 'rep')  34.2 us
    ppermute x3, waiting for transfers between devices, ring(): found.append(lax.ppermute(found[-1], 'rep', pairs))  29.3 us
  transfers between devices with their start and end apart: 65, of which 37 were waited for; matrix products, arithmetic and copies ran while one was open for 32% of the time, Pallas kernels for 11%

profile of v4, /device:TPU:0, one launch (start us, length us, event | category | flops | bytes accessed | tf_op | source)
XLA Modules:
  0.0 854.4 jit_solution(8071267411119594357)
XLA Ops:
  10.4 10.7 %all-gather.3 = bf16[8,2,3456]{2,1,0:T(2,128)(2,1)S(1)} all-gather(bf16[1,2,3456]{2,1,0:T(2,128)(2,1)S(1)} %bitcast.375), channel_id=2, replica_groups=mesh['shard'=8,'rep'=4] {'shard'}, dimensions={0}, use_global_device_ids=true | all-gather | bytes 124416 | tf_op jit(solution)/shard_map/all_gather | solution.py:903
  27.3 4.3 all-to-all-start.5
  31.8 6.1 fusion.44
  37.9 10.2 %all-to-all-done.5.refs_0_ = bf16[8,2,48,576]{3,2,1,0:T(8,128)(2,1)} async-done(((bf16[8,2,48,576]{3,2,1,0:T(8,128)(2,1)}), bf16[8,2,48,576]{3,2,1,0:T(8,128)(2,1)}, u32[]{:S(2)}, u32[]{:S(2)}) %all-to-all-start.5) | async-done | bytes 884768 | tf_op jit(solution)/shard_map/all_to_all | solution.py:374
  55.4 24.7 %collective-permute-done.30.refs_1_ = bf16[8,2,48,576]{3,2,1,0:T(8,128)(2,1)} collective-permute-done((bf16[8,2,48,576]{3,2,1,0:T(8,128)(2,1)}, bf16[8,2,48,576]{3,2,1,0:T(8,128)(2,1)}, u32[]{:S(2)}, u32[]{:S(2)}) %collective-permute-start.30) | collective-permute-done | bytes 884768 | tf_op jit(solution)/shard_map/ppermute | solution.py:493
  92.1 21.9 %collective-permute-done.31 = bf16[2,64,1536]{2,1,0:T(8,128)(2,1)S(1)} collective-permute-done((bf16[2,64,1536]{2,1,0:T(8,128)(2,1)S(1)}, bf16[2,64,1536]{2,1,0:T(8,128)(2,1)S(1)}, u32[]{:S(2)}, u32[]{:S(2)}) %collective-permute-start.31) | collective-permute-done | bytes 393248 | tf_op jit(solution)/shard_map/ppermute | solution.py:346
  123.5 13.6 %collective-permute-done.33 = bf16[4,64,1536]{2,1,0:T(8,128)(2,1)S(1)} collective-permute-done((bf16[4,64,1536]{2,1,0:T(8,128)(2,1)S(1)}, bf16[4,64,1536]{2,1,0:T(8,128)(2,1)S(1)}, u32[]{:S(2)}, u32[]{:S(2)}) %collective-permute-start.33) | collective-permute-done | bytes 786464 | tf_op jit(solution)/shard_map/ppermute | solution.py:346
  137.3 4.6 collective-permute-done.34.refs_3_
  150.6 5.2 collective-permute-done.39
  173.4 3.8 fusion.53
  182.1 10.8 %attend.1 = (bf16[8,2,144,192]{3,2,1,0:T(8,128)(2,1)}, bf16[8,2,64,192]{3,2,1,0:T(8,128)(2,1)}, bf16[8,2,80,192]{3,2,1,0:T(8,128)(2,1)}) custom-call(s32[1]{0:T(128)} %bitcast.4.refs_0_, bf16[8,2,64,576]{3,2,1,0:T(8,128)(2,1)} %bitcast.330, bf16[8,2,80,576]{3,2,1,0:T(8,128)(2,1)S(1)} %bitcast.327), custom_call_target="tpu_custom_call" | custom-call | flops 254803968 | bytes 3538944 | tf_op jit(solution)/shard_map/attend/pallas_call | solution.py:630
  192.9 4.3 all-to-all-start.8
  197.2 6.5 convert_element_type.681
  209.7 6.1 all-to-all-done.8.refs_0_
  218.7 12.6 %middle.1 = (f32[2,64,1536]{2,1,0:T(8,128)}, f32[2,64,1536]{2,1,0:T(8,128)}, bf16[2,64,1536]{2,1,0:T(8,128)(2,1)}, f32[2,80,1536]{2,1,0:T(8,128)}, f32[2,80,1536]{2,1,0:T(8,128)}, /*index=5*/bf16[2,80,1536]{2,1,0:T(8,128)(2,1)}) custom-call(bf16[8,2,144,192]{3,2,1,0:T(8,128)(2,1)} %all-to-all-done.8.refs_0_, bf16[8,2,192,1536]{3,2,1,0:T(8,128)(2,1)} %bitcast.316, ...), custom_call_target="tpu_custom_call" | custom-call | flops 1358954496 | bytes 13437184 | tf_op jit(solution)/shard_map/middle/pallas_call | solution.py:748
  233.3 9.2 %collective-permute-done.43 = bf16[2,64,1536]{2,1,0:T(8,128)(2,1)S(1)} collective-permute-done((bf16[2,64,1536]{2,1,0:T(8,128)(2,1)}, bf16[2,64,1536]{2,1,0:T(8,128)(2,1)S(1)}, u32[]{:S(2)}, u32[]{:S(2)}) %collective-permute-start.43) | collective-permute-done | bytes 393248 | tf_op jit(solution)/shard_map/ppermute | solution.py:346
  253.2 4.1 copy.129
  257.3 5.4 collective-permute-done.44
  264.0 5.5 collective-permute-done.46
  286.3 4.2 fusion.54
  290.5 4.1 fusion.52
  294.7 3.9 convolution_convert_fusion.11
  300.3 4.0 multiply_convert_fusion.2
  304.3 4.7 fusion.55
  309.0 5.5 fusion.42
  314.5 4.8 convolution_convert_fusion.13
  333.2 308.0 %while.67 = (s32[]{:T(128)}, bf16[8,192,576]{2,1,0:T(8,128)(2,1)}, bf16[8,192,576]{2,1,0:T(8,128)(2,1)}, bf16[192,1536]{1,0:T(8,128)(2,1)}, bf16[192,1536]{1,0:T...) while((s32[]{:T(128)}, bf16[8,192,576]{2,1,0:T(8,128)(2,1)}, ...), condition=%wide.region_28.29_spmd.clone, body=%wide.region_5.28_spmd.clone.sunk | while | flops 22458298368 | bytes 543878528 | solution.py:415
  333.6 6.4 convolution_convert_fusion.21
  355.9 13.6 %collective-permute-done.2 = bf16[4,64,1536]{2,1,0:T(8,128)(2,1)S(1)} collective-permute-done((bf16[4,64,1536]{2,1,0:T(8,128)(2,1)S(1)}, bf16[4,64,1536]{2,1,0:T(8,128)(2,1)S(1)}, u32[]{:S(2)}, u32[]{:S(2)}) %collective-permute-start.2) | collective-permute-done | bytes 786464 | tf_op jit(solution)/shard_map/while/body/ppermute | solution.py:346
  371.1 8.0 collective-permute-done.4
  381.6 3.9 convolution_convert_fusion.24
  387.1 5.7 collective-permute-done.5.refs_9_
  393.5 15.1 %back.5 = (f32[2,64,1536]{2,1,0:T(8,128)}, bf16[2,64,1536]{2,1,0:T(8,128)(2,1)}, f32[2,3,1536]{2,1,0:T(4,128)}, f32[2,80,1536]{2,1,0:T(8,128)}, bf16[2,80,1536]{...) custom-call(bf16[8,2,192,1536]{3,2,1,0:T(8,128)(2,1)} %get-tuple-element.2891.refs_0_, ...), custom_call_target="tpu_custom_call" | custom-call | flops 1358954496 | bytes 19437184 | tf_op jit(solution)/shard_map/while/body/back/pallas_call | solution.py:830
  408.6 4.4 all-to-all-start
  422.1 3.8 fusion.240
  425.9 4.1 all-to-all-done.refs_3_
  431.2 28.9 %attend_back.5 = (bf16[8,2,64,576]{3,2,1,0:T(8,128)(2,1)}, bf16[8,2,80,576]{3,2,1,0:T(8,128)(2,1)}) custom-call(s32[1]{0:T(128)} %get-tuple-element.2897.refs_0_, bf16[8,2,64,576]{3,2,1,0:T(8,128)(2,1)} %get-tuple-element.2898.refs_1_, bf16[8,2,80,576]{3,2,1,0:T(8,128)(2,1)} %copy-done.6, bf16[8,2,144,192]{3,2,1,0:T(8,128)(2,1)} %all-to-all-done.refs_3_), custom_call_target="tpu_custom_call" | custom-call | flops 637009920 | bytes 6193152 | tf_op jit(solution)/shard_map/while/body/attend_back/pallas_call | solution.py:665
  465.6 5.2 convolution_convert_fusion.23
  492.3 4.3 copy.200
  496.6 4.5 all-to-all-start.1
  501.9 3.9 copy.201
  506.2 3.9 pad_maximum_fusion.59
  510.1 4.4 pad_maximum_fusion.60
  514.6 11.7 %all-to-all-done.1 = bf16[8,192,576]{2,1,0:T(8,128)(2,1)} async-done(((bf16[8,192,576]{2,1,0:T(8,128)(2,1)}), bf16[8,192,576]{2,1,0:T(8,128)(2,1)}, u32[]{:S(2)}, u32[]{:S(2)}) %all-to-all-start.1) | async-done | bytes 1769504 | tf_op jit(solution)/shard_map/while/body/all_to_all | solution.py:374
  526.3 4.3 all-to-all-start.2
  548.5 7.9 all-to-all-done.2
  556.4 15.4 %collective-permute-done.14 = bf16[4,64,1536]{2,1,0:T(8,128)(2,1)} collective-permute-done((bf16[4,64,1536]{2,1,0:T(8,128)(2,1)}, bf16[4,64,1536]{2,1,0:T(8,128)(2,1)}, u32[]{:S(2)}, u32[]{:S(2)}) %collective-permute-start.14) | collective-permute-done | bytes 786464 | tf_op jit(solution)/shard_map/while/body/ppermute | solution.py:346
  571.8 4.3 collective-permute-done.15
  610.5 9.1 %collective-permute-done.20 = bf16[4,64,1536]{2,1,0:T(8,128)(2,1)S(1)} collective-permute-done((bf16[4,64,1536]{2,1,0:T(8,128)(2,1)S(1)}, bf16[4,64,1536]{2,1,0:T(8,128)(2,1)S(1)}, u32[]{:S(2)}, u32[]{:S(2)}) %collective-permute-start.20) | collective-permute-done | bytes 786464 | tf_op jit(solution)/shard_map/while/body/ppermute | solution.py:346
  622.9 7.4 collective-permute-done.22
  652.7 99.7 %while.68 = (s32[]{:T(128)}, bf16[4,2304]{1,0:T(4,128)(2,1)}, bf16[8,4,40704]{2,1,0:T(4,128)(2,1)}, bf16[8,192,768]{2,1,0:T(8,128)(2,1)}, bf16[8,192,768]{2,1,0:...) while((s32[]{:T(128)}, bf16[4,2304]{1,0:T(4,128)(2,1)}, ...), condition=%wide.wide.region_38.39_spmd, body=%wide.wide.region_37.38_spmd.sunk | while | flops 8325183 | bytes 37135528 | solution.py:415
  660.6 11.6 %collective-permute-done.25 = bf16[43008]{0:T(1024)(128)(2,1)S(1)} collective-permute-done((bf16[43008]{0:T(1024)(128)(2,1)S(1)}, bf16[43008]{0:T(1024)(128)(2,1)S(1)}, u32[]{:S(2)}, u32[]{:S(2)}) %collective-permute-start.25) | collective-permute-done | bytes 86048 | tf_op jit(solution)/shard_map/while/body/ppermute | solution.py:387
  676.3 5.5 collective-permute-done.27
  683.9 4.4 all-to-all-start.3
  688.3 6.3 collective-permute-done.28
  697.2 21.1 %all-to-all-done.3 = bf16[8,192,768]{2,1,0:T(8,128)(2,1)} async-done(((bf16[8,192,768]{2,1,0:T(8,128)(2,1)}), bf16[8,192,768]{2,1,0:T(8,128)(2,1)}, u32[]{:S(2)}, u32[]{:S(2)}) %all-to-all-start.3) | async-done | bytes 2359328 | tf_op jit(solution)/shard_map/while/body/all_to_all | solution.py:374
  718.3 4.4 all-to-all-start.4
  725.8 26.4 %all-to-all-done.4 = bf16[8,192,768]{2,1,0:T(8,128)(2,1)} async-done(((bf16[8,192,768]{2,1,0:T(8,128)(2,1)}), bf16[8,192,768]{2,1,0:T(8,128)(2,1)}, u32[]{:S(2)}, u32[]{:S(2)}) %all-to-all-start.4) | async-done | bytes 2359328 | tf_op jit(solution)/shard_map/while/body/all_to_all | solution.py:374
  764.7 7.2 fusion.69
  777.7 7.4 convolution_bitcast_fusion
  787.9 8.0 unpack.4
  795.9 8.0 unpack.3
  804.7 34.2 %all-reduce.9.cloned.1.call-done = (bf16[8,192,576]{2,1,0:T(8,128)(2,1)}, bf16[8,192,576]{2,1,0:T(8,128)(2,1)}, bf16[192,1536]{1,0:T(8,128)(2,1)}, bf16[192,1536]{1,0:T(8,128)(2,1)}) async-done(((bf16[8,192,576]{2,1,0:T(8,128)(2,1)}, bf16[8,192,576]{2,1,0:T(8,128)(2,1)}, bf16[192,1536]{1,0:T(8,128)(2,1)}, bf16[192,1536]{1,0:T(8,128)(2,1)}), (bf16[8,192,576]{2,1,0:T(8,128)(2,1)}, ...) | async-done | bytes 4718608 | tf_op jit(solution)/shard_map/psum | solution.py:1160
  841.7 5.7 unpack.5
  (513 shorter events, 298.0 us)
Async XLA Ops:
  7.2 138.1 %all-gather.7.cloned.1.call-start = ((), (), s32[]{:S(2)}) async-start(), calls=%async_computation.10 | async-start | bytes 10616832 | tf_op jit(solution)/shard_map/all_gather | solution.py:932
  27.3 20.9 %all-to-all-start.5 = ((bf16[8,2,48,576]{3,2,1,0:T(8,128)(2,1)}), bf16[8,2,48,576]{3,2,1,0:T(8,128)(2,1)}, u32[]{:S(2)}, u32[]{:S(2)}) async-start(bf16[8,2,48,576]{3,2,1,0:T(8,128)(2,1)} %pack.2), calls=%async_computation.5 | async-start | bytes 1966080 | tf_op jit(solution)/shard_map/all_to_all | solution.py:374
  49.9 33.2 %all-to-all-start.6 = ((f32[8,2,2,9216]{3,1,2,0:T(2,128)}), f32[8,2,2,9216]{3,1,2,0:T(2,128)S(1)}, u32[]{:S(2)}, u32[]{:S(2)}) async-start(f32[8,2,2,9216]{3,1,2,0:T(2,128)} %copy.122), calls=%async_computation.6 | async-start | bytes 2359296 | tf_op jit(solution)/shard_map/all_to_all | solution.py:374
  53.8 26.3 %collective-permute-start.30 = (bf16[8,2,48,576]{3,2,1,0:T(8,128)(2,1)}, bf16[8,2,48,576]{3,2,1,0:T(8,128)(2,1)}, u32[]{:S(2)}, u32[]{:S(2)}) collective-permute-start(bf16[8,2,48,576]{3,2,1,0:T(8,128)(2,1)} %all-to-all-done.5.refs_0_), channel_id=1, source_target_pairs={{0,1},{1,2},{2,3},{3,0},{4,5},{5,6},{6,7},{7,4},{8,9},{9,10},{10,1... | collective-permute-start | bytes 2654216 | tf_op jit(solution)/shard_map/ppermute | solution.py:493
  80.0 36.3 %collective-permute-start.32 = (bf16[8,2,48,576]{3,2,1,0:T(8,128)(2,1)}, bf16[8,2,48,576]{3,2,1,0:T(8,128)(2,1)}, u32[]{:S(2)}, u32[]{:S(2)}) collective-permute-start(bf16[8,2,48,576]{3,2,1,0:T(8,128)(2,1)} %collective-permute-done.30.refs_1_), channel_id=1, source_target_pairs={{0,1},{1,2},{2,3},{3,0},{4,5},{5,6},{6,7},{7,4},{8,9},{9,10},{10,1... | collective-permute-start | bytes 2654216 | tf_op jit(solution)/shard_map/ppermute | solution.py:493
  85.6 28.5 %collective-permute-start.35 = (bf16[2,80,1536]{2,1,0:T(8,128)(2,1)}, bf16[2,80,1536]{2,1,0:T(8,128)(2,1)}, u32[]{:S(2)}, u32[]{:S(2)}) collective-permute-start(bf16[2,80,1536]{2,1,0:T(8,128)(2,1)} %fusion.75), channel_id=1, source_target_pairs={{0,16},{4,20},{8,24},{12,28},{16,0},{20,4},{24,8},{28,12},{1,17},{... | collective-permute-start | bytes 1474568 | tf_op jit(solution)/shard_map/ppermute | solution.py:346
  86.2 31.8 %all-to-all-start.7 = ((bf16[8,2,48,768]{3,2,1,0:T(8,128)(2,1)}), bf16[8,2,48,768]{3,2,1,0:T(8,128)(2,1)S(1)}, u32[]{:S(2)}, u32[]{:S(2)}) async-start(bf16[8,2,48,768]{3,2,1,0:T(8,128)(2,1)} %pack.3), calls=%async_computation.7 | async-start | bytes 2359296 | tf_op jit(solution)/shard_map/all_to_all | solution.py:374
  89.8 181.2 %all-gather.9.cloned.1.call-start = ((), (), s32[]{:S(2)}) async-start(), calls=%async_computation.11 | async-start | bytes 5898240 | tf_op jit(solution)/shard_map/all_gather | solution.py:934
  90.1 23.9 %collective-permute-start.31 = (bf16[2,64,1536]{2,1,0:T(8,128)(2,1)S(1)}, bf16[2,64,1536]{2,1,0:T(8,128)(2,1)S(1)}, u32[]{:S(2)}, u32[]{:S(2)}) collective-permute-start(bf16[2,64,1536]{2,1,0:T(8,128)(2,1)S(1)} %fusion.81), channel_id=1, source_target_pairs={{0,8},{4,12},{8,0},{12,4},{16,24},{20,28},{24,16},{28,20},{1,9},{5... | collective-permute-start | bytes 1179656 | tf_op jit(solution)/shard_map/ppermute | solution.py:346
  116.3 25.6 %collective-permute-start.34 = (bf16[8,2,48,576]{3,2,1,0:T(8,128)(2,1)}, bf16[8,2,48,576]{3,2,1,0:T(8,128)(2,1)}, u32[]{:S(2)}, u32[]{:S(2)}) collective-permute-start(bf16[8,2,48,576]{3,2,1,0:T(8,128)(2,1)} %collective-permute-done.32.refs_2_), channel_id=1, source_target_pairs={{0,1},{1,2},{2,3},{3,0},{4,5},{5,6},{6,7},{7,4},{8,9},{9,10},{10,1... | collective-permute-start | bytes 2654216 | tf_op jit(solution)/shard_map/ppermute | solution.py:493
  118.0 23.9 %collective-permute-start.36 = (bf16[4,80,1536]{2,1,0:T(8,128)(2,1)}, bf16[4,80,1536]{2,1,0:T(8,128)(2,1)S(1)}, u32[]{:S(2)}, u32[]{:S(2)}) collective-permute-start(bf16[4,80,1536]{2,1,0:T(8,128)(2,1)} %pad_maximum_fusion.29), channel_id=1, source_target_pairs={{0,8},{4,12},{8,0},{12,4},{16,24},{20,28},{24,16},{28,20},{1,9},{5... | collective-permute-start | bytes 2949128 | tf_op jit(solution)/shard_map/ppermute | solution.py:346
  118.4 18.8 %collective-permute-start.33 = (bf16[4,64,1536]{2,1,0:T(8,128)(2,1)S(1)}, bf16[4,64,1536]{2,1,0:T(8,128)(2,1)S(1)}, u32[]{:S(2)}, u32[]{:S(2)}) collective-permute-start(bf16[4,64,1536]{2,1,0:T(8,128)(2,1)S(1)} %pad_maximum_fusion.32), channel_id=1, source_target_pairs={{0,16},{4,20},{8,24},{12,28},{16,0},{20,4},{24,8},{28,12},{1,17},{... | collective-permute-start | bytes 2359304 | tf_op jit(solution)/shard_map/ppermute | solution.py:346
  143.4 18.4 %collective-permute-start.37 = (bf16[8,64,1536]{2,1,0:T(8,128)(2,1)S(1)}, bf16[8,64,1536]{2,1,0:T(8,128)(2,1)}, u32[]{:S(2)}, u32[]{:S(2)}) collective-permute-start(bf16[8,64,1536]{2,1,0:T(8,128)(2,1)S(1)} %pad_maximum_fusion.26), channel_id=1, source_target_pairs={{0,4},{4,0},{8,12},{12,8},{16,20},{20,16},{24,28},{28,24},{1,5},{5... | collective-permute-start | bytes 4718600 | tf_op jit(solution)/shard_map/ppermute | solution.py:346
  143.4 25.5 %collective-permute-start.38 = (bf16[8,80,1536]{2,1,0:T(8,128)(2,1)}, bf16[8,80,1536]{2,1,0:T(8,128)(2,1)}, u32[]{:S(2)}, u32[]{:S(2)}) collective-permute-start(bf16[8,80,1536]{2,1,0:T(8,128)(2,1)} %pad_maximum_fusion.23), channel_id=1, source_target_pairs={{0,4},{4,0},{8,12},{12,8},{16,20},{20,16},{24,28},{28,24},{1,5},{5... | collective-permute-start | bytes 5898248 | tf_op jit(solution)/shard_map/ppermute | solution.py:346
  144.6 11.2 %collective-permute-start.39 = (bf16[2,64,1536]{2,1,0:T(8,128)(2,1)S(1)}, bf16[2,64,1536]{2,1,0:T(8,128)(2,1)}, u32[]{:S(2)}, u32[]{:S(2)}) collective-permute-start(bf16[2,64,1536]{2,1,0:T(8,128)(2,1)S(1)} %copy-done.45), channel_id=1, source_target_pairs={{0,8},{4,12},{8,0},{12,4},{16,24},{20,28},{24,16},{28,20},{1,9},{5... | collective-permute-start | bytes 1179656 | tf_op jit(solution)/shard_map/ppermute | solution.py:346
  145.5 13.2 %collective-permute-start.40 = (bf16[2,80,1536]{2,0,1:T(2,128)(2,1)}, bf16[2,80,1536]{2,0,1:T(2,128)(2,1)}, u32[]{:S(2)}, u32[]{:S(2)}) collective-permute-start(bf16[2,80,1536]{2,0,1:T(2,128)(2,1)} %multiply_convert_fusion.4), channel_id=1, source_target_pairs={{0,16},{4,20},{8,24},{12,28},{16,0},{20,4},{24,8},{28,12},{1,17},{... | collective-permute-start | bytes 1474568 | tf_op jit(solution)/shard_map/ppermute | solution.py:346
  179.1 24.6 %collective-permute-start.41 = (bf16[4,64,1536]{2,1,0:T(8,128)(2,1)S(1)}, bf16[4,64,1536]{2,1,0:T(8,128)(2,1)}, u32[]{:S(2)}, u32[]{:S(2)}) collective-permute-start(bf16[4,64,1536]{2,1,0:T(8,128)(2,1)S(1)} %pad_maximum_fusion.33), channel_id=1, source_target_pairs={{0,16},{4,20},{8,24},{12,28},{16,0},{20,4},{24,8},{28,12},{1,17},{... | collective-permute-start | bytes 2359304 | tf_op jit(solution)/shard_map/ppermute | solution.py:346
  180.6 25.6 %collective-permute-start.42 = (bf16[4,80,1536]{2,0,1:T(4,128)(2,1)}, bf16[4,80,1536]{2,0,1:T(4,128)(2,1)}, u32[]{:S(2)}, u32[]{:S(2)}) collective-permute-start(bf16[4,80,1536]{2,0,1:T(4,128)(2,1)} %pad_maximum_fusion.30), channel_id=1, source_target_pairs={{0,8},{4,12},{8,0},{12,4},{16,24},{20,28},{24,16},{28,20},{1,9},{5... | collective-permute-start | bytes 2949128 | tf_op jit(solution)/shard_map/ppermute | solution.py:346
  192.9 22.9 %all-to-all-start.8 = ((bf16[8,2,144,192]{3,2,1,0:T(8,128)(2,1)}), bf16[8,2,144,192]{3,2,1,0:T(8,128)(2,1)}, u32[]{:S(2)}, u32[]{:S(2)}) async-start(bf16[8,2,144,192]{3,2,1,0:T(8,128)(2,1)} %get-tuple-element.1160), calls=%async_computation.8 | async-start | bytes 2359296 | tf_op jit(solution)/shard_map/all_to_all | solution.py:374
  197.1 449.3 %all-reduce.11.cloned.1.call-start = ((), (), s32[]{:S(2)}) async-start(), calls=%async_computation.13 | async-start | bytes 18874368 | tf_op jit(solution)/shard_map/psum | solution.py:1024
  215.8 35.2 %collective-permute-start.48 = (bf16[8,80,1536]{2,0,1:T(8,128)(2,1)}, bf16[8,80,1536]{2,0,1:T(8,128)(2,1)}, u32[]{:S(2)}, u32[]{:S(2)}) collective-permute-start(bf16[8,80,1536]{2,0,1:T(8,128)(2,1)} %pad_maximum_fusion.24), channel_id=1, source_target_pairs={{0,4},{4,0},{8,12},{12,8},{16,20},{20,16},{24,28},{28,24},{1,5},{5... | collective-permute-start | bytes 5898248 | tf_op jit(solution)/shard_map/ppermute | solution.py:346
  215.8 31.7 %collective-permute-start.47 = (bf16[8,64,1536]{2,1,0:T(8,128)(2,1)}, bf16[8,64,1536]{2,1,0:T(8,128)(2,1)}, u32[]{:S(2)}, u32[]{:S(2)}) collective-permute-start(bf16[8,64,1536]{2,1,0:T(8,128)(2,1)} %pad_maximum_fusion.27), channel_id=1, source_target_pairs={{0,4},{4,0},{8,12},{12,8},{16,20},{20,16},{24,28},{28,24},{1,5},{5... | collective-permute-start | bytes 4718600 | tf_op jit(solution)/shard_map/ppermute | solution.py:346
  231.3 11.2 %collective-permute-start.43 = (bf16[2,64,1536]{2,1,0:T(8,128)(2,1)}, bf16[2,64,1536]{2,1,0:T(8,128)(2,1)S(1)}, u32[]{:S(2)}, u32[]{:S(2)}) collective-permute-start(bf16[2,64,1536]{2,1,0:T(8,128)(2,1)} %get-tuple-element.1165), channel_id=1, source_target_pairs={{0,8},{4,12},{8,0},{12,4},{16,24},{20,28},{24,16},{28,20},{1,9},{5... | collective-permute-start | bytes 1179656 | tf_op jit(solution)/shard_map/ppermute | solution.py:346
  232.8 13.4 %collective-permute-start.45 = (bf16[2,80,1536]{2,1,0:T(8,128)(2,1)}, bf16[2,80,1536]{2,1,0:T(8,128)(2,1)S(1)}, u32[]{:S(2)}, u32[]{:S(2)}) collective-permute-start(bf16[2,80,1536]{2,1,0:T(8,128)(2,1)} %get-tuple-element.1166), channel_id=1, source_target_pairs={{0,16},{4,20},{8,24},{12,28},{16,0},{20,4},{24,8},{28,12},{1,17},{... | collective-permute-start | bytes 1474568 | tf_op jit(solution)/shard_map/ppermute | solution.py:346
  243.6 19.1 %collective-permute-start.44 = (bf16[4,64,1536]{2,1,0:T(8,128)(2,1)S(1)}, bf16[4,64,1536]{2,1,0:T(8,128)(2,1)S(1)}, u32[]{:S(2)}, u32[]{:S(2)}) collective-permute-start(bf16[4,64,1536]{2,1,0:T(8,128)(2,1)S(1)} %pad_maximum_fusion.34), channel_id=1, source_target_pairs={{0,16},{4,20},{8,24},{12,28},{16,0},{20,4},{24,8},{28,12},{1,17},{... | collective-permute-start | bytes 2359304 | tf_op jit(solution)/shard_map/ppermute | solution.py:346
  247.3 22.2 %collective-permute-start.46 = (bf16[4,80,1536]{2,1,0:T(8,128)(2,1)S(1)}, bf16[4,80,1536]{2,1,0:T(8,128)(2,1)S(1)}, u32[]{:S(2)}, u32[]{:S(2)}) collective-permute-start(bf16[4,80,1536]{2,1,0:T(8,128)(2,1)S(1)} %pad_maximum_fusion.31), channel_id=1, source_target_pairs={{0,8},{4,12},{8,0},{12,4},{16,24},{20,28},{24,16},{28,20},{1,9},{5... | collective-permute-start | bytes 2949128 | tf_op jit(solution)/shard_map/ppermute | solution.py:346
  279.1 19.5 %collective-permute-start.50 = (bf16[8,80,1536]{2,1,0:T(8,128)(2,1)}, bf16[8,80,1536]{2,1,0:T(8,128)(2,1)S(1)}, u32[]{:S(2)}, u32[]{:S(2)}) collective-permute-start(bf16[8,80,1536]{2,1,0:T(8,128)(2,1)} %pad_maximum_fusion.25), channel_id=1, source_target_pairs={{0,4},{4,0},{8,12},{12,8},{16,20},{20,16},{24,28},{28,24},{1,5},{5... | collective-permute-start | bytes 5898248 | tf_op jit(solution)/shard_map/ppermute | solution.py:346
  319.4 519.5 %all-reduce.9.cloned.1.call-start = ((), (), s32[]{:S(2)}) async-start(), calls=%async_computation.12 | async-start | bytes 10223616 | tf_op jit(solution)/shard_map/psum | solution.py:1160
  340.3 9.1 %collective-permute-start.1 = (bf16[8,80,1536]{2,1,0:T(8,128)(2,1)S(1)}, bf16[8,80,1536]{2,1,0:T(8,128)(2,1)S(1)}, u32[]{:S(2)}, u32[]{:S(2)}) collective-permute-start(bf16[8,80,1536]{2,1,0:T(8,128)(2,1)S(1)} %bitcast.332), channel_id=1, source_target_pairs={{0,4},{4,0},{8,12},{12,8},{16,20},{20,16},{24,28},{28,24},{1,5},{5... | collective-permute-start | bytes 5898248 | tf_op jit(solution)/shard_map/while/body/ppermute | solution.py:346
  344.6 4.8 collective-permute-start
  349.9 19.6 %collective-permute-start.2 = (bf16[4,64,1536]{2,1,0:T(8,128)(2,1)S(1)}, bf16[4,64,1536]{2,1,0:T(8,128)(2,1)S(1)}, u32[]{:S(2)}, u32[]{:S(2)}) collective-permute-start(bf16[4,64,1536]{2,1,0:T(8,128)(2,1)S(1)} %slice.807), channel_id=1, source_target_pairs={{0,16},{4,20},{8,24},{12,28},{16,0},{20,4},{24,8},{28,12},{1,17},{... | collective-permute-start | bytes 2359304 | tf_op jit(solution)/shard_map/while/body/ppermute | solution.py:346
  352.1 237.5 %collective-permute-start.19 = (bf16[8,80,1536]{2,1,0:T(8,128)(2,1)}, bf16[8,80,1536]{2,1,0:T(8,128)(2,1)}, u32[]{:S(2)}, u32[]{:S(2)}) collective-permute-start(bf16[8,80,1536]{2,1,0:T(8,128)(2,1)} %bitcast.306), channel_id=1, source_target_pairs={{0,4},{4,0},{8,12},{12,8},{16,20},{20,16},{24,28},{28,24},{1,5},{5... | collective-permute-start | bytes 5898248 | tf_op jit(solution)/shard_map/while/body/ppermute | solution.py:346
  354.4 24.6 %collective-permute-start.4 = (bf16[4,80,1536]{2,1,0:T(8,128)(2,1)S(1)}, bf16[4,80,1536]{2,1,0:T(8,128)(2,1)S(1)}, u32[]{:S(2)}, u32[]{:S(2)}) collective-permute-start(bf16[4,80,1536]{2,1,0:T(8,128)(2,1)S(1)} %slice.808), channel_id=1, source_target_pairs={{0,8},{4,12},{8,0},{12,4},{16,24},{20,28},{24,16},{28,20},{1,9},{5... | collective-permute-start | bytes 2949128 | tf_op jit(solution)/shard_map/while/body/ppermute | solution.py:346
  370.5 16.6 %collective-permute-start.3 = (bf16[2,64,1536]{2,1,0:T(8,128)(2,1)S(1)}, bf16[2,64,1536]{2,1,0:T(8,128)(2,1)S(1)}, u32[]{:S(2)}, u32[]{:S(2)}) collective-permute-start(bf16[2,64,1536]{2,1,0:T(8,128)(2,1)S(1)} %get-tuple-element.2591), channel_id=1, source_target_pairs={{0,8},{4,12},{8,0},{12,4},{16,24},{20,28},{24,16},{28,20},{1,9},{5... | collective-permute-start | bytes 1179656 | tf_op jit(solution)/shard_map/while/body/ppermute | solution.py:346
  380.1 12.7 %collective-permute-start.5 = (bf16[2,80,1536]{2,1,0:T(8,128)(2,1)S(1)}, bf16[2,80,1536]{2,1,0:T(8,128)(2,1)}, u32[]{:S(2)}, u32[]{:S(2)}) collective-permute-start(bf16[2,80,1536]{2,1,0:T(8,128)(2,1)S(1)} %get-tuple-element.2596), channel_id=1, source_target_pairs={{0,16},{4,20},{8,24},{12,28},{16,0},{20,4},{24,8},{28,12},{1,17},{... | collective-permute-start | bytes 1474568 | tf_op jit(solution)/shard_map/while/body/ppermute | solution.py:346
  408.6 21.3 %all-to-all-start = ((bf16[8,2,144,192]{3,2,1,0:T(8,128)(2,1)}), bf16[8,2,144,192]{3,2,1,0:T(8,128)(2,1)}, u32[]{:S(2)}, u32[]{:S(2)}) async-start(bf16[8,2,144,192]{3,2,1,0:T(8,128)(2,1)} %get-tuple-element.2598), calls=%async_computation | async-start | bytes 2359296 | tf_op jit(solution)/shard_map/while/body/all_to_all | solution.py:374
  429.9 30.2 %collective-permute-start.6 = (bf16[2,64,1536]{2,1,0:T(8,128)(2,1)}, bf16[2,64,1536]{2,1,0:T(8,128)(2,1)}, u32[]{:S(2)}, u32[]{:S(2)}) collective-permute-start(bf16[2,64,1536]{2,1,0:T(8,128)(2,1)} %get-tuple-element.2604), channel_id=1, source_target_pairs={{0,8},{4,12},{8,0},{12,4},{16,24},{20,28},{24,16},{28,20},{1,9},{5... | collective-permute-start | bytes 1179656 | tf_op jit(solution)/shard_map/while/body/ppermute | solution.py:346
  430.5 31.0 %collective-permute-start.7 = (bf16[2,80,1536]{2,1,0:T(8,128)(2,1)S(1)}, bf16[2,80,1536]{2,1,0:T(8,128)(2,1)}, u32[]{:S(2)}, u32[]{:S(2)}) collective-permute-start(bf16[2,80,1536]{2,1,0:T(8,128)(2,1)S(1)} %copy-done.23), channel_id=1, source_target_pairs={{0,16},{4,20},{8,24},{12,28},{16,0},{20,4},{24,8},{28,12},{1,17},{... | collective-permute-start | bytes 1474568 | tf_op jit(solution)/shard_map/while/body/ppermute | solution.py:346
  462.6 22.9 %collective-permute-start.9 = (bf16[4,80,1536]{2,1,0:T(8,128)(2,1)S(1)}, bf16[4,80,1536]{2,1,0:T(8,128)(2,1)S(1)}, u32[]{:S(2)}, u32[]{:S(2)}) collective-permute-start(bf16[4,80,1536]{2,1,0:T(8,128)(2,1)S(1)} %pad_maximum_fusion.56), channel_id=1, source_target_pairs={{0,8},{4,12},{8,0},{12,4},{16,24},{20,28},{24,16},{28,20},{1,9},{5... | collective-permute-start | bytes 2949128 | tf_op jit(solution)/shard_map/while/body/ppermute | solution.py:346
  464.1 17.3 %collective-permute-start.8 = (bf16[4,64,1536]{2,1,0:T(8,128)(2,1)S(1)}, bf16[4,64,1536]{2,1,0:T(8,128)(2,1)S(1)}, u32[]{:S(2)}, u32[]{:S(2)}) collective-permute-start(bf16[4,64,1536]{2,1,0:T(8,128)(2,1)S(1)} %pad_maximum_fusion.55), channel_id=1, source_target_pairs={{0,16},{4,20},{8,24},{12,28},{16,0},{20,4},{24,8},{28,12},{1,17},{... | collective-permute-start | bytes 2359304 | tf_op jit(solution)/shard_map/while/body/ppermute | solution.py:346
  487.0 23.1 %collective-permute-start.11 = (bf16[8,80,1536]{2,1,0:T(8,128)(2,1)}, bf16[8,80,1536]{2,1,0:T(8,128)(2,1)}, u32[]{:S(2)}, u32[]{:S(2)}) collective-permute-start(bf16[8,80,1536]{2,1,0:T(8,128)(2,1)} %pad_maximum_fusion.58), channel_id=1, source_target_pairs={{0,4},{4,0},{8,12},{12,8},{16,20},{20,16},{24,28},{28,24},{1,5},{5... | collective-permute-start | bytes 5898248 | tf_op jit(solution)/shard_map/while/body/ppermute | solution.py:346
  487.0 18.8 %collective-permute-start.10 = (bf16[8,64,1536]{2,1,0:T(8,128)(2,1)}, bf16[8,64,1536]{2,1,0:T(8,128)(2,1)}, u32[]{:S(2)}, u32[]{:S(2)}) collective-permute-start(bf16[8,64,1536]{2,1,0:T(8,128)(2,1)} %pad_maximum_fusion.57), channel_id=1, source_target_pairs={{0,4},{4,0},{8,12},{12,8},{16,20},{20,16},{24,28},{28,24},{1,5},{5... | collective-permute-start | bytes 4718600 | tf_op jit(solution)/shard_map/while/body/ppermute | solution.py:346
  489.9 40.8 %collective-permute-start.13 = (bf16[8,80,1536]{2,1,0:T(8,128)(2,1)}, bf16[8,80,1536]{2,1,0:T(8,128)(2,1)}, u32[]{:S(2)}, u32[]{:S(2)}) collective-permute-start(bf16[8,80,1536]{2,1,0:T(8,128)(2,1)} %get-tuple-element.2618), channel_id=1, source_target_pairs={{0,4},{4,0},{8,12},{12,8},{16,20},{20,16},{24,28},{28,24},{1,5},{5... | collective-permute-start | bytes 5898248 | tf_op jit(solution)/shard_map/while/body/ppermute | solution.py:346
  491.8 38.9 %collective-permute-start.12 = (bf16[8,64,1536]{2,1,0:T(8,128)(2,1)}, bf16[8,64,1536]{2,1,0:T(8,128)(2,1)}, u32[]{:S(2)}, u32[]{:S(2)}) collective-permute-start(bf16[8,64,1536]{2,1,0:T(8,128)(2,1)} %get-tuple-element.2615), channel_id=1, source_target_pairs={{0,4},{4,0},{8,12},{12,8},{16,20},{20,16},{24,28},{28,24},{1,5},{5... | collective-permute-start | bytes 4718600 | tf_op jit(solution)/shard_map/while/body/ppermute | solution.py:346
  496.6 29.7 %all-to-all-start.1 = ((bf16[8,192,576]{2,1,0:T(8,128)(2,1)}), bf16[8,192,576]{2,1,0:T(8,128)(2,1)}, u32[]{:S(2)}, u32[]{:S(2)}) async-start(bf16[8,192,576]{2,1,0:T(8,128)(2,1)} %bitcast.297), calls=%async_computation.1 | async-start | bytes 3932160 | tf_op jit(solution)/shard_map/while/body/all_to_all | solution.py:374
  505.8 83.8 %collective-permute-start.18 = (bf16[8,64,1536]{2,1,0:T(8,128)(2,1)}, bf16[8,64,1536]{2,1,0:T(8,128)(2,1)}, u32[]{:S(2)}, u32[]{:S(2)}) collective-permute-start(bf16[8,64,1536]{2,1,0:T(8,128)(2,1)} %bitcast.335), channel_id=1, source_target_pairs={{0,4},{4,0},{8,12},{12,8},{16,20},{20,16},{24,28},{28,24},{1,5},{5... | collective-permute-start | bytes 4718600 | tf_op jit(solution)/shard_map/while/body/ppermute | solution.py:346
  526.3 30.1 %all-to-all-start.2 = ((bf16[8,192,576]{2,1,0:T(8,128)(2,1)}), bf16[8,192,576]{2,1,0:T(8,128)(2,1)}, u32[]{:S(2)}, u32[]{:S(2)}) async-start(bf16[8,192,576]{2,1,0:T(8,128)(2,1)} %bitcast.298), calls=%async_computation.2 | async-start | bytes 3932160 | tf_op jit(solution)/shard_map/while/body/all_to_all | solution.py:374
  534.8 41.3 %collective-permute-start.15 = (bf16[4,80,1536]{2,1,0:T(8,128)(2,1)}, bf16[4,80,1536]{2,1,0:T(8,128)(2,1)}, u32[]{:S(2)}, u32[]{:S(2)}) collective-permute-start(bf16[4,80,1536]{2,1,0:T(8,128)(2,1)} %get-tuple-element.2628), channel_id=1, source_target_pairs={{0,8},{4,12},{8,0},{12,4},{16,24},{20,28},{24,16},{28,20},{1,9},{5... | collective-permute-start | bytes 2949128 | tf_op jit(solution)/shard_map/while/body/ppermute | solution.py:346
  539.8 32.0 %collective-permute-start.14 = (bf16[4,64,1536]{2,1,0:T(8,128)(2,1)}, bf16[4,64,1536]{2,1,0:T(8,128)(2,1)}, u32[]{:S(2)}, u32[]{:S(2)}) collective-permute-start(bf16[4,64,1536]{2,1,0:T(8,128)(2,1)} %get-tuple-element.2624), channel_id=1, source_target_pairs={{0,16},{4,20},{8,24},{12,28},{16,0},{20,4},{24,8},{28,12},{1,17},{... | collective-permute-start | bytes 2359304 | tf_op jit(solution)/shard_map/while/body/ppermute | solution.py:346
  578.7 14.4 %collective-permute-start.17 = (bf16[2,80,1536]{2,1,0:T(8,128)(2,1)}, bf16[2,80,1536]{2,1,0:T(8,128)(2,1)}, u32[]{:S(2)}, u32[]{:S(2)}) collective-permute-start(bf16[2,80,1536]{2,1,0:T(8,128)(2,1)} %get-tuple-element.2642), channel_id=1, source_target_pairs={{0,16},{4,20},{8,24},{12,28},{16,0},{20,4},{24,8},{28,12},{1,17},{... | collective-permute-start | bytes 1474568 | tf_op jit(solution)/shard_map/while/body/ppermute | solution.py:346
  582.5 10.7 %collective-permute-start.16 = (bf16[2,64,1536]{2,1,0:T(8,128)(2,1)}, bf16[2,64,1536]{2,1,0:T(8,128)(2,1)}, u32[]{:S(2)}, u32[]{:S(2)}) collective-permute-start(bf16[2,64,1536]{2,1,0:T(8,128)(2,1)} %get-tuple-element.2638), channel_id=1, source_target_pairs={{0,8},{4,12},{8,0},{12,4},{16,24},{20,28},{24,16},{28,20},{1,9},{5... | collective-permute-start | bytes 1179656 | tf_op jit(solution)/shard_map/while/body/ppermute | solution.py:346
  598.5 22.1 %collective-permute-start.21 = (bf16[4,80,1536]{2,1,0:T(8,128)(2,1)S(1)}, bf16[4,80,1536]{2,1,0:T(8,128)(2,1)S(1)}, u32[]{:S(2)}, u32[]{:S(2)}) collective-permute-start(bf16[4,80,1536]{2,1,0:T(8,128)(2,1)S(1)} %get-tuple-element.2656), channel_id=1, source_target_pairs={{0,8},{4,12},{8,0},{12,4},{16,24},{20,28},{24,16},{28,20},{1,9},{5... | collective-permute-start | bytes 2949128 | tf_op jit(solution)/shard_map/while/body/ppermute | solution.py:346
  601.7 17.9 %collective-permute-start.20 = (bf16[4,64,1536]{2,1,0:T(8,128)(2,1)S(1)}, bf16[4,64,1536]{2,1,0:T(8,128)(2,1)S(1)}, u32[]{:S(2)}, u32[]{:S(2)}) collective-permute-start(bf16[4,64,1536]{2,1,0:T(8,128)(2,1)S(1)} %get-tuple-element.2652), channel_id=1, source_target_pairs={{0,16},{4,20},{8,24},{12,28},{16,0},{20,4},{24,8},{28,12},{1,17},{... | collective-permute-start | bytes 2359304 | tf_op jit(solution)/shard_map/while/body/ppermute | solution.py:346
  621.0 10.8 %collective-permute-start.23 = (bf16[2,80,1536]{2,1,0:T(8,128)(2,1)S(1)}, bf16[2,80,1536]{2,1,0:T(8,128)(2,1)S(1)}, u32[]{:S(2)}, u32[]{:S(2)}) collective-permute-start(bf16[2,80,1536]{2,1,0:T(8,128)(2,1)S(1)} %slice.810), channel_id=1, source_target_pairs={{0,16},{4,20},{8,24},{12,28},{16,0},{20,4},{24,8},{28,12},{1,17},{... | collective-permute-start | bytes 1474568 | tf_op jit(solution)/shard_map/while/body/ppermute | solution.py:346
  621.9 8.4 collective-permute-start.22
  653.0 7.5 collective-permute-start.24
  654.7 17.5 %collective-permute-start.25 = (bf16[43008]{0:T(1024)(128)(2,1)S(1)}, bf16[43008]{0:T(1024)(128)(2,1)S(1)}, u32[]{:S(2)}, u32[]{:S(2)}) collective-permute-start(bf16[43008]{0:T(1024)(128)(2,1)S(1)} %concatenate.208), channel_id=1, source_target_pairs={{0,2},{1,3},{2,0},{3,1},{4,6},{5,7},{6,4},{7,5},{8,10},{9,11},{10,... | collective-permute-start | bytes 258056 | tf_op jit(solution)/shard_map/while/body/ppermute | solution.py:387
  655.3 17.0 %collective-permute-start.26 = (bf16[43008]{0:T(1024)(128)(2,1)S(1)}, bf16[43008]{0:T(1024)(128)(2,1)S(1)}, u32[]{:S(2)}, u32[]{:S(2)}) collective-permute-start(bf16[43008]{0:T(1024)(128)(2,1)S(1)} %concatenate.208), channel_id=1, source_target_pairs={{0,1},{1,2},{2,3},{3,0},{4,5},{5,6},{6,7},{7,4},{8,9},{9,10},{10,1... | collective-permute-start | bytes 258056 | tf_op jit(solution)/shard_map/while/body/ppermute | solution.py:387
  674.7 7.1 collective-permute-start.27
  682.3 12.3 %collective-permute-start.28 = (bf16[2,4,40704]{2,1,0:T(4,128)(2,1)S(1)}, bf16[2,4,40704]{2,1,0:T(4,128)(2,1)S(1)}, u32[]{:S(2)}, u32[]{:S(2)}) collective-permute-start(bf16[2,4,40704]{2,1,0:T(4,128)(2,1)S(1)} %pad_maximum_fusion.65), channel_id=1, source_target_pairs={{0,16},{4,20},{8,24},{12,28},{16,0},{20,4},{24,8},{28,12},{1,17},{... | collective-permute-start | bytes 1953800 | tf_op jit(solution)/shard_map/while/body/ppermute | solution.py:346
  683.9 34.4 %all-to-all-start.3 = ((bf16[8,192,768]{2,1,0:T(8,128)(2,1)}), bf16[8,192,768]{2,1,0:T(8,128)(2,1)}, u32[]{:S(2)}, u32[]{:S(2)}) async-start(bf16[8,192,768]{2,1,0:T(8,128)(2,1)} %get-tuple-element.2743), calls=%async_computation.3 | async-start | bytes 4718592 | tf_op jit(solution)/shard_map/while/body/all_to_all | solution.py:374
  696.6 26.1 %collective-permute-start.29 = (bf16[4,4,40704]{2,1,0:T(4,128)(2,1)}, bf16[4,4,40704]{2,1,0:T(4,128)(2,1)S(1)}, u32[]{:S(2)}, u32[]{:S(2)}) collective-permute-start(bf16[4,4,40704]{2,1,0:T(4,128)(2,1)} %pad_maximum_fusion.66), channel_id=1, source_target_pairs={{0,4},{4,0},{8,12},{12,8},{16,20},{20,16},{24,28},{28,24},{1,5},{5... | collective-permute-start | bytes 3907592 | tf_op jit(solution)/shard_map/while/body/ppermute | solution.py:346
  718.3 33.8 %all-to-all-start.4 = ((bf16[8,192,768]{2,1,0:T(8,128)(2,1)}), bf16[8,192,768]{2,1,0:T(8,128)(2,1)}, u32[]{:S(2)}, u32[]{:S(2)}) async-start(bf16[8,192,768]{2,1,0:T(8,128)(2,1)} %get-tuple-element.2744), calls=%async_computation.4 | async-start | bytes 4718592 | tf_op jit(solution)/shard_map/while/body/all_to_all | solution.py:374
  772.5 31.4 %all-to-all-start.9 = ((f32[8,2,192]{2,1,0:T(2,128)}), f32[8,2,192]{2,1,0:T(2,128)S(1)}, u32[]{:S(2)}, u32[]{:S(2)}) async-start(f32[8,2,192]{2,1,0:T(2,128)} %copy.142), calls=%async_computation.9 | async-start | bytes 32768 | tf_op jit(solution)/shard_map/all_to_all | solution.py:1214
  (89 other events, 837.1 us)
Sparse Core Ops, SparseCore 0:
  10.5 85.7 all-gather.6
  145.4 88.6 all-gather.8
  319.5 325.0 all-reduce.10
  647.0 191.8 all-reduce.8

commit v5 on v4

--- a/solution.py
+++ b/solution.py
@@ -954,7 +954,7 @@
                 for which in range(2)
             ]
             hiddens, d_seconds = together(hiddens, d_seconds)
-            d_seconds = [grow(d_seconds[which], orders[which][0]) for which in range(2)]
+            swapped = [swap(d_seconds[which], orders[which][0]) for which in range(2)]
         hiddens = [grow(hiddens[which], orders[which][stage]) for which in range(2)]
     attend_own = arrange(turns, place_array)
     for which in range(2):
@@ -962,8 +962,11 @@
         fronts.append(front)
         triple = (project("rd,de->re", front, attend_own[which]) + triple_bias[which]).astype(LOWER)
         triples.append(triple.reshape(GROUP, slots, spans[which], 3 * share))
-    triples, d_seconds = together(triples, d_seconds)
-    d_seconds = [grow(d_seconds[which], orders[which][1]) for which in range(2)]
+    triples, swapped = together(triples, swapped)
+    d_seconds = [
+        grow(jnp.concatenate([d_seconds[which], swapped[which]], axis=0), orders[which][1])
+        for which in range(2)
+    ]
     attended, *pieces = attend_forward(triples[0], triples[1], me_array, size, rows + extra)
     joint = spread(attended)
     reduce_own = after(reduce_weight, attended).astype(LOWER)

time: 863 us -> 857 us (level)
  waiting for transfers between devices: 320 us -> 310 us
    concatenate x27 -> x25, other arithmetic: 51 us -> 49.1 us  [grow(): return jnp.concatenate([array, swap(array, step)], axis=0)]
  transfers between devices with their start and end apart: 65 -> 65, of which waited for: 37 -> 35; matrix products, arithmetic and copies ran while one was open for 32% -> 33% of each run, Pallas kernels for 11% -> 11%
where the time goes in v5:
time: 857 us; the launch traced here: 848 us
  waiting for transfers between devices  310 us (36%)
  other arithmetic  123 us (14%)
  Pallas kernels  98.2 us (11%)
  matrix products  98.2 us (11%)
  local copies, waits for them, and re-layouts  98 us (11%)
  starting transfers between devices  85 us (10%)
  between operations  15.9 us (2%)
  blocking collectives  10.7 us (1%)
  loops' own time  9.17 us (1%)
    ppermute x45, waiting for transfers between devices, swap(): lax.ppermute(array, 'shard', [(item, item ^ step) for item in range(GROUP)])  143 us
    dot_general x23, matrix products, project(): return jnp.einsum(form, left, right, preferred_element_type=WIDE)  98.2 us
    all_to_all x9, waiting for transfers between devices, spread(): lax.all_to_all(array, 'shard', split_axis=0, concat_axis=0, tiled=True)  90.7 us
    concatenate x25, other arithmetic, grow(): return jnp.concatenate([array, swap(array, step)], axis=0)  49.1 us
    all_to_all x9, starting transfers between devices, spread(): lax.all_to_all(array, 'shard', split_axis=0, concat_axis=0, tiled=True)  37.6 us
    ppermute x45, starting transfers between devices, swap(): lax.ppermute(array, 'shard', [(item, item ^ step) for item in range(GROUP)])  36.8 us
    psum x1, waiting for transfers between devices, split_body(): late_totals = lax.psum(tuple(late), 'rep')  34.3 us
    pallas_call x1, Pallas kernels, attend_backward(): pl.pallas_call(lambda *refs: attend_back_kernel(size, length, *refs), out...  29 us
  transfers between devices with their start and end apart: 65, of which 35 were waited for; matrix products, arithmetic and copies ran while one was open for 33% of the time, Pallas kernels for 11%

profile of v5, /device:TPU:0, one launch (start us, length us, event | category | flops | bytes accessed | tf_op | source)
XLA Modules:
  0.0 848.1 jit_solution(17839481865171063769)
XLA Ops:
  10.8 10.7 %all-gather.3 = bf16[8,2,3456]{2,1,0:T(2,128)(2,1)S(1)} all-gather(bf16[1,2,3456]{2,1,0:T(2,128)(2,1)S(1)} %bitcast.375), channel_id=2, replica_groups=mesh['shard'=8,'rep'=4] {'shard'}, dimensions={0}, use_global_device_ids=true | all-gather | bytes 124416 | tf_op jit(solution)/shard_map/all_gather | solution.py:903
  27.8 4.3 all-to-all-start.5
  32.4 6.1 fusion.44
  38.5 9.6 %all-to-all-done.5.refs_0_ = bf16[8,2,48,576]{3,2,1,0:T(8,128)(2,1)} async-done(((bf16[8,2,48,576]{3,2,1,0:T(8,128)(2,1)}), bf16[8,2,48,576]{3,2,1,0:T(8,128)(2,1)}, u32[]{:S(2)}, u32[]{:S(2)}) %all-to-all-start.5) | async-done | bytes 884768 | tf_op jit(solution)/shard_map/all_to_all | solution.py:374
  55.4 24.7 %collective-permute-done.30.refs_1_ = bf16[8,2,48,576]{3,2,1,0:T(8,128)(2,1)} collective-permute-done((bf16[8,2,48,576]{3,2,1,0:T(8,128)(2,1)}, bf16[8,2,48,576]{3,2,1,0:T(8,128)(2,1)}, u32[]{:S(2)}, u32[]{:S(2)}) %collective-permute-start.30) | collective-permute-done | bytes 884768 | tf_op jit(solution)/shard_map/ppermute | solution.py:493
  92.0 21.4 %collective-permute-done.31 = bf16[2,64,1536]{2,1,0:T(8,128)(2,1)S(1)} collective-permute-done((bf16[2,64,1536]{2,1,0:T(8,128)(2,1)S(1)}, bf16[2,64,1536]{2,1,0:T(8,128)(2,1)S(1)}, u32[]{:S(2)}, u32[]{:S(2)}) %collective-permute-start.31) | collective-permute-done | bytes 393248 | tf_op jit(solution)/shard_map/ppermute | solution.py:346
  122.6 14.7 %collective-permute-done.33 = bf16[4,64,1536]{2,1,0:T(8,128)(2,1)S(1)} collective-permute-done((bf16[4,64,1536]{2,1,0:T(8,128)(2,1)}, bf16[4,64,1536]{2,1,0:T(8,128)(2,1)S(1)}, u32[]{:S(2)}, u32[]{:S(2)}) %collective-permute-start.33) | collective-permute-done | bytes 786464 | tf_op jit(solution)/shard_map/ppermute | solution.py:346
  162.2 3.8 fusion.53
  174.9 10.8 %attend.1 = (bf16[8,2,144,192]{3,2,1,0:T(8,128)(2,1)}, bf16[8,2,64,192]{3,2,1,0:T(8,128)(2,1)}, bf16[8,2,80,192]{3,2,1,0:T(8,128)(2,1)}) custom-call(s32[1]{0:T(128)} %bitcast.4.refs_0_, bf16[8,2,64,576]{3,2,1,0:T(8,128)(2,1)} %bitcast.330, bf16[8,2,80,576]{3,2,1,0:T(8,128)(2,1)S(1)} %bitcast.327), custom_call_target="tpu_custom_call" | custom-call | flops 254803968 | bytes 3538944 | tf_op jit(solution)/shard_map/attend/pallas_call | solution.py:630
  185.6 4.3 all-to-all-start.8
  190.0 6.5 convert_element_type.681
  199.0 4.2 pad_maximum_fusion.24
  203.2 7.0 all-to-all-done.8.refs_0_
  213.0 12.6 %middle.1 = (f32[2,64,1536]{2,1,0:T(8,128)}, f32[2,64,1536]{2,1,0:T(8,128)}, bf16[2,64,1536]{2,1,0:T(8,128)(2,1)}, f32[2,80,1536]{2,1,0:T(8,128)}, f32[2,80,1536]{2,1,0:T(8,128)}, /*index=5*/bf16[2,80,1536]{2,1,0:T(8,128)(2,1)}) custom-call(bf16[8,2,144,192]{3,2,1,0:T(8,128)(2,1)} %all-to-all-done.8.refs_0_, bf16[8,2,192,1536]{3,2,1,0:T(8,128)(2,1)} %bitcast.316, ...), custom_call_target="tpu_custom_call" | custom-call | flops 1358954496 | bytes 13437184 | tf_op jit(solution)/shard_map/middle/pallas_call | solution.py:748
  227.6 9.2 %collective-permute-done.43 = bf16[2,64,1536]{2,1,0:T(8,128)(2,1)S(1)} collective-permute-done((bf16[2,64,1536]{2,1,0:T(8,128)(2,1)}, bf16[2,64,1536]{2,1,0:T(8,128)(2,1)S(1)}, u32[]{:S(2)}, u32[]{:S(2)}) %collective-permute-start.43) | collective-permute-done | bytes 393248 | tf_op jit(solution)/shard_map/ppermute | solution.py:346
  247.8 4.1 copy.129
  251.9 4.6 collective-permute-done.44
  257.9 5.0 collective-permute-done.46
  279.6 4.2 fusion.54
  283.8 4.1 fusion.52
  288.0 3.9 convolution_convert_fusion.11
  293.6 4.0 multiply_convert_fusion.2
  297.7 4.6 fusion.55
  302.3 5.5 fusion.42
  307.9 4.8 convolution_convert_fusion.13
  326.5 309.1 %while.67 = (s32[]{:T(128)}, bf16[8,192,576]{2,1,0:T(8,128)(2,1)}, bf16[8,192,576]{2,1,0:T(8,128)(2,1)}, bf16[192,1536]{1,0:T(8,128)(2,1)}, bf16[192,1536]{1,0:T...) while((s32[]{:T(128)}, bf16[8,192,576]{2,1,0:T(8,128)(2,1)}, ...), condition=%wide.region_28.29_spmd.clone, body=%wide.region_5.28_spmd.clone.sunk | while | flops 22458298368 | bytes 543878528 | solution.py:415
  326.9 6.4 convolution_convert_fusion.21
  349.5 13.3 %collective-permute-done.2 = bf16[4,64,1536]{2,1,0:T(8,128)(2,1)S(1)} collective-permute-done((bf16[4,64,1536]{2,1,0:T(8,128)(2,1)S(1)}, bf16[4,64,1536]{2,1,0:T(8,128)(2,1)S(1)}, u32[]{:S(2)}, u32[]{:S(2)}) %collective-permute-start.2) | collective-permute-done | bytes 786464 | tf_op jit(solution)/shard_map/while/body/ppermute | solution.py:346
  365.4 7.9 collective-permute-done.4
  374.9 3.9 convolution_convert_fusion.24
  381.3 5.7 collective-permute-done.5.refs_9_
  387.7 15.2 %back.5 = (f32[2,64,1536]{2,1,0:T(8,128)}, bf16[2,64,1536]{2,1,0:T(8,128)(2,1)}, f32[2,3,1536]{2,1,0:T(4,128)}, f32[2,80,1536]{2,1,0:T(8,128)}, bf16[2,80,1536]{...) custom-call(bf16[8,2,192,1536]{3,2,1,0:T(8,128)(2,1)} %get-tuple-element.2891.refs_0_, ...), custom_call_target="tpu_custom_call" | custom-call | flops 1358954496 | bytes 19437184 | tf_op jit(solution)/shard_map/while/body/back/pallas_call | solution.py:830
  403.0 4.4 all-to-all-start
  416.4 3.9 fusion.240
  420.4 3.9 all-to-all-done.refs_3_
  425.5 29.0 %attend_back.5 = (bf16[8,2,64,576]{3,2,1,0:T(8,128)(2,1)}, bf16[8,2,80,576]{3,2,1,0:T(8,128)(2,1)}) custom-call(s32[1]{0:T(128)} %get-tuple-element.2897.refs_0_, bf16[8,2,64,576]{3,2,1,0:T(8,128)(2,1)} %get-tuple-element.2898.refs_1_, bf16[8,2,80,576]{3,2,1,0:T(8,128)(2,1)} %copy-done.6, bf16[8,2,144,192]{3,2,1,0:T(8,128)(2,1)} %all-to-all-done.refs_3_), custom_call_target="tpu_custom_call" | custom-call | flops 637009920 | bytes 6193152 | tf_op jit(solution)/shard_map/while/body/attend_back/pallas_call | solution.py:665
  460.0 5.2 convolution_convert_fusion.23
  486.6 4.3 copy.200
  490.9 4.5 all-to-all-start.1
  496.2 3.9 copy.201
  500.5 3.9 pad_maximum_fusion.59
  504.4 4.4 pad_maximum_fusion.60
  508.9 11.8 %all-to-all-done.1 = bf16[8,192,576]{2,1,0:T(8,128)(2,1)} async-done(((bf16[8,192,576]{2,1,0:T(8,128)(2,1)}), bf16[8,192,576]{2,1,0:T(8,128)(2,1)}, u32[]{:S(2)}, u32[]{:S(2)}) %all-to-all-start.1) | async-done | bytes 1769504 | tf_op jit(solution)/shard_map/while/body/all_to_all | solution.py:374
  520.6 4.3 all-to-all-start.2
  542.9 7.9 all-to-all-done.2
  550.8 15.4 %collective-permute-done.14 = bf16[4,64,1536]{2,1,0:T(8,128)(2,1)} collective-permute-done((bf16[4,64,1536]{2,1,0:T(8,128)(2,1)}, bf16[4,64,1536]{2,1,0:T(8,128)(2,1)}, u32[]{:S(2)}, u32[]{:S(2)}) %collective-permute-start.14) | collective-permute-done | bytes 786464 | tf_op jit(solution)/shard_map/while/body/ppermute | solution.py:346
  566.1 4.3 collective-permute-done.15
  604.9 9.2 %collective-permute-done.20 = bf16[4,64,1536]{2,1,0:T(8,128)(2,1)S(1)} collective-permute-done((bf16[4,64,1536]{2,1,0:T(8,128)(2,1)S(1)}, bf16[4,64,1536]{2,1,0:T(8,128)(2,1)S(1)}, u32[]{:S(2)}, u32[]{:S(2)}) %collective-permute-start.20) | collective-permute-done | bytes 786464 | tf_op jit(solution)/shard_map/while/body/ppermute | solution.py:346
  617.3 7.3 collective-permute-done.22
  647.0 99.0 %while.68 = (s32[]{:T(128)}, bf16[4,2304]{1,0:T(4,128)(2,1)}, bf16[8,4,40704]{2,1,0:T(4,128)(2,1)}, bf16[8,192,768]{2,1,0:T(8,128)(2,1)}, bf16[8,192,768]{2,1,0:...) while((s32[]{:T(128)}, bf16[4,2304]{1,0:T(4,128)(2,1)}, ...), condition=%wide.wide.region_38.39_spmd, body=%wide.wide.region_37.38_spmd.sunk | while | flops 8325183 | bytes 37135528 | solution.py:415
  651.4 4.0 collective-permute-done.24
  655.5 10.3 %collective-permute-done.25 = bf16[43008]{0:T(1024)(128)(2,1)S(1)} collective-permute-done((bf16[43008]{0:T(1024)(128)(2,1)S(1)}, bf16[43008]{0:T(1024)(128)(2,1)S(1)}, u32[]{:S(2)}, u32[]{:S(2)}) %collective-permute-start.25) | collective-permute-done | bytes 86048 | tf_op jit(solution)/shard_map/while/body/ppermute | solution.py:387
  669.9 5.5 collective-permute-done.27
  677.5 4.4 all-to-all-start.3
  681.9 6.3 collective-permute-done.28
  690.8 21.1 %all-to-all-done.3 = bf16[8,192,768]{2,1,0:T(8,128)(2,1)} async-done(((bf16[8,192,768]{2,1,0:T(8,128)(2,1)}), bf16[8,192,768]{2,1,0:T(8,128)(2,1)}, u32[]{:S(2)}, u32[]{:S(2)}) %all-to-all-start.3) | async-done | bytes 2359328 | tf_op jit(solution)/shard_map/while/body/all_to_all | solution.py:374
  711.9 4.4 all-to-all-start.4
  719.4 26.4 %all-to-all-done.4 = bf16[8,192,768]{2,1,0:T(8,128)(2,1)} async-done(((bf16[8,192,768]{2,1,0:T(8,128)(2,1)}), bf16[8,192,768]{2,1,0:T(8,128)(2,1)}, u32[]{:S(2)}, u32[]{:S(2)}) %all-to-all-start.4) | async-done | bytes 2359328 | tf_op jit(solution)/shard_map/while/body/all_to_all | solution.py:374
  758.3 7.2 fusion.69
  771.3 7.4 convolution_bitcast_fusion
  781.5 8.0 unpack.4
  789.5 8.0 unpack.3
  798.3 34.3 %all-reduce.9.cloned.1.call-done = (bf16[8,192,576]{2,1,0:T(8,128)(2,1)}, bf16[8,192,576]{2,1,0:T(8,128)(2,1)}, bf16[192,1536]{1,0:T(8,128)(2,1)}, bf16[192,1536]{1,0:T(8,128)(2,1)}) async-done(((bf16[8,192,576]{2,1,0:T(8,128)(2,1)}, bf16[8,192,576]{2,1,0:T(8,128)(2,1)}, bf16[192,1536]{1,0:T(8,128)(2,1)}, bf16[192,1536]{1,0:T(8,128)(2,1)}), (bf16[8,192,576]{2,1,0:T(8,128)(2,1)}, ...) | async-done | bytes 4718608 | tf_op jit(solution)/shard_map/psum | solution.py:1163
  835.3 5.7 unpack.5
  (517 shorter events, 295.4 us)
Async XLA Ops:
  7.2 136.7 %all-gather.7.cloned.1.call-start = ((), (), s32[]{:S(2)}) async-start(), calls=%async_computation.10 | async-start | bytes 10616832 | tf_op jit(solution)/shard_map/all_gather | solution.py:932
  27.8 20.3 %all-to-all-start.5 = ((bf16[8,2,48,576]{3,2,1,0:T(8,128)(2,1)}), bf16[8,2,48,576]{3,2,1,0:T(8,128)(2,1)}, u32[]{:S(2)}, u32[]{:S(2)}) async-start(bf16[8,2,48,576]{3,2,1,0:T(8,128)(2,1)} %pack.2), calls=%async_computation.5 | async-start | bytes 1966080 | tf_op jit(solution)/shard_map/all_to_all | solution.py:374
  49.9 33.2 %all-to-all-start.6 = ((f32[8,2,2,9216]{3,1,2,0:T(2,128)}), f32[8,2,2,9216]{3,1,2,0:T(2,128)S(1)}, u32[]{:S(2)}, u32[]{:S(2)}) async-start(f32[8,2,2,9216]{3,1,2,0:T(2,128)} %copy.122), calls=%async_computation.6 | async-start | bytes 2359296 | tf_op jit(solution)/shard_map/all_to_all | solution.py:374
  53.8 26.3 %collective-permute-start.30 = (bf16[8,2,48,576]{3,2,1,0:T(8,128)(2,1)}, bf16[8,2,48,576]{3,2,1,0:T(8,128)(2,1)}, u32[]{:S(2)}, u32[]{:S(2)}) collective-permute-start(bf16[8,2,48,576]{3,2,1,0:T(8,128)(2,1)} %all-to-all-done.5.refs_0_), channel_id=1, source_target_pairs={{0,1},{1,2},{2,3},{3,0},{4,5},{5,6},{6,7},{7,4},{8,9},{9,10},{10,1... | collective-permute-start | bytes 2654216 | tf_op jit(solution)/shard_map/ppermute | solution.py:493
  80.0 36.3 %collective-permute-start.32 = (bf16[8,2,48,576]{3,2,1,0:T(8,128)(2,1)}, bf16[8,2,48,576]{3,2,1,0:T(8,128)(2,1)}, u32[]{:S(2)}, u32[]{:S(2)}) collective-permute-start(bf16[8,2,48,576]{3,2,1,0:T(8,128)(2,1)} %collective-permute-done.30.refs_1_), channel_id=1, source_target_pairs={{0,1},{1,2},{2,3},{3,0},{4,5},{5,6},{6,7},{7,4},{8,9},{9,10},{10,1... | collective-permute-start | bytes 2654216 | tf_op jit(solution)/shard_map/ppermute | solution.py:493
  84.8 29.5 %collective-permute-start.35 = (bf16[2,80,1536]{2,1,0:T(8,128)(2,1)S(1)}, bf16[2,80,1536]{2,1,0:T(8,128)(2,1)}, u32[]{:S(2)}, u32[]{:S(2)}) collective-permute-start(bf16[2,80,1536]{2,1,0:T(8,128)(2,1)S(1)} %fusion.75), channel_id=1, source_target_pairs={{0,16},{4,20},{8,24},{12,28},{16,0},{20,4},{24,8},{28,12},{1,17},{... | collective-permute-start | bytes 1474568 | tf_op jit(solution)/shard_map/ppermute | solution.py:346
  85.4 32.6 %all-to-all-start.7 = ((bf16[8,2,48,768]{3,2,1,0:T(8,128)(2,1)}), bf16[8,2,48,768]{3,2,1,0:T(8,128)(2,1)S(1)}, u32[]{:S(2)}, u32[]{:S(2)}) async-start(bf16[8,2,48,768]{3,2,1,0:T(8,128)(2,1)} %pack.3), calls=%async_computation.7 | async-start | bytes 2359296 | tf_op jit(solution)/shard_map/all_to_all | solution.py:374
  89.0 175.3 %all-gather.9.cloned.1.call-start = ((), (), s32[]{:S(2)}) async-start(), calls=%async_computation.11 | async-start | bytes 5898240 | tf_op jit(solution)/shard_map/all_gather | solution.py:934
  89.4 23.9 %collective-permute-start.31 = (bf16[2,64,1536]{2,1,0:T(8,128)(2,1)S(1)}, bf16[2,64,1536]{2,1,0:T(8,128)(2,1)S(1)}, u32[]{:S(2)}, u32[]{:S(2)}) collective-permute-start(bf16[2,64,1536]{2,1,0:T(8,128)(2,1)S(1)} %fusion.81), channel_id=1, source_target_pairs={{0,8},{4,12},{8,0},{12,4},{16,24},{20,28},{24,16},{28,20},{1,9},{5... | collective-permute-start | bytes 1179656 | tf_op jit(solution)/shard_map/ppermute | solution.py:346
  116.3 25.6 %collective-permute-start.34 = (bf16[8,2,48,576]{3,2,1,0:T(8,128)(2,1)}, bf16[8,2,48,576]{3,2,1,0:T(8,128)(2,1)}, u32[]{:S(2)}, u32[]{:S(2)}) collective-permute-start(bf16[8,2,48,576]{3,2,1,0:T(8,128)(2,1)} %collective-permute-done.32.refs_2_), channel_id=1, source_target_pairs={{0,1},{1,2},{2,3},{3,0},{4,5},{5,6},{6,7},{7,4},{8,9},{9,10},{10,1... | collective-permute-start | bytes 2654216 | tf_op jit(solution)/shard_map/ppermute | solution.py:493
  118.0 23.9 %collective-permute-start.36 = (bf16[4,80,1536]{2,1,0:T(8,128)(2,1)}, bf16[4,80,1536]{2,1,0:T(8,128)(2,1)S(1)}, u32[]{:S(2)}, u32[]{:S(2)}) collective-permute-start(bf16[4,80,1536]{2,1,0:T(8,128)(2,1)} %pad_maximum_fusion.29), channel_id=1, source_target_pairs={{0,8},{4,12},{8,0},{12,4},{16,24},{20,28},{24,16},{28,20},{1,9},{5... | collective-permute-start | bytes 2949128 | tf_op jit(solution)/shard_map/ppermute | solution.py:346
  118.4 19.0 %collective-permute-start.33 = (bf16[4,64,1536]{2,1,0:T(8,128)(2,1)}, bf16[4,64,1536]{2,1,0:T(8,128)(2,1)S(1)}, u32[]{:S(2)}, u32[]{:S(2)}) collective-permute-start(bf16[4,64,1536]{2,1,0:T(8,128)(2,1)} %pad_maximum_fusion.32), channel_id=1, source_target_pairs={{0,16},{4,20},{8,24},{12,28},{16,0},{20,4},{24,8},{28,12},{1,17},{... | collective-permute-start | bytes 2359304 | tf_op jit(solution)/shard_map/ppermute | solution.py:346
  143.4 7.2 collective-permute-start.37
  143.4 14.2 %collective-permute-start.38 = (bf16[8,80,1536]{2,1,0:T(8,128)(2,1)}, bf16[8,80,1536]{2,1,0:T(8,128)(2,1)}, u32[]{:S(2)}, u32[]{:S(2)}) collective-permute-start(bf16[8,80,1536]{2,1,0:T(8,128)(2,1)} %pad_maximum_fusion.23), channel_id=1, source_target_pairs={{0,4},{4,0},{8,12},{12,8},{16,20},{20,16},{24,28},{28,24},{1,5},{5... | collective-permute-start | bytes 5898248 | tf_op jit(solution)/shard_map/ppermute | solution.py:346
  148.5 19.4 %collective-permute-start.40 = (bf16[2,80,1536]{2,0,1:T(2,128)(2,1)S(1)}, bf16[2,80,1536]{2,0,1:T(2,128)(2,1)}, u32[]{:S(2)}, u32[]{:S(2)}) collective-permute-start(bf16[2,80,1536]{2,0,1:T(2,128)(2,1)S(1)} %multiply_convert_fusion.4), channel_id=1, source_target_pairs={{0,16},{4,20},{8,24},{12,28},{16,0},{20,4},{24,8},{28,12},{1,17},{... | collective-permute-start | bytes 1474568 | tf_op jit(solution)/shard_map/ppermute | solution.py:346
  150.0 17.9 %collective-permute-start.39 = (bf16[2,64,1536]{2,1,0:T(8,128)(2,1)S(1)}, bf16[2,64,1536]{2,1,0:T(8,128)(2,1)}, u32[]{:S(2)}, u32[]{:S(2)}) collective-permute-start(bf16[2,64,1536]{2,1,0:T(8,128)(2,1)S(1)} %multiply_convert_fusion.5), channel_id=1, source_target_pairs={{0,8},{4,12},{8,0},{12,4},{16,24},{20,28},{24,16},{28,20},{1,9},{5... | collective-permute-start | bytes 1179656 | tf_op jit(solution)/shard_map/ppermute | solution.py:346
  169.8 26.6 %collective-permute-start.41 = (bf16[4,64,1536]{2,1,0:T(8,128)(2,1)}, bf16[4,64,1536]{2,1,0:T(8,128)(2,1)}, u32[]{:S(2)}, u32[]{:S(2)}) collective-permute-start(bf16[4,64,1536]{2,1,0:T(8,128)(2,1)} %pad_maximum_fusion.33), channel_id=1, source_target_pairs={{0,16},{4,20},{8,24},{12,28},{16,0},{20,4},{24,8},{28,12},{1,17},{... | collective-permute-start | bytes 2359304 | tf_op jit(solution)/shard_map/ppermute | solution.py:346
  173.4 25.5 %collective-permute-start.42 = (bf16[4,80,1536]{2,0,1:T(4,128)(2,1)}, bf16[4,80,1536]{2,0,1:T(4,128)(2,1)}, u32[]{:S(2)}, u32[]{:S(2)}) collective-permute-start(bf16[4,80,1536]{2,0,1:T(4,128)(2,1)} %pad_maximum_fusion.30), channel_id=1, source_target_pairs={{0,8},{4,12},{8,0},{12,4},{16,24},{20,28},{24,16},{28,20},{1,9},{5... | collective-permute-start | bytes 2949128 | tf_op jit(solution)/shard_map/ppermute | solution.py:346
  185.6 24.5 %all-to-all-start.8 = ((bf16[8,2,144,192]{3,2,1,0:T(8,128)(2,1)}), bf16[8,2,144,192]{3,2,1,0:T(8,128)(2,1)}, u32[]{:S(2)}, u32[]{:S(2)}) async-start(bf16[8,2,144,192]{3,2,1,0:T(8,128)(2,1)} %get-tuple-element.1160), calls=%async_computation.8 | async-start | bytes 2359296 | tf_op jit(solution)/shard_map/all_to_all | solution.py:374
  189.9 451.0 %all-reduce.11.cloned.1.call-start = ((), (), s32[]{:S(2)}) async-start(), calls=%async_computation.13 | async-start | bytes 18874368 | tf_op jit(solution)/shard_map/psum | solution.py:1027
  210.2 35.5 %collective-permute-start.48 = (bf16[8,80,1536]{2,0,1:T(8,128)(2,1)}, bf16[8,80,1536]{2,0,1:T(8,128)(2,1)}, u32[]{:S(2)}, u32[]{:S(2)}) collective-permute-start(bf16[8,80,1536]{2,0,1:T(8,128)(2,1)} %pad_maximum_fusion.24), channel_id=1, source_target_pairs={{0,4},{4,0},{8,12},{12,8},{16,20},{20,16},{24,28},{28,24},{1,5},{5... | collective-permute-start | bytes 5898248 | tf_op jit(solution)/shard_map/ppermute | solution.py:346
  210.2 32.2 %collective-permute-start.47 = (bf16[8,64,1536]{2,1,0:T(8,128)(2,1)}, bf16[8,64,1536]{2,1,0:T(8,128)(2,1)}, u32[]{:S(2)}, u32[]{:S(2)}) collective-permute-start(bf16[8,64,1536]{2,1,0:T(8,128)(2,1)} %pad_maximum_fusion.27), channel_id=1, source_target_pairs={{0,4},{4,0},{8,12},{12,8},{16,20},{20,16},{24,28},{28,24},{1,5},{5... | collective-permute-start | bytes 4718600 | tf_op jit(solution)/shard_map/ppermute | solution.py:346
  225.6 11.2 %collective-permute-start.43 = (bf16[2,64,1536]{2,1,0:T(8,128)(2,1)}, bf16[2,64,1536]{2,1,0:T(8,128)(2,1)S(1)}, u32[]{:S(2)}, u32[]{:S(2)}) collective-permute-start(bf16[2,64,1536]{2,1,0:T(8,128)(2,1)} %get-tuple-element.1165), channel_id=1, source_target_pairs={{0,8},{4,12},{8,0},{12,4},{16,24},{20,28},{24,16},{28,20},{1,9},{5... | collective-permute-start | bytes 1179656 | tf_op jit(solution)/shard_map/ppermute | solution.py:346
  226.1 13.1 %collective-permute-start.45 = (bf16[2,80,1536]{2,1,0:T(8,128)(2,1)}, bf16[2,80,1536]{2,1,0:T(8,128)(2,1)S(1)}, u32[]{:S(2)}, u32[]{:S(2)}) collective-permute-start(bf16[2,80,1536]{2,1,0:T(8,128)(2,1)} %get-tuple-element.1166), channel_id=1, source_target_pairs={{0,16},{4,20},{8,24},{12,28},{16,0},{20,4},{24,8},{28,12},{1,17},{... | collective-permute-start | bytes 1474568 | tf_op jit(solution)/shard_map/ppermute | solution.py:346
  237.9 18.7 %collective-permute-start.44 = (bf16[4,64,1536]{2,1,0:T(8,128)(2,1)S(1)}, bf16[4,64,1536]{2,1,0:T(8,128)(2,1)S(1)}, u32[]{:S(2)}, u32[]{:S(2)}) collective-permute-start(bf16[4,64,1536]{2,1,0:T(8,128)(2,1)S(1)} %pad_maximum_fusion.34), channel_id=1, source_target_pairs={{0,16},{4,20},{8,24},{12,28},{16,0},{20,4},{24,8},{28,12},{1,17},{... | collective-permute-start | bytes 2359304 | tf_op jit(solution)/shard_map/ppermute | solution.py:346
  240.3 22.6 %collective-permute-start.46 = (bf16[4,80,1536]{2,1,0:T(8,128)(2,1)S(1)}, bf16[4,80,1536]{2,1,0:T(8,128)(2,1)S(1)}, u32[]{:S(2)}, u32[]{:S(2)}) collective-permute-start(bf16[4,80,1536]{2,1,0:T(8,128)(2,1)S(1)} %pad_maximum_fusion.31), channel_id=1, source_target_pairs={{0,8},{4,12},{8,0},{12,4},{16,24},{20,28},{24,16},{28,20},{1,9},{5... | collective-permute-start | bytes 2949128 | tf_op jit(solution)/shard_map/ppermute | solution.py:346
  272.5 19.5 %collective-permute-start.50 = (bf16[8,80,1536]{2,1,0:T(8,128)(2,1)}, bf16[8,80,1536]{2,1,0:T(8,128)(2,1)S(1)}, u32[]{:S(2)}, u32[]{:S(2)}) collective-permute-start(bf16[8,80,1536]{2,1,0:T(8,128)(2,1)} %pad_maximum_fusion.25), channel_id=1, source_target_pairs={{0,4},{4,0},{8,12},{12,8},{16,20},{20,16},{24,28},{28,24},{1,5},{5... | collective-permute-start | bytes 5898248 | tf_op jit(solution)/shard_map/ppermute | solution.py:346
  312.7 519.8 %all-reduce.9.cloned.1.call-start = ((), (), s32[]{:S(2)}) async-start(), calls=%async_computation.12 | async-start | bytes 10223616 | tf_op jit(solution)/shard_map/psum | solution.py:1163
  333.6 9.1 %collective-permute-start.1 = (bf16[8,80,1536]{2,1,0:T(8,128)(2,1)S(1)}, bf16[8,80,1536]{2,1,0:T(8,128)(2,1)S(1)}, u32[]{:S(2)}, u32[]{:S(2)}) collective-permute-start(bf16[8,80,1536]{2,1,0:T(8,128)(2,1)S(1)} %bitcast.332), channel_id=1, source_target_pairs={{0,4},{4,0},{8,12},{12,8},{16,20},{20,16},{24,28},{28,24},{1,5},{5... | collective-permute-start | bytes 5898248 | tf_op jit(solution)/shard_map/while/body/ppermute | solution.py:346
  337.9 4.8 collective-permute-start
  343.2 19.6 %collective-permute-start.2 = (bf16[4,64,1536]{2,1,0:T(8,128)(2,1)S(1)}, bf16[4,64,1536]{2,1,0:T(8,128)(2,1)S(1)}, u32[]{:S(2)}, u32[]{:S(2)}) collective-permute-start(bf16[4,64,1536]{2,1,0:T(8,128)(2,1)S(1)} %slice.807), channel_id=1, source_target_pairs={{0,16},{4,20},{8,24},{12,28},{16,0},{20,4},{24,8},{28,12},{1,17},{... | collective-permute-start | bytes 2359304 | tf_op jit(solution)/shard_map/while/body/ppermute | solution.py:346
  346.4 237.6 %collective-permute-start.19 = (bf16[8,80,1536]{2,1,0:T(8,128)(2,1)}, bf16[8,80,1536]{2,1,0:T(8,128)(2,1)}, u32[]{:S(2)}, u32[]{:S(2)}) collective-permute-start(bf16[8,80,1536]{2,1,0:T(8,128)(2,1)} %bitcast.306), channel_id=1, source_target_pairs={{0,4},{4,0},{8,12},{12,8},{16,20},{20,16},{24,28},{28,24},{1,5},{5... | collective-permute-start | bytes 5898248 | tf_op jit(solution)/shard_map/while/body/ppermute | solution.py:346
  348.7 24.6 %collective-permute-start.4 = (bf16[4,80,1536]{2,1,0:T(8,128)(2,1)S(1)}, bf16[4,80,1536]{2,1,0:T(8,128)(2,1)S(1)}, u32[]{:S(2)}, u32[]{:S(2)}) collective-permute-start(bf16[4,80,1536]{2,1,0:T(8,128)(2,1)S(1)} %slice.808), channel_id=1, source_target_pairs={{0,8},{4,12},{8,0},{12,4},{16,24},{20,28},{24,16},{28,20},{1,9},{5... | collective-permute-start | bytes 2949128 | tf_op jit(solution)/shard_map/while/body/ppermute | solution.py:346
  363.8 17.5 %collective-permute-start.3 = (bf16[2,64,1536]{2,1,0:T(8,128)(2,1)S(1)}, bf16[2,64,1536]{2,1,0:T(8,128)(2,1)S(1)}, u32[]{:S(2)}, u32[]{:S(2)}) collective-permute-start(bf16[2,64,1536]{2,1,0:T(8,128)(2,1)S(1)} %get-tuple-element.2591), channel_id=1, source_target_pairs={{0,8},{4,12},{8,0},{12,4},{16,24},{20,28},{24,16},{28,20},{1,9},{5... | collective-permute-start | bytes 1179656 | tf_op jit(solution)/shard_map/while/body/ppermute | solution.py:346
  374.4 12.7 %collective-permute-start.5 = (bf16[2,80,1536]{2,1,0:T(8,128)(2,1)S(1)}, bf16[2,80,1536]{2,1,0:T(8,128)(2,1)}, u32[]{:S(2)}, u32[]{:S(2)}) collective-permute-start(bf16[2,80,1536]{2,1,0:T(8,128)(2,1)S(1)} %get-tuple-element.2596), channel_id=1, source_target_pairs={{0,16},{4,20},{8,24},{12,28},{16,0},{20,4},{24,8},{28,12},{1,17},{... | collective-permute-start | bytes 1474568 | tf_op jit(solution)/shard_map/while/body/ppermute | solution.py:346
  403.0 21.3 %all-to-all-start = ((bf16[8,2,144,192]{3,2,1,0:T(8,128)(2,1)}), bf16[8,2,144,192]{3,2,1,0:T(8,128)(2,1)}, u32[]{:S(2)}, u32[]{:S(2)}) async-start(bf16[8,2,144,192]{3,2,1,0:T(8,128)(2,1)} %get-tuple-element.2598), calls=%async_computation | async-start | bytes 2359296 | tf_op jit(solution)/shard_map/while/body/all_to_all | solution.py:374
  424.3 30.3 %collective-permute-start.6 = (bf16[2,64,1536]{2,1,0:T(8,128)(2,1)}, bf16[2,64,1536]{2,1,0:T(8,128)(2,1)}, u32[]{:S(2)}, u32[]{:S(2)}) collective-permute-start(bf16[2,64,1536]{2,1,0:T(8,128)(2,1)} %get-tuple-element.2604), channel_id=1, source_target_pairs={{0,8},{4,12},{8,0},{12,4},{16,24},{20,28},{24,16},{28,20},{1,9},{5... | collective-permute-start | bytes 1179656 | tf_op jit(solution)/shard_map/while/body/ppermute | solution.py:346
  424.8 31.1 %collective-permute-start.7 = (bf16[2,80,1536]{2,1,0:T(8,128)(2,1)S(1)}, bf16[2,80,1536]{2,1,0:T(8,128)(2,1)}, u32[]{:S(2)}, u32[]{:S(2)}) collective-permute-start(bf16[2,80,1536]{2,1,0:T(8,128)(2,1)S(1)} %copy-done.23), channel_id=1, source_target_pairs={{0,16},{4,20},{8,24},{12,28},{16,0},{20,4},{24,8},{28,12},{1,17},{... | collective-permute-start | bytes 1474568 | tf_op jit(solution)/shard_map/while/body/ppermute | solution.py:346
  457.0 22.9 %collective-permute-start.9 = (bf16[4,80,1536]{2,1,0:T(8,128)(2,1)S(1)}, bf16[4,80,1536]{2,1,0:T(8,128)(2,1)S(1)}, u32[]{:S(2)}, u32[]{:S(2)}) collective-permute-start(bf16[4,80,1536]{2,1,0:T(8,128)(2,1)S(1)} %pad_maximum_fusion.56), channel_id=1, source_target_pairs={{0,8},{4,12},{8,0},{12,4},{16,24},{20,28},{24,16},{28,20},{1,9},{5... | collective-permute-start | bytes 2949128 | tf_op jit(solution)/shard_map/while/body/ppermute | solution.py:346
  458.4 17.3 %collective-permute-start.8 = (bf16[4,64,1536]{2,1,0:T(8,128)(2,1)S(1)}, bf16[4,64,1536]{2,1,0:T(8,128)(2,1)S(1)}, u32[]{:S(2)}, u32[]{:S(2)}) collective-permute-start(bf16[4,64,1536]{2,1,0:T(8,128)(2,1)S(1)} %pad_maximum_fusion.55), channel_id=1, source_target_pairs={{0,16},{4,20},{8,24},{12,28},{16,0},{20,4},{24,8},{28,12},{1,17},{... | collective-permute-start | bytes 2359304 | tf_op jit(solution)/shard_map/while/body/ppermute | solution.py:346
  481.4 23.1 %collective-permute-start.11 = (bf16[8,80,1536]{2,1,0:T(8,128)(2,1)}, bf16[8,80,1536]{2,1,0:T(8,128)(2,1)}, u32[]{:S(2)}, u32[]{:S(2)}) collective-permute-start(bf16[8,80,1536]{2,1,0:T(8,128)(2,1)} %pad_maximum_fusion.58), channel_id=1, source_target_pairs={{0,4},{4,0},{8,12},{12,8},{16,20},{20,16},{24,28},{28,24},{1,5},{5... | collective-permute-start | bytes 5898248 | tf_op jit(solution)/shard_map/while/body/ppermute | solution.py:346
  481.4 18.7 %collective-permute-start.10 = (bf16[8,64,1536]{2,1,0:T(8,128)(2,1)}, bf16[8,64,1536]{2,1,0:T(8,128)(2,1)}, u32[]{:S(2)}, u32[]{:S(2)}) collective-permute-start(bf16[8,64,1536]{2,1,0:T(8,128)(2,1)} %pad_maximum_fusion.57), channel_id=1, source_target_pairs={{0,4},{4,0},{8,12},{12,8},{16,20},{20,16},{24,28},{28,24},{1,5},{5... | collective-permute-start | bytes 4718600 | tf_op jit(solution)/shard_map/while/body/ppermute | solution.py:346
  484.2 40.8 %collective-permute-start.13 = (bf16[8,80,1536]{2,1,0:T(8,128)(2,1)}, bf16[8,80,1536]{2,1,0:T(8,128)(2,1)}, u32[]{:S(2)}, u32[]{:S(2)}) collective-permute-start(bf16[8,80,1536]{2,1,0:T(8,128)(2,1)} %get-tuple-element.2618), channel_id=1, source_target_pairs={{0,4},{4,0},{8,12},{12,8},{16,20},{20,16},{24,28},{28,24},{1,5},{5... | collective-permute-start | bytes 5898248 | tf_op jit(solution)/shard_map/while/body/ppermute | solution.py:346
  486.1 38.9 %collective-permute-start.12 = (bf16[8,64,1536]{2,1,0:T(8,128)(2,1)}, bf16[8,64,1536]{2,1,0:T(8,128)(2,1)}, u32[]{:S(2)}, u32[]{:S(2)}) collective-permute-start(bf16[8,64,1536]{2,1,0:T(8,128)(2,1)} %get-tuple-element.2615), channel_id=1, source_target_pairs={{0,4},{4,0},{8,12},{12,8},{16,20},{20,16},{24,28},{28,24},{1,5},{5... | collective-permute-start | bytes 4718600 | tf_op jit(solution)/shard_map/while/body/ppermute | solution.py:346
  490.9 29.7 %all-to-all-start.1 = ((bf16[8,192,576]{2,1,0:T(8,128)(2,1)}), bf16[8,192,576]{2,1,0:T(8,128)(2,1)}, u32[]{:S(2)}, u32[]{:S(2)}) async-start(bf16[8,192,576]{2,1,0:T(8,128)(2,1)} %bitcast.297), calls=%async_computation.1 | async-start | bytes 3932160 | tf_op jit(solution)/shard_map/while/body/all_to_all | solution.py:374
  500.1 83.8 %collective-permute-start.18 = (bf16[8,64,1536]{2,1,0:T(8,128)(2,1)}, bf16[8,64,1536]{2,1,0:T(8,128)(2,1)}, u32[]{:S(2)}, u32[]{:S(2)}) collective-permute-start(bf16[8,64,1536]{2,1,0:T(8,128)(2,1)} %bitcast.335), channel_id=1, source_target_pairs={{0,4},{4,0},{8,12},{12,8},{16,20},{20,16},{24,28},{28,24},{1,5},{5... | collective-permute-start | bytes 4718600 | tf_op jit(solution)/shard_map/while/body/ppermute | solution.py:346
  520.6 30.1 %all-to-all-start.2 = ((bf16[8,192,576]{2,1,0:T(8,128)(2,1)}), bf16[8,192,576]{2,1,0:T(8,128)(2,1)}, u32[]{:S(2)}, u32[]{:S(2)}) async-start(bf16[8,192,576]{2,1,0:T(8,128)(2,1)} %bitcast.298), calls=%async_computation.2 | async-start | bytes 3932160 | tf_op jit(solution)/shard_map/while/body/all_to_all | solution.py:374
  529.1 41.3 %collective-permute-start.15 = (bf16[4,80,1536]{2,1,0:T(8,128)(2,1)}, bf16[4,80,1536]{2,1,0:T(8,128)(2,1)}, u32[]{:S(2)}, u32[]{:S(2)}) collective-permute-start(bf16[4,80,1536]{2,1,0:T(8,128)(2,1)} %get-tuple-element.2628), channel_id=1, source_target_pairs={{0,8},{4,12},{8,0},{12,4},{16,24},{20,28},{24,16},{28,20},{1,9},{5... | collective-permute-start | bytes 2949128 | tf_op jit(solution)/shard_map/while/body/ppermute | solution.py:346
  534.2 32.0 %collective-permute-start.14 = (bf16[4,64,1536]{2,1,0:T(8,128)(2,1)}, bf16[4,64,1536]{2,1,0:T(8,128)(2,1)}, u32[]{:S(2)}, u32[]{:S(2)}) collective-permute-start(bf16[4,64,1536]{2,1,0:T(8,128)(2,1)} %get-tuple-element.2624), channel_id=1, source_target_pairs={{0,16},{4,20},{8,24},{12,28},{16,0},{20,4},{24,8},{28,12},{1,17},{... | collective-permute-start | bytes 2359304 | tf_op jit(solution)/shard_map/while/body/ppermute | solution.py:346
  573.1 14.5 %collective-permute-start.17 = (bf16[2,80,1536]{2,1,0:T(8,128)(2,1)}, bf16[2,80,1536]{2,1,0:T(8,128)(2,1)}, u32[]{:S(2)}, u32[]{:S(2)}) collective-permute-start(bf16[2,80,1536]{2,1,0:T(8,128)(2,1)} %get-tuple-element.2642), channel_id=1, source_target_pairs={{0,16},{4,20},{8,24},{12,28},{16,0},{20,4},{24,8},{28,12},{1,17},{... | collective-permute-start | bytes 1474568 | tf_op jit(solution)/shard_map/while/body/ppermute | solution.py:346
  576.9 10.7 %collective-permute-start.16 = (bf16[2,64,1536]{2,1,0:T(8,128)(2,1)}, bf16[2,64,1536]{2,1,0:T(8,128)(2,1)}, u32[]{:S(2)}, u32[]{:S(2)}) collective-permute-start(bf16[2,64,1536]{2,1,0:T(8,128)(2,1)} %get-tuple-element.2638), channel_id=1, source_target_pairs={{0,8},{4,12},{8,0},{12,4},{16,24},{20,28},{24,16},{28,20},{1,9},{5... | collective-permute-start | bytes 1179656 | tf_op jit(solution)/shard_map/while/body/ppermute | solution.py:346
  592.9 22.2 %collective-permute-start.21 = (bf16[4,80,1536]{2,1,0:T(8,128)(2,1)S(1)}, bf16[4,80,1536]{2,1,0:T(8,128)(2,1)S(1)}, u32[]{:S(2)}, u32[]{:S(2)}) collective-permute-start(bf16[4,80,1536]{2,1,0:T(8,128)(2,1)S(1)} %get-tuple-element.2656), channel_id=1, source_target_pairs={{0,8},{4,12},{8,0},{12,4},{16,24},{20,28},{24,16},{28,20},{1,9},{5... | collective-permute-start | bytes 2949128 | tf_op jit(solution)/shard_map/while/body/ppermute | solution.py:346
  596.1 17.9 %collective-permute-start.20 = (bf16[4,64,1536]{2,1,0:T(8,128)(2,1)S(1)}, bf16[4,64,1536]{2,1,0:T(8,128)(2,1)S(1)}, u32[]{:S(2)}, u32[]{:S(2)}) collective-permute-start(bf16[4,64,1536]{2,1,0:T(8,128)(2,1)S(1)} %get-tuple-element.2652), channel_id=1, source_target_pairs={{0,16},{4,20},{8,24},{12,28},{16,0},{20,4},{24,8},{28,12},{1,17},{... | collective-permute-start | bytes 2359304 | tf_op jit(solution)/shard_map/while/body/ppermute | solution.py:346
  615.4 10.8 %collective-permute-start.23 = (bf16[2,80,1536]{2,1,0:T(8,128)(2,1)S(1)}, bf16[2,80,1536]{2,1,0:T(8,128)(2,1)S(1)}, u32[]{:S(2)}, u32[]{:S(2)}) collective-permute-start(bf16[2,80,1536]{2,1,0:T(8,128)(2,1)S(1)} %slice.810), channel_id=1, source_target_pairs={{0,16},{4,20},{8,24},{12,28},{16,0},{20,4},{24,8},{28,12},{1,17},{... | collective-permute-start | bytes 1474568 | tf_op jit(solution)/shard_map/while/body/ppermute | solution.py:346
  616.2 8.4 collective-permute-start.22
  647.4 8.0 collective-permute-start.24
  649.0 16.8 %collective-permute-start.25 = (bf16[43008]{0:T(1024)(128)(2,1)S(1)}, bf16[43008]{0:T(1024)(128)(2,1)S(1)}, u32[]{:S(2)}, u32[]{:S(2)}) collective-permute-start(bf16[43008]{0:T(1024)(128)(2,1)S(1)} %concatenate.210), channel_id=1, source_target_pairs={{0,2},{1,3},{2,0},{3,1},{4,6},{5,7},{6,4},{7,5},{8,10},{9,11},{10,... | collective-permute-start | bytes 258056 | tf_op jit(solution)/shard_map/while/body/ppermute | solution.py:387
  649.5 16.4 %collective-permute-start.26 = (bf16[43008]{0:T(1024)(128)(2,1)S(1)}, bf16[43008]{0:T(1024)(128)(2,1)S(1)}, u32[]{:S(2)}, u32[]{:S(2)}) collective-permute-start(bf16[43008]{0:T(1024)(128)(2,1)S(1)} %concatenate.210), channel_id=1, source_target_pairs={{0,1},{1,2},{2,3},{3,0},{4,5},{5,6},{6,7},{7,4},{8,9},{9,10},{10,1... | collective-permute-start | bytes 258056 | tf_op jit(solution)/shard_map/while/body/ppermute | solution.py:387
  668.3 7.1 collective-permute-start.27
  675.9 12.3 %collective-permute-start.28 = (bf16[2,4,40704]{2,1,0:T(4,128)(2,1)S(1)}, bf16[2,4,40704]{2,1,0:T(4,128)(2,1)S(1)}, u32[]{:S(2)}, u32[]{:S(2)}) collective-permute-start(bf16[2,4,40704]{2,1,0:T(4,128)(2,1)S(1)} %pad_maximum_fusion.65), channel_id=1, source_target_pairs={{0,16},{4,20},{8,24},{12,28},{16,0},{20,4},{24,8},{28,12},{1,17},{... | collective-permute-start | bytes 1953800 | tf_op jit(solution)/shard_map/while/body/ppermute | solution.py:346
  677.5 34.4 %all-to-all-start.3 = ((bf16[8,192,768]{2,1,0:T(8,128)(2,1)}), bf16[8,192,768]{2,1,0:T(8,128)(2,1)}, u32[]{:S(2)}, u32[]{:S(2)}) async-start(bf16[8,192,768]{2,1,0:T(8,128)(2,1)} %get-tuple-element.2743), calls=%async_computation.3 | async-start | bytes 4718592 | tf_op jit(solution)/shard_map/while/body/all_to_all | solution.py:374
  690.2 26.1 %collective-permute-start.29 = (bf16[4,4,40704]{2,1,0:T(4,128)(2,1)}, bf16[4,4,40704]{2,1,0:T(4,128)(2,1)S(1)}, u32[]{:S(2)}, u32[]{:S(2)}) collective-permute-start(bf16[4,4,40704]{2,1,0:T(4,128)(2,1)} %pad_maximum_fusion.66), channel_id=1, source_target_pairs={{0,4},{4,0},{8,12},{12,8},{16,20},{20,16},{24,28},{28,24},{1,5},{5... | collective-permute-start | bytes 3907592 | tf_op jit(solution)/shard_map/while/body/ppermute | solution.py:346
  711.9 33.8 %all-to-all-start.4 = ((bf16[8,192,768]{2,1,0:T(8,128)(2,1)}), bf16[8,192,768]{2,1,0:T(8,128)(2,1)}, u32[]{:S(2)}, u32[]{:S(2)}) async-start(bf16[8,192,768]{2,1,0:T(8,128)(2,1)} %get-tuple-element.2744), calls=%async_computation.4 | async-start | bytes 4718592 | tf_op jit(solution)/shard_map/while/body/all_to_all | solution.py:374
  766.1 31.4 %all-to-all-start.9 = ((f32[8,2,192]{2,1,0:T(2,128)}), f32[8,2,192]{2,1,0:T(2,128)S(1)}, u32[]{:S(2)}, u32[]{:S(2)}) async-start(f32[8,2,192]{2,1,0:T(2,128)} %copy.142), calls=%async_computation.9 | async-start | bytes 32768 | tf_op jit(solution)/shard_map/all_to_all | solution.py:1217
  (91 other events, 680.3 us)
Sparse Core Ops, SparseCore 0:
  10.5 80.5 all-gather.6
  144.0 87.7 all-gather.8
  312.8 325.2 all-reduce.10
  641.1 191.4 all-reduce.8
